TPU v7x, 32 devices: a whole 2x2x4 slice. The times are simulated.
32 devices in a mesh: wide: 4 (over y, core), blk: 8 (over z, x).
Axes of the slice: x: 2, y: 2, z: 4, core: 2. Of those that a mesh axis runs over, the one named last changes fastest.
Arguments:
- text_blocks: bfloat16 [8, 1024, 768], P('wide', 'blk'), may hold values from -6 to 6
- image_blocks: bfloat16 [8, 1024, 768], P('wide', 'blk'), may hold values from -6 to 6
- cotangent: bfloat16 [8, 1024, 768], P('wide', 'blk'), may hold values from -6 to 6
- text_mask: int32 [8, 1024], P('wide', 'blk'), may hold values 0 or 1
- page_regions: int32 [8, 8], P('wide', 'blk'), may hold values from 5 to 100
- doc_pages: int32 [8], P('wide'), may hold values from 1 to 8, as said below
- self_project: bfloat16 [768, 2304], replicated, may hold values from -0.21875 to 0.21875
- self_output: bfloat16 [768, 768], replicated, may hold values from -1.25 to 1.25
- cross_query: bfloat16 [768, 768], replicated, may hold values from -0.21875 to 0.21875
- cross_pairs: bfloat16 [768, 1536], replicated, may hold values from -0.21875 to 0.21875
- cross_output: bfloat16 [768, 768], replicated, may hold values from -1.25 to 1.25
- gate_weight: bfloat16 [768, 12], replicated, may hold values from -0.21875 to 0.21875
- expand_weight: bfloat16 [768, 3072], replicated, may hold values from -0.21875 to 0.21875
- expand_bias: float32 [3072], replicated, may hold values from -3 to 3
- reduce_weight: bfloat16 [3072, 768], replicated, may hold values from -0.109375 to 0.109375
- reduce_bias: float32 [768], replicated, may hold values from -3 to 3
- norm_gain: float32 [4, 768], replicated, may hold values from 0.5 to 1.5
- norm_bias: float32 [4, 768], replicated, may hold values from -2 to 2
Outputs:
- joined_blocks: bfloat16 [8, 1024, 768], P('wide', 'blk')
- text_grad: bfloat16 [8, 1024, 768], P('wide', 'blk')
- image_grad: bfloat16 [8, 1024, 768], P('wide', 'blk')
- grad_self_project: float32 [768, 2304], P('wide', 'blk')
- grad_self_output: float32 [768, 768], P('wide', 'blk')
- grad_cross_query: float32 [768, 768], P('wide', 'blk')
- grad_cross_pairs: float32 [768, 1536], P('wide', 'blk')
- grad_cross_output: float32 [768, 768], P('wide', 'blk')
- grad_expand_weight: float32 [768, 3072], P('wide', 'blk')
- grad_reduce_weight: float32 [3072, 768], P('wide', 'blk')
- grad_gate_weight: float32 [768, 12], replicated
- grad_expand_bias: float32 [3072], replicated
- grad_reduce_bias: float32 [768], replicated
- grad_norm_gain: float32 [4, 768], replicated
- grad_norm_bias: float32 [4, 768], replicated
Inputs may be any that keep to these rules, and one draw needn't show every extreme that they name: `doc_pages`: of the 2 documents of each index of wide, one uses all pages.
All inputs are finite; a program needn't handle non-finite values. No bound on the sum of `text_mask` on one device may be relied on, other than what follows from the above.
Results may differ from a plain program's by a relative error of at most 0.024.
Values may be sent and summed in bfloat16 or wider, within the bound.
A program may use at most 320 MiB of HBM per device.

v0:
```python
import jax
import jax.numpy as jnp
from jax import lax
from jax.sharding import PartitionSpec as P

D = 768
H = 12
HD = 64
PAGE = 128
DOCS = 2


EPSILON = 1e-05
NEGATIVE = -1e30
HIGHEST = lax.Precision.HIGHEST


def normalize(values, gains, biases):
    centred = values - jnp.mean(values, axis=-1, keepdims=True)
    inverse = lax.rsqrt(jnp.mean(centred * centred, axis=-1, keepdims=True) + EPSILON)
    scaled = centred * inverse
    return (scaled * gains + biases, scaled, inverse)


def normalize_back(upstream, scaled, inverse, gains):
    weighted = upstream * gains
    result = inverse * (
        weighted
        - jnp.mean(weighted, axis=-1, keepdims=True)
        - scaled * jnp.mean(weighted * scaled, axis=-1, keepdims=True)
    )
    return (result, jnp.sum(upstream * scaled, axis=0), jnp.sum(upstream, axis=0))


def product(left, right):
    return jnp.dot(left, right, preferred_element_type=jnp.float32)


def against(left, right):
    return lax.dot_general(
        left, right, (((1,), (1,)), ((), ())), preferred_element_type=jnp.float32
    )


def transposed(left, right):
    return lax.dot_general(
        left, right, (((0,), (0,)), ((), ())), preferred_element_type=jnp.float32
    )


def gelu_tanh(values):
    return jax.nn.gelu(values, approximate=True)


def forward_doc(queries, carried, key_pairs, allowed, scaling):
    running_max, summed, accumulated = carried
    key_count = key_pairs.shape[0]
    keys_part = key_pairs[:, :D].reshape(key_count, H, HD)
    values_part = key_pairs[:, D:].reshape(key_count, H, HD)
    open_keys = (allowed > 0)[None, None, :]
    scores = (
        jnp.einsum("qhd,khd->hqk", queries, keys_part, preferred_element_type=jnp.float32) * scaling
    )
    scores = jnp.where(open_keys, scores, NEGATIVE)
    new_max = jnp.maximum(running_max, jnp.max(scores, axis=-1))
    fading = jnp.exp(running_max - new_max)
    weights = jnp.where(open_keys, jnp.exp(scores - new_max[..., None]), 0.0)
    summed = summed * fading + jnp.sum(weights, axis=-1)
    accumulated = accumulated * fading[..., None] + jnp.einsum(
        "hqk,khd->hqd",
        weights.astype(jnp.bfloat16),
        values_part,
        preferred_element_type=jnp.float32,
    )
    return (new_max, summed, accumulated)


def forward_fold(queries, scaling, carried, pieces):
    key_pairs, allowed = pieces

    def forward_per_doc(doc_items):
        doc_queries, doc_max, doc_sum, doc_acc, doc_pairs, doc_allowed = doc_items
        doc_carry = (doc_max, doc_sum, doc_acc)
        result = forward_doc(doc_queries, doc_carry, doc_pairs, doc_allowed, scaling)
        return result

    return lax.map(
        forward_per_doc, (queries, carried[0], carried[1], carried[2], key_pairs, allowed)
    )


def backward_doc(queries, grad_out, log_sum, row_delta, key_pairs, allowed, scaling):
    key_count = key_pairs.shape[0]
    keys_part = key_pairs[:, :D].reshape(key_count, H, HD)
    values_part = key_pairs[:, D:].reshape(key_count, H, HD)
    open_keys = (allowed > 0)[None, None, :]
    scores = (
        jnp.einsum("qhd,khd->hqk", queries, keys_part, preferred_element_type=jnp.float32) * scaling
    )
    probabilities = jnp.where(open_keys, jnp.exp(scores - log_sum[..., None]), 0.0)
    grad_probs = jnp.einsum(
        "qhd,khd->hqk", grad_out, values_part, preferred_element_type=jnp.float32
    )
    grad_scores = (probabilities * (grad_probs - row_delta[..., None])).astype(jnp.bfloat16)
    query_grad = (
        jnp.einsum("hqk,khd->qhd", grad_scores, keys_part, preferred_element_type=jnp.float32)
        * scaling
    )
    key_grad = (
        jnp.einsum("hqk,qhd->khd", grad_scores, queries, preferred_element_type=jnp.float32)
        * scaling
    )
    value_grad = jnp.einsum(
        "hqk,qhd->khd",
        probabilities.astype(jnp.bfloat16),
        grad_out,
        preferred_element_type=jnp.float32,
    )
    return (
        query_grad,
        jnp.concatenate(
            [key_grad.reshape(key_count, D), value_grad.reshape(key_count, D)], axis=-1
        ),
    )


def backward_fold(queries, grad_out, log_sum, row_delta, scaling, pieces):
    key_pairs, allowed = pieces

    def backward_per_doc(doc_items):
        doc_queries, doc_grad, doc_log, doc_delta, doc_pairs, doc_allowed = doc_items
        result = backward_doc(
            doc_queries, doc_grad, doc_log, doc_delta, doc_pairs, doc_allowed, scaling
        )
        return result

    query_parts, pair_parts = lax.map(
        backward_per_doc, (queries, grad_out, log_sum, row_delta, key_pairs, allowed)
    )
    return (query_parts, pair_parts)


def start_state():
    return (
        jnp.full((DOCS, H, PAGE), NEGATIVE, jnp.float32),
        jnp.zeros((DOCS, H, PAGE), jnp.float32),
        jnp.zeros((DOCS, H, PAGE, HD), jnp.float32),
    )


def finish(state):
    running_max, summed, accumulated = state
    result = jnp.transpose(accumulated / summed[..., None], (0, 2, 1, 3))
    return (result, running_max + jnp.log(summed))


def tile_order(grad, wide_count, blk_count):
    rows, cols = grad.shape
    tiled = grad.reshape(wide_count, rows // wide_count, blk_count, cols // blk_count)
    return jnp.transpose(tiled, (0, 2, 1, 3)).reshape(
        wide_count * blk_count * (rows // wide_count), cols // blk_count
    )


def body(
    text_blocks,
    image_blocks,
    cotangent,
    text_mask,
    page_regions,
    doc_pages,
    self_project,
    self_output,
    cross_query,
    cross_pairs,
    cross_output,
    gate_weight,
    expand_weight,
    expand_bias,
    reduce_weight,
    reduce_bias,
    norm_gain,
    norm_bias,
):
    scaling = HD ** (-0.5)
    block_shape = text_blocks.shape
    offsets = jnp.arange(PAGE, dtype=jnp.int32)
    living = (lax.axis_index("blk") < doc_pages)[:, None]
    text_open = (living & ((text_mask > 0) | (offsets[None, :] == 0))).astype(jnp.bfloat16)
    image_open = (living & (offsets[None, :] < page_regions)).astype(jnp.bfloat16)
    text_rows = text_blocks.reshape(-1, D).astype(jnp.float32)
    image_rows = image_blocks.reshape(-1, D).astype(jnp.float32)
    normed_text, scaled_first, inverse_first = normalize(text_rows, norm_gain[0], norm_bias[0])
    normed_low = normed_text.astype(jnp.bfloat16)
    triples = product(normed_low, self_project).astype(jnp.bfloat16)
    self_queries = triples[:, :D].reshape(DOCS, PAGE, H, HD)
    self_pairs = triples[:, D:].reshape(DOCS, PAGE, 2 * D)
    self_state = forward_fold(
        self_queries,
        scaling,
        start_state(),
        (
            lax.all_gather(self_pairs, "blk", axis=1, tiled=True),
            lax.all_gather(text_open, "blk", axis=1, tiled=True),
        ),
    )
    self_result, self_logsum = finish(self_state)
    self_low = self_result.reshape(-1, D).astype(jnp.bfloat16)
    hidden = text_rows + product(self_low, self_output)
    cross_normed, scaled_cross, inverse_cross = normalize(hidden, norm_gain[1], norm_bias[1])
    cross_low = cross_normed.astype(jnp.bfloat16)
    gate_values = jax.nn.sigmoid(product(cross_low, gate_weight))
    image_normed, scaled_image, inverse_image = normalize(image_rows, norm_gain[2], norm_bias[2])
    image_low = image_normed.astype(jnp.bfloat16)
    image_pairs = product(image_low, cross_pairs).astype(jnp.bfloat16).reshape(DOCS, PAGE, 2 * D)
    cross_queries = product(cross_low, cross_query).astype(jnp.bfloat16).reshape(DOCS, PAGE, H, HD)
    cross_state = forward_fold(
        cross_queries,
        scaling,
        start_state(),
        (
            lax.all_gather(image_pairs, "blk", axis=1, tiled=True),
            lax.all_gather(image_open, "blk", axis=1, tiled=True),
        ),
    )
    cross_result, cross_logsum = finish(cross_state)
    gate_heads = gate_values.reshape(DOCS, PAGE, H, 1)
    gated_low = (cross_result * gate_heads).reshape(-1, D).astype(jnp.bfloat16)
    mixed_rows = hidden + product(gated_low, cross_output)
    final_normed, scaled_final, inverse_final = normalize(mixed_rows, norm_gain[3], norm_bias[3])
    final_low = final_normed.astype(jnp.bfloat16)
    inner_rows = product(final_low, expand_weight) + expand_bias
    active_low = gelu_tanh(inner_rows).astype(jnp.bfloat16)
    joined_blocks = (
        (mixed_rows + product(active_low, reduce_weight) + reduce_bias)
        .reshape(block_shape)
        .astype(jnp.bfloat16)
    )
    upstream = cotangent.reshape(-1, D)
    upstream_float = upstream.astype(jnp.float32)
    grad_reduce_bias = jnp.sum(upstream_float, axis=0)
    grad_reduce_weight = transposed(active_low, upstream)
    grad_active = against(upstream, reduce_weight).astype(jnp.bfloat16)
    gelu_value, gelu_pull = jax.vjp(gelu_tanh, inner_rows)
    grad_inner = gelu_pull(grad_active.astype(jnp.float32))[0].astype(jnp.bfloat16)
    grad_expand_bias = jnp.sum(grad_inner.astype(jnp.float32), axis=0)
    grad_expand_weight = transposed(final_low, grad_inner)
    back_final, gain_final, shift_final = normalize_back(
        against(grad_inner, expand_weight), scaled_final, inverse_final, norm_gain[3]
    )
    grad_mixed = upstream_float + back_final
    grad_branch = grad_mixed.astype(jnp.bfloat16)
    grad_cross_output = transposed(gated_low, grad_branch)
    grad_gated = against(grad_branch, cross_output).astype(jnp.bfloat16)
    grad_gated_heads = grad_gated.astype(jnp.float32).reshape(DOCS, PAGE, H, HD)
    grad_gate = jnp.sum(grad_gated_heads * cross_result, axis=-1).reshape(-1, H)
    grad_logit = grad_gate * gate_values * (1.0 - gate_values)
    grad_gate_weight = lax.dot_general(
        cross_low.astype(jnp.float32), grad_logit, (((0,), (0,)), ((), ())), precision=HIGHEST
    )
    grad_raw = (grad_gated_heads * gate_heads).astype(jnp.bfloat16)
    cross_delta = jnp.transpose(
        jnp.sum(grad_raw.astype(jnp.float32) * cross_result, axis=-1), (0, 2, 1)
    )
    cross_carry = backward_fold(
        cross_queries,
        grad_raw,
        cross_logsum,
        cross_delta,
        scaling,
        (
            lax.all_gather(image_pairs, "blk", axis=1, tiled=True),
            lax.all_gather(image_open, "blk", axis=1, tiled=True),
        ),
    )
    cross_home = lax.psum_scatter(
        cross_carry[1].astype(jnp.bfloat16), "blk", scatter_dimension=1, tiled=True
    ).astype(jnp.float32)
    cross_query_sum = cross_carry[0]
    cross_query_low = cross_query_sum.reshape(-1, D).astype(jnp.bfloat16)
    cross_pair_low = cross_home.reshape(-1, 2 * D).astype(jnp.bfloat16)
    grad_cross_query = transposed(cross_low, cross_query_low)
    grad_cross_pairs = transposed(image_low, cross_pair_low)
    back_image, gain_image, shift_image = normalize_back(
        against(cross_pair_low, cross_pairs), scaled_image, inverse_image, norm_gain[2]
    )
    image_grad = back_image.reshape(block_shape).astype(jnp.bfloat16)
    grad_cross_in = against(cross_query_low, cross_query) + lax.dot_general(
        grad_logit, gate_weight.astype(jnp.float32), (((1,), (1,)), ((), ())), precision=HIGHEST
    )
    back_cross, gain_cross, shift_cross = normalize_back(
        grad_cross_in, scaled_cross, inverse_cross, norm_gain[1]
    )
    grad_hidden = grad_mixed + back_cross
    grad_self_branch = grad_hidden.astype(jnp.bfloat16)
    grad_self_output = transposed(self_low, grad_self_branch)
    grad_self_result = (
        against(grad_self_branch, self_output).astype(jnp.bfloat16).reshape(DOCS, PAGE, H, HD)
    )
    self_delta = jnp.transpose(
        jnp.sum(grad_self_result.astype(jnp.float32) * self_result, axis=-1), (0, 2, 1)
    )
    self_carry = backward_fold(
        self_queries,
        grad_self_result,
        self_logsum,
        self_delta,
        scaling,
        (
            lax.all_gather(self_pairs, "blk", axis=1, tiled=True),
            lax.all_gather(text_open, "blk", axis=1, tiled=True),
        ),
    )
    self_home = lax.psum_scatter(
        self_carry[1].astype(jnp.bfloat16), "blk", scatter_dimension=1, tiled=True
    ).astype(jnp.float32)
    self_query_sum = self_carry[0]
    grad_triples = jnp.concatenate(
        [self_query_sum.reshape(-1, D), self_home.reshape(-1, 2 * D)], axis=-1
    ).astype(jnp.bfloat16)
    grad_self_project = transposed(normed_low, grad_triples)
    back_first, gain_first, shift_first = normalize_back(
        against(grad_triples, self_project), scaled_first, inverse_first, norm_gain[0]
    )
    text_grad = (grad_hidden + back_first).reshape(block_shape).astype(jnp.bfloat16)
    wide_count = lax.axis_size("wide")
    blk_count = lax.axis_size("blk")
    large_grads = (
        grad_self_project,
        grad_self_output,
        grad_cross_query,
        grad_cross_pairs,
        grad_cross_output,
        grad_expand_weight,
        grad_reduce_weight,
    )
    ordered = tuple((tile_order(grad, wide_count, blk_count) for grad in large_grads))
    summed_grads = lax.psum_scatter(ordered, ("wide", "blk"), scatter_dimension=0, tiled=True)
    small_sums = lax.psum(
        (
            grad_gate_weight,
            grad_expand_bias,
            grad_reduce_bias,
            jnp.stack([gain_first, gain_cross, gain_image, gain_final]),
            jnp.stack([shift_first, shift_cross, shift_image, shift_final]),
        ),
        ("wide", "blk"),
    )
    return (
        joined_blocks,
        text_grad,
        image_grad,
        summed_grads[0],
        summed_grads[1],
        summed_grads[2],
        summed_grads[3],
        summed_grads[4],
        summed_grads[5],
        summed_grads[6],
        small_sums[0],
        small_sums[1],
        small_sums[2],
        small_sums[3],
        small_sums[4],
    )


def solution(mesh):
    return jax.shard_map(
        body,
        mesh=mesh,
        in_specs=(
            P("wide", "blk", None),
            P("wide", "blk", None),
            P("wide", "blk", None),
            P("wide", "blk"),
            P("wide", "blk"),
            P("wide"),
            P(),
            P(),
            P(),
            P(),
            P(),
            P(),
            P(),
            P(),
            P(),
            P(),
            P(),
            P(),
        ),
        out_specs=(
            P("wide", "blk", None),
            P("wide", "blk", None),
            P("wide", "blk", None),
            P("wide", "blk"),
            P("wide", "blk"),
            P("wide", "blk"),
            P("wide", "blk"),
            P("wide", "blk"),
            P("wide", "blk"),
            P("wide", "blk"),
            P(),
            P(),
            P(),
            P(),
            P(),
        ),
        check_vma=False,
    )
```

profile of v0, /device:TPU:1, one launch (start us, length us, event | category | flops | bytes accessed | tf_op | source)
XLA Modules:
  0.0 1635.9 jit_solution(8825490683803476989)
XLA Ops:
  29.2 17.9 %all_gather.16 = bf16[2,1024]{1,0:T(2,128)(2,1)S(1)} all-gather(bf16[2,128]{1,0:T(2,128)(2,1)S(1)} %get-tuple-element.460), channel_id=1, replica_groups=mesh['wide'=4,'blk'=8] {'blk'}, dimensions={1}, use_global_device_ids=true | all-gather | bytes 4608 | tf_op jit(solution)/shard_map/all_gather | solution.py:204
  50.6 71.1 %all-gather.3.cloned.1.call-done = bf16[2,1024,1536]{1,2,0:T(8,128)(2,1)} async-done(((bf16[2,128,1536]{1,2,0:T(8,128)(2,1)}), bf16[2,1024,1536]{1,2,0:T(8,128)(2,1)}) %all-gather.3.cloned.1.call-update) | async-done | bytes 6291472 | tf_op jit(solution)/shard_map/all_gather | solution.py:203
  124.1 40.0 %while.52 = (s32[]{:T(128)}, f32[2,12,128]{2,1,0:T(8,128)}, f32[2,12,128]{2,1,0:T(8,128)}, f32[2,12,128,64]{2,0,3,1:T(2,128)}, bf16[2,1024]{1,0:T(2,128)(2,1)S(1...) while((s32[]{:T(128)}, f32[2,12,128]{2,1,0:T(8,128)}, ...), condition=%wide.region_5.6_spmd, body=%wide.region_2.5_spmd.sunk | while | flops 423209472 | bytes 37837060 | solution.py:87
  131.5 2.5 fusion.251
  134.0 10.1 dynamic_update_slice.51
  151.5 2.5 fusion.251
  154.0 10.1 dynamic_update_slice.51
  164.9 2.5 bitcast_convert_fusion
  173.4 2.4 copy.122
  175.8 14.9 all_gather.18
  193.9 2.6 convolution_convert_fusion.5
  202.1 71.9 %all-gather.5.cloned.1.call-done = bf16[2,1024,1536]{1,2,0:T(8,128)(2,1)} async-done(((bf16[2,128,1536]{1,2,0:T(8,128)(2,1)}), bf16[2,1024,1536]{1,2,0:T(8,128)(2,1)}) %all-gather.5.cloned.1.call-update) | async-done | bytes 6291472 | tf_op jit(solution)/shard_map/all_gather | solution.py:222
  276.4 40.0 %while.53 = (s32[]{:T(128)}, f32[2,12,128]{2,1,0:T(8,128)}, f32[2,12,128]{2,1,0:T(8,128)}, f32[2,12,128,64]{2,0,3,1:T(2,128)}, bf16[2,1024]{1,0:T(2,128)(2,1)S(1...) while((s32[]{:T(128)}, f32[2,12,128]{2,1,0:T(8,128)}, ...), condition=%wide.region_13.14_spmd, body=%wide.region_10.13_spmd.sunk | while | flops 423209472 | bytes 37837060 | solution.py:87
  283.8 2.5 fusion.259
  286.3 10.1 dynamic_update_slice.53
  303.8 2.5 fusion.259
  306.3 10.1 dynamic_update_slice.53
  317.2 2.7 fusion.116
  322.5 5.8 fusion.103
  328.4 3.7 convert_reduce_fusion
  340.6 2.4 reshape.425
  343.0 2.8 fusion.118
  347.5 3.1 broadcast.376.clone2
  350.7 41.0 %while.54 = (s32[]{:T(128)}, bf16[2,128,12,64]{1,3,2,0:T(8,128)(2,1)}, bf16[2,1024,1536]{2,1,0:T(8,128)(2,1)}, bf16[2,1024,1536]{1,2,0:T(8,128)(2,1)}, bf16[2,10...) while((s32[]{:T(128)}, ...), condition=%wide.region_20.21_spmd, body=%wide.region_19.20_spmd.sunk | while | flops 1030327296 | bytes 75220248 | solution.py:137
  355.0 2.4 multiply_convert_fusion.15
  362.7 4.6 copy.226
  367.3 3.8 constant_dynamic-update-slice_fusion.4
  383.1 4.6 copy.226
  387.8 3.8 constant_dynamic-update-slice_fusion.4
  410.1 3.0 broadcast.376.clone
  413.1 41.2 %while.55 = (s32[]{:T(128)}, bf16[2,128,12,64]{1,3,2,0:T(8,128)(2,1)}, bf16[2,1024,1536]{2,1,0:T(8,128)(2,1)}, bf16[2,1024,1536]{1,2,0:T(8,128)(2,1)}, bf16[2,10...) while((s32[]{:T(128)}, ...), condition=%wide.region_26.27_spmd, body=%wide.region_25.26_spmd.sunk | while | flops 1030327296 | bytes 75220248 | solution.py:137
  417.5 2.4 multiply_convert_fusion.16
  425.3 4.7 copy.228
  429.9 3.8 constant_dynamic-update-slice_fusion.5
  438.1 2.4 multiply_convert_fusion.16
  445.9 4.6 copy.228
  450.5 3.9 constant_dynamic-update-slice_fusion.5
  458.2 3.3 fusion.145
  464.6 3.3 fusion.146
  471.9 3.4 fusion.148
  475.4 3.2 fusion.137
  478.7 5.8 copy.201
  484.5 4.3 bitcast_bitcast_fusion
  488.8 5.3 copy.146
  496.1 2.6 copy.156
  498.8 2.9 convolution_bitcast_fusion
  501.7 4.6 copy.202
  521.4 2.4 copy.144
  523.7 4.4 multiply_reduce_fusion.1
  528.1 100.1 %reduce-scatter.10.cloned.1.call-done = bf16[2,128,1536]{2,1,0:T(8,128)(2,1)} async-done(((bf16[2,1024,1536]{2,1,0:T(8,128)(2,1)}), bf16[2,128,1536]{2,1,0:T(8,128)(2,1)}) %reduce-scatter.10.cloned.1.call-update) | async-done | bytes 786448 | tf_op jit(solution)/shard_map/reduce_scatter | solution.py:314
  628.2 4.0 multiply_reduce_fusion.3
  633.6 4.9 fusion.147
  640.5 2.3 fusion.122
  642.8 2.4 copy.140
  645.2 6.6 fusion.144
  651.9 6.4 fusion.111
  660.6 73.2 %reduce-scatter.16.cloned.1.call-done = f32[192,96]{1,0:T(8,128)} async-done(((f32[6144,96]{1,0:T(8,128)}), f32[192,96]{1,0:T(8,128)}) %reduce-scatter.16.cloned.1.call-update) | async-done | bytes 73744 | tf_op jit(solution)/shard_map/reduce_scatter | solution.py:338
  733.8 106.4 %reduce-scatter.18.cloned.1.call-done = f32[192,96]{1,0:T(8,128)} async-done(((f32[6144,96]{1,0:T(8,128)}), f32[192,96]{1,0:T(8,128)}) %reduce-scatter.18.cloned.1.call-update) | async-done | bytes 73744 | tf_op jit(solution)/shard_map/reduce_scatter | solution.py:338
  840.3 106.6 %reduce-scatter.22.cloned.1.call-done = f32[192,96]{1,0:T(8,128)} async-done(((f32[6144,96]{1,0:T(8,128)}), f32[192,96]{1,0:T(8,128)}) %reduce-scatter.22.cloned.1.call-update) | async-done | bytes 73744 | tf_op jit(solution)/shard_map/reduce_scatter | solution.py:338
  946.8 140.9 %reduce-scatter.24.cloned.1.call-done = f32[192,384]{1,0:T(8,128)} async-done(((f32[6144,384]{1,0:T(8,128)}), f32[192,384]{1,0:T(8,128)}) %reduce-scatter.24.cloned.1.call-update) | async-done | bytes 294928 | tf_op jit(solution)/shard_map/reduce_scatter | solution.py:338
  1087.7 142.1 %reduce-scatter.26.cloned.1.call-done = f32[768,96]{0,1:T(8,128)} async-done(((f32[24576,96]{0,1:T(8,128)}), f32[768,96]{0,1:T(8,128)}) %reduce-scatter.26.cloned.1.call-update) | async-done | bytes 294928 | tf_op jit(solution)/shard_map/reduce_scatter | solution.py:338
  1229.8 130.0 %all-reduce.3.cloned.1.call-done = (f32[768,12]{0,1:T(8,128)}, f32[3072]{0:T(1024)}, f32[768]{0:T(1024)}, f32[4,768]{1,0:T(4,128)}, f32[4,768]{1,0:T(4,128)}) async-done(((f32[768,12]{0,1:T(8,128)}, f32[3072]{0:T(1024)}, f32[768]{0:T(1024)}, f32[4,768]{1,0:T(4,128)}, f32[4,768]{1,0:T(4,128)}), (f32[768,12]{0,1:T(8,128)}, f32[3072]{0:T(1024)}, f32[768]{0:T(1024)}, f32[4,768]{1,0:T(4,128)}, ...) | async-done | bytes 76816 | tf_op jit(solution)/shard_map/psum | solution.py:339
  1359.8 120.5 %reduce-scatter.20.cloned.1.call-done = f32[192,192]{1,0:T(8,128)} async-done(((f32[6144,192]{1,0:T(8,128)}), f32[192,192]{1,0:T(8,128)}) %reduce-scatter.20.cloned.1.call-update) | async-done | bytes 147472 | tf_op jit(solution)/shard_map/reduce_scatter | solution.py:338
  1480.2 141.8 %reduce-scatter.14.cloned.1.call-done = f32[192,288]{1,0:T(8,128)} async-done(((f32[6144,288]{1,0:T(8,128)}), f32[192,288]{1,0:T(8,128)}) %reduce-scatter.14.cloned.1.call-update) | async-done | bytes 221200 | tf_op jit(solution)/shard_map/reduce_scatter | solution.py:338
  (433 shorter events, 187.6 us)
Async XLA Ops:
  7.2 7.3 copy-start
  7.2 114.5 %all-gather.3.cloned.1.call-start = ((), (), s32[]{:S(2)}) async-start(), calls=%async_computation.9 | async-start | bytes 7077888 | tf_op jit(solution)/shard_map/all_gather | solution.py:203
  8.8 313.6 %copy-start.47 = (f32[768]{0:T(1024)}, f32[768]{0:T(1024)S(1)}, u32[]{:S(2)}) copy-start(f32[768]{0:T(1024)S(1)} %get-tuple-element.349) | copy-start | bytes 9220
  10.3 159.5 %copy-start.50 = (f32[768]{0:T(1024)}, f32[768]{0:T(1024)S(1)}, u32[]{:S(2)}) copy-start(f32[768]{0:T(1024)S(1)} %get-tuple-element.346) | copy-start | bytes 9220
  10.3 324.6 %copy-start.39 = (f32[768]{0:T(1024)}, f32[768]{0:T(1024)S(1)}, u32[]{:S(2)}) copy-start(f32[768]{0:T(1024)S(1)} %get-tuple-element.345) | copy-start | bytes 9220
  17.6 10.4 copy-start.85
  19.9 254.1 %all-gather.5.cloned.1.call-start = ((), (), s32[]{:S(2)}) async-start(), calls=%async_computation.10 | async-start | bytes 7077888 | tf_op jit(solution)/shard_map/all_gather | solution.py:222
  164.1 6.9 copy-start.31
  164.1 5.7 copy-start.13
  164.1 5.7 copy-start.59
  164.1 5.7 copy-start.67
  164.1 5.7 copy-start.68
  164.1 5.7 copy-start.77
  164.1 5.7 copy-start.81
  167.4 6.0 copy-start.19
  167.4 4.3 copy-start.90
  170.9 4.8 copy-start.84
  175.7 345.6 %reduce-scatter.12.cloned.1.call-start = ((), (), s32[]{:S(2)}) async-start(), calls=%async_computation.12 | async-start | bytes 7077888 | tf_op jit(solution)/shard_map/reduce_scatter | solution.py:276
  316.4 6.0 copy-start.91
  317.2 11.2 slice-start.2
  322.1 12.8 copy-start.7
  322.2 12.8 copy-start.63
  322.4 12.5 copy-start.69
  322.4 5.9 copy-start.17
  322.4 5.9 slice-start.3
  322.5 9.6 slice-start
  391.6 5.7 copy-start.35
  391.7 236.5 %reduce-scatter.10.cloned.1.call-start = ((), (), s32[]{:S(2)}) async-start(), calls=%async_computation.11 | async-start | bytes 7077888 | tf_op jit(solution)/shard_map/reduce_scatter | solution.py:314
  391.9 5.5 copy-start.6
  391.9 5.5 copy-start.49
  391.9 5.5 copy-start.51
  391.9 5.5 copy-start.62
  391.9 5.5 copy-start.66
  391.9 6.9 copy-start.12
  394.8 4.0 copy-start.18
  454.4 279.4 %reduce-scatter.16.cloned.1.call-start = ((), (), s32[]{:S(2)}) async-start(), calls=%async_computation.14 | async-start | bytes 3244032 | tf_op jit(solution)/shard_map/reduce_scatter | solution.py:338
  461.5 378.7 %reduce-scatter.18.cloned.1.call-start = ((), (), s32[]{:S(2)}) async-start(), calls=%async_computation.15 | async-start | bytes 3244032 | tf_op jit(solution)/shard_map/reduce_scatter | solution.py:338
  467.9 479.0 %reduce-scatter.22.cloned.1.call-start = ((), (), s32[]{:S(2)}) async-start(), calls=%async_computation.17 | async-start | bytes 3244032 | tf_op jit(solution)/shard_map/reduce_scatter | solution.py:338
  475.4 612.3 %reduce-scatter.24.cloned.1.call-start = ((), (), s32[]{:S(2)}) async-start(), calls=%async_computation.18 | async-start | bytes 9732096 | tf_op jit(solution)/shard_map/reduce_scatter | solution.py:338
  494.2 735.6 %reduce-scatter.26.cloned.1.call-start = ((), (), s32[]{:S(2)}) async-start(), calls=%async_computation.19 | async-start | bytes 9732096 | tf_op jit(solution)/shard_map/reduce_scatter | solution.py:338
  506.3 13.1 copy-start.36
  506.3 853.4 %all-reduce.3.cloned.1.call-start = ((), (), s32[]{:S(2)}) async-start(), calls=%async_computation.20 | async-start | bytes 180224 | tf_op jit(solution)/shard_map/psum | solution.py:339
  523.7 104.5 %copy-start.58 = (f32[768]{0:T(1024)S(1)}, f32[768]{0:T(1024)}, u32[]{:S(2)}) copy-start(f32[768]{0:T(1024)} %copy-done.57) | copy-start | bytes 9220
  523.7 104.5 %copy-start.76 = (f32[256]{0:T(256)S(1)}, f32[256]{0:T(256)}, u32[]{:S(2)}) copy-start(f32[256]{0:T(256)} %copy-done.75) | copy-start | bytes 3076
  523.7 104.5 %copy-start.80 = (f32[256]{0:T(256)S(1)}, f32[256]{0:T(256)}, u32[]{:S(2)}) copy-start(f32[256]{0:T(256)} %copy-done.79) | copy-start | bytes 3076
  628.2 4.1 copy-start.83
  628.2 4.1 copy-start.71
  628.2 4.1 copy-start.73
  628.2 4.7 copy-start.72
  628.2 4.7 copy-start.74
  633.6 846.6 %reduce-scatter.20.cloned.1.call-start = ((), (), s32[]{:S(2)}) async-start(), calls=%async_computation.16 | async-start | bytes 6488064 | tf_op jit(solution)/shard_map/reduce_scatter | solution.py:338
  638.5 983.5 %reduce-scatter.14.cloned.1.call-start = ((), (), s32[]{:S(2)}) async-start(), calls=%async_computation.13 | async-start | bytes 9732096 | tf_op jit(solution)/shard_map/reduce_scatter | solution.py:338
  651.8 6.6 copy-start.89
  651.8 6.6 copy-start.88
  651.8 6.6 copy-start.87
  651.9 6.6 copy-start.86
  651.9 6.6 copy-start.14
  651.9 6.6 copy-start.29
  651.9 6.6 copy-start.60
  651.9 6.6 copy-start.78
  651.9 6.6 copy-start.82
  651.9 7.6 copy-start.8
  651.9 7.6 copy-start.10
  651.9 7.6 copy-start.30
  (65 other events, 116.7 us)
Sparse Core Ops, SparseCore 0:
  20.0 101.5 all-gather.2
  175.9 98.1 all-gather.4
  391.8 115.8 reduce-scatter.11
  511.1 117.0 reduce-scatter.9
  634.0 99.7 reduce-scatter.15
  739.7 100.5 reduce-scatter.17
  846.3 100.5 reduce-scatter.21
  953.3 134.3 reduce-scatter.23
  1095.2 134.5 reduce-scatter.25
  1236.6 123.0 all-reduce.2
  1366.0 114.1 reduce-scatter.19
  1487.5 134.4 reduce-scatter.13
where the time goes:
time: 1650 us; the launch traced here: 1640 us
  waiting for transfers between devices  1200 us (73%)
  local copies, waits for them, and re-layouts  219 us (13%)
  matrix products  115 us (7%)
  other arithmetic  47 us (3%)
  blocking collectives  32.8 us (2%)
    reduce_scatter x7, waiting for transfers between devices, body(): lax.psum_scatter(ordered, ('wide', 'blk'), scatter_dimension=0, tiled=True)  831 us
    psum x1, waiting for transfers between devices, body(): lax.psum((grad_gate_weight, grad_expand_bias, grad_reduce_bias, jnp.stack...  130 us
    reduce_scatter x1, waiting for transfers between devices, body(): lax.psum_scatter(self_carry[1].astype(jnp.bfloat16), 'blk', scatter_dimen...  100 us
    all_gather x1, waiting for transfers between devices, body(): lax.all_gather(image_pairs, 'blk', axis=1, tiled=True)  71.9 us
    all_gather x1, waiting for transfers between devices, body(): lax.all_gather(self_pairs, 'blk', axis=1, tiled=True)  71.1 us
    dynamic_update_slice x4, local copies, waits for them, and re-layouts, forward_fold(): lax.map(forward_per_doc, (queries, carried[0], carried[1], carried[2], ke...  40.4 us
    dynamic_update_slice x8, local copies, waits for them, and re-layouts, backward_fold(): lax.map(backward_per_doc, (queries, grad_out, log_sum, row_delta, key_pai...  33.9 us
  transfers between devices with their start and end apart: 12, of which 11 were waited for; matrix products, arithmetic and copies ran while one was open for 12% of the time, Pallas kernels for 0%

commit v1 on v0

v1 whole, which is shorter than its diff:
```python
import functools

import jax
import jax.numpy as jnp
from jax import lax
from jax.experimental import pallas as pl
from jax.experimental.pallas import tpu as pltpu
from jax.sharding import PartitionSpec as P

D = 768
H = 12
HD = 64
FF = 3072
PAGE = 128
DOCS = 2
ROWS = DOCS * PAGE
QUAD = 256
QUADS = D // QUAD
PAIR = 128
EPSILON = 1e-05
NEGATIVE = -1e30
HIGHEST = lax.Precision.HIGHEST
AXES = ("wide", "blk")
BF16 = jnp.bfloat16
F32 = jnp.float32
VMEM_LIMIT = 60 * 1024 * 1024


def product(left, right):
    return jnp.dot(left, right, preferred_element_type=F32)


def against(left, right, precision=None):
    return lax.dot_general(
        left, right, (((1,), (1,)), ((), ())), preferred_element_type=F32, precision=precision
    )


def transposed(left, right, precision=None):
    return lax.dot_general(
        left, right, (((0,), (0,)), ((), ())), preferred_element_type=F32, precision=precision
    )


def standardize(values):
    centred = values - jnp.mean(values, axis=-1, keepdims=True)
    inverse = lax.rsqrt(jnp.mean(centred * centred, axis=-1, keepdims=True) + EPSILON)
    return centred * inverse, inverse


def norm_back(upstream, scaled, inverse, gains):
    weighted = upstream * gains
    return inverse * (
        weighted
        - jnp.mean(weighted, axis=-1, keepdims=True)
        - scaled * jnp.mean(weighted * scaled, axis=-1, keepdims=True)
    )


def column_sum(values):
    return jnp.sum(values, axis=0, keepdims=True)


def normalize_pages(pages, gain, shift, normed):
    for index, page in enumerate(pages):
        scaled, _ = standardize(page[...].astype(F32))
        normed[index * PAGE : (index + 1) * PAGE, :] = (scaled * gain + shift).astype(BF16)


def lane_index(rows):
    return lax.broadcasted_iota(jnp.int32, (rows, PAIR), 1)


def side_masks(rows):
    lanes = lane_index(rows)
    return [(lanes < HD).astype(BF16), (lanes >= HD).astype(BF16)]


def attend_forward(q_ref, k_ref, v_ref, closed_ref, out_ref, lse_ref):
    lanes = lane_index(ROWS)
    masks = side_masks(ROWS)
    first_lane = (lanes == 0).astype(BF16)
    stats = jnp.zeros((ROWS, PAIR), F32)
    for pair in range(QUAD // PAIR):
        cols = slice(pair * PAIR, (pair + 1) * PAIR)
        keys = jnp.concatenate([k_ref[:, cols], closed_ref[...]], axis=1)
        values = v_ref[:, cols]
        queries = q_ref[:, cols]
        results = []
        for side in range(2):
            query = jnp.concatenate([queries * masks[side], first_lane], axis=1)
            scores = against(query, keys)
            top = jnp.max(scores, axis=1, keepdims=True)
            weights = jnp.exp(scores - top)
            total = jnp.sum(weights, axis=1, keepdims=True)
            results.append(product(weights.astype(BF16), values) / total)
            stats = jnp.where(lanes == pair * 2 + side, top + jnp.log(total), stats)
        out_ref[:, cols] = jnp.where(lanes < HD, results[0], results[1])
    lse_ref[...] = jnp.transpose(stats)[:8, :]


def attend_backward(q_ref, k_ref, v_ref, do_ref, lse_ref, delta_ref, closed_ref, dq_ref, dkv_ref):
    lanes = lane_index(ROWS)
    masks = side_masks(ROWS)
    first_lane = (lanes == 0).astype(BF16)
    for pair in range(QUAD // PAIR):
        cols = slice(pair * PAIR, (pair + 1) * PAIR)
        key_part = k_ref[:, cols]
        keys = jnp.concatenate([key_part, closed_ref[...]], axis=1)
        values = v_ref[:, cols]
        dq_parts = []
        dk = None
        dv = None
        for side in range(2):
            row = pair * 2 + side
            query = q_ref[:, cols] * masks[side]
            grad_out = do_ref[:, cols] * masks[side]
            scores = against(keys, jnp.concatenate([query, first_lane], axis=1))
            weights = jnp.exp(scores - lse_ref[row : row + 1, :])
            grad_weights = against(values, grad_out)
            grad_scores = (weights * (grad_weights - delta_ref[row : row + 1, :])).astype(BF16)
            dv_part = product(weights.astype(BF16), grad_out)
            dk_part = product(grad_scores, query)
            dv = dv_part if dv is None else dv + dv_part
            dk = dk_part if dk is None else dk + dk_part
            dq_parts.append(transposed(grad_scores, key_part))
        dq_ref[:, cols] = (jnp.where(lanes < HD, dq_parts[0], dq_parts[1]) * HD ** (-0.5)).astype(
            BF16
        )
        dkv_ref[:, cols] = dk.astype(BF16)
        dkv_ref[:, QUAD + pair * PAIR : QUAD + (pair + 1) * PAIR] = dv.astype(BF16)


def head_sums(values):
    sums = []
    lanes = lane_index(values.shape[0])
    for pair in range(H // 2):
        part = values[:, pair * PAIR : (pair + 1) * PAIR]
        sums.append(jnp.sum(jnp.where(lanes < HD, part, 0.0), axis=1, keepdims=True))
        sums.append(jnp.sum(jnp.where(lanes >= HD, part, 0.0), axis=1, keepdims=True))
    return sums


def head_rows(sums):
    lanes = lane_index(ROWS)
    stats = jnp.zeros((ROWS, PAIR), F32)
    for head, value in enumerate(sums):
        stats = jnp.where(lanes == (head // 4) * 8 + head % 4, value, stats)
    return jnp.transpose(stats)[: 8 * QUADS, :]


def spread_heads(gates):
    lanes = lane_index(gates.shape[0])
    parts = []
    for pair in range(H // 2):
        parts.append(
            jnp.where(lanes < HD, gates[:, 2 * pair : 2 * pair + 1], gates[:, 2 * pair + 1 : 2 * pair + 2])
        )
    return jnp.concatenate(parts, axis=1)


def store_tiles(out_ref, rows, value):
    cuts = out_ref.shape[0]
    lanes = out_ref.shape[2]
    for cut in range(cuts):
        out_ref[cut, rows, :] = value[:, cut * lanes : (cut + 1) * lanes].astype(BF16)


def self_forward_kernel(count, *refs):
    pages = refs[:count]
    gain, shift, closed, wq, wk, wv, out, lse, q_out, k_out, v_out, normed = refs[count:]

    @pl.when(pl.program_id(0) == 0)
    def _():
        normalize_pages(pages, gain[0:1, :], shift[0:1, :], normed)

    q_out[...] = (product(normed[0:ROWS, :], wq[...]).astype(BF16) * HD ** (-0.5)).astype(BF16)
    k_out[...] = product(normed[...], wk[...]).astype(BF16)
    v_out[...] = product(normed[...], wv[...]).astype(BF16)
    attend_forward(q_out, k_out, v_out, closed, out, lse)


def cross_forward_kernel(count, *refs):
    texts = refs[:DOCS]
    pages = refs[DOCS : DOCS + count]
    (
        self_out, w_self, w_gate, gain, shift, closed, wq, wk, wv,
        hidden, gate, out, lse, q_out, k_out, v_out, normed, cross,
    ) = refs[DOCS + count :]

    @pl.when(pl.program_id(0) == 0)
    def _():
        normalize_pages(pages, gain[2:3, :], shift[2:3, :], normed)
        branch = product(self_out[...].astype(BF16), w_self[...])
        for index, text in enumerate(texts):
            rows = slice(index * PAGE, (index + 1) * PAGE)
            hidden[rows, :] = text[...].astype(F32) + branch[rows, :]
        scaled, _ = standardize(hidden[...])
        cross[...] = (scaled * gain[1:2, :] + shift[1:2, :]).astype(BF16)
        gate[...] = jax.nn.sigmoid(product(cross[...], w_gate[...]))

    q_out[...] = (product(cross[...], wq[...]).astype(BF16) * HD ** (-0.5)).astype(BF16)
    k_out[...] = product(normed[...], wk[...]).astype(BF16)
    v_out[...] = product(normed[...], wv[...]).astype(BF16)
    attend_forward(q_out, k_out, v_out, closed, out, lse)


def forward_back_kernel(
    steps, hidden, raw, gate, cot0, cot1, w_out, gain, shift, w_expand, b_expand, w_reduce, b_reduce,
    joined, d_expand, d_reduce, d_out, grad_mixed, grad_raw, delta, grad_logit, d_bias, small,
    gated, mixed, final, upstream, joined_sum, back_sum,
):
    step = pl.program_id(0)

    @pl.when(step == 0)
    def _():
        upstream[0:PAGE, :] = cot0[...]
        upstream[PAGE:ROWS, :] = cot1[...]
        gated[...] = (spread_heads(gate[...]) * raw[...]).astype(BF16)
        rows = hidden[...] + product(gated[...], w_out[...])
        mixed[...] = rows
        scaled, _ = standardize(rows)
        final[...] = (scaled * gain[3:4, :] + shift[3:4, :]).astype(BF16)
        joined_sum[...] = rows + b_reduce[...]
        back_sum[...] = jnp.zeros_like(back_sum)

    inner = product(final[...], w_expand[...]) + b_expand[...]
    squared = inner * inner
    root = (2.0 / jnp.pi) ** 0.5
    curve = jnp.tanh(root * inner * (1.0 + 0.044715 * squared))
    half = 0.5 * (1.0 + curve)
    active = (inner * half).astype(BF16)
    slope = half + 0.5 * inner * (1.0 - curve * curve) * (root * (1.0 + 3.0 * 0.044715 * squared))
    joined_sum[...] += product(active, w_reduce[...])
    grad_active = against(upstream[...], w_reduce[...]).astype(BF16)
    grad_inner = (grad_active.astype(F32) * slope).astype(BF16)
    d_bias[...] = column_sum(grad_inner.astype(F32))
    back_sum[...] += against(grad_inner, w_expand[...])
    store_tiles(d_expand, slice(None), transposed(grad_inner, final[...]))
    store_tiles(d_reduce, slice(None), transposed(upstream[...], active))

    @pl.when(step == steps - 1)
    def _():
        joined[...] = joined_sum[...].astype(BF16)
        scaled, inverse = standardize(mixed[...])
        back = back_sum[...]
        cotangent = upstream[...].astype(F32)
        grad = cotangent + norm_back(back, scaled, inverse, gain[3:4, :])
        grad_mixed[...] = grad
        branch = grad.astype(BF16)
        store_tiles(d_out, slice(None), transposed(branch, gated[...]))
        grad_gated = against(branch, w_out[...]).astype(BF16).astype(F32)
        gates = gate[...]
        lanes = lane_index(ROWS)
        logit = jnp.zeros((ROWS, PAIR), F32)
        for head, value in enumerate(head_sums(grad_gated * raw[...])):
            logit = jnp.where(lanes == head, value, logit)
        grad_logit[...] = logit * gates * (1.0 - gates)
        rounded = (spread_heads(gates) * grad_gated).astype(BF16)
        grad_raw[...] = rounded
        delta[...] = head_rows(head_sums(rounded.astype(F32) * raw[...]))
        small[...] = jnp.concatenate(
            [
                column_sum(cotangent),
                column_sum(back * scaled),
                column_sum(back),
                jnp.zeros((5, D), F32),
            ],
            axis=0,
        )


def spread_back(normed, dkv, wk, wv, dx, dw_k, dw_v, k_rows, v_rows):
    store_tiles(dw_k, k_rows, transposed(dkv[:, :QUAD], normed[...]))
    store_tiles(dw_v, v_rows, transposed(dkv[:, QUAD:], normed[...]))
    weights = jnp.concatenate([wk[...], wv[...]], axis=1)

    def chunk(index, carry):
        rows = pl.ds(pl.multiple_of(index * ROWS, ROWS), ROWS)
        dx[rows, :] += against(dkv[rows, :], weights)
        return carry

    lax.fori_loop(0, dx.shape[0] // ROWS, chunk, 0)


def finish_pages(pages, dx, keep, send):
    gain_sum = jnp.zeros((1, D), F32)
    shift_sum = jnp.zeros((1, D), F32)
    half = len(pages) // 2
    for index, page in enumerate(pages):
        scaled, _ = standardize(page[...].astype(F32))
        part = dx[index * PAGE : (index + 1) * PAGE, :]
        gain_sum += column_sum(part * scaled)
        shift_sum += column_sum(part)
        target = keep if index < half else send
        place = index % half
        target[place * PAGE : (place + 1) * PAGE, :] = part.astype(BF16)
    return gain_sum, shift_sum


def cross_back_kernel(count, *refs):
    pages = refs[:count]
    (
        gain, shift, closed, q_in, k_in, v_in, do_in, lse, delta, wk, wv,
        w_query, w_gate, w_self, hidden, self_out, grad_mixed, grad_logit,
        keep, send, dw_pairs, dw_query, dw_self, dw_gate, grad_hidden, self_do, self_delta, small,
        normed, dkv, dx, dq,
    ) = refs[count:]
    step = pl.program_id(0)

    @pl.when(step == 0)
    def _():
        normalize_pages(pages, gain[2:3, :], shift[2:3, :], normed)
        dx[...] = jnp.zeros_like(dx)

    cols = pl.ds(pl.multiple_of(step * QUAD, QUAD), QUAD)
    attend_backward(
        q_in, k_in, v_in, do_in, lse, delta, closed, dq.at[:, cols], dkv
    )
    spread_back(
        normed, dkv, wk, wv, dx, dw_pairs, dw_pairs,
        cols, pl.ds(pl.multiple_of(D + step * QUAD, QUAD), QUAD),
    )

    @pl.when(step == QUADS - 1)
    def _():
        image_gain, image_shift = finish_pages(pages, dx, keep, send)
        scaled, inverse = standardize(hidden[...])
        cross = (scaled * gain[1:2, :] + shift[1:2, :]).astype(BF16)
        grad_query = dq[...]
        store_tiles(dw_query, slice(None), transposed(grad_query, cross))
        dw_gate[...] = transposed(grad_logit[...], cross.astype(F32), HIGHEST)[:16, :]
        upstream = against(grad_query, w_query[...]) + against(
            grad_logit[...], w_gate[...].astype(F32), HIGHEST
        )
        grad = grad_mixed[...] + norm_back(upstream, scaled, inverse, gain[1:2, :])
        grad_hidden[...] = grad
        branch = grad.astype(BF16)
        store_tiles(dw_self, slice(None), transposed(branch, self_out[...].astype(BF16)))
        grad_result = against(branch, w_self[...]).astype(BF16)
        self_do[...] = grad_result
        self_delta[...] = head_rows(head_sums(grad_result.astype(F32) * self_out[...]))
        small[...] = jnp.concatenate(
            [
                column_sum(upstream * scaled),
                column_sum(upstream),
                image_gain,
                image_shift,
                jnp.zeros((4, D), F32),
            ],
            axis=0,
        )


def self_back_kernel(count, *refs):
    pages = refs[:count]
    (
        gain, shift, closed, q_in, k_in, v_in, do_in, lse, delta, wq, wk, wv,
        keep, send, dw_project, small,
        normed, dkv, dx, dq,
    ) = refs[count:]
    step = pl.program_id(0)

    @pl.when(step == 0)
    def _():
        normalize_pages(pages, gain[0:1, :], shift[0:1, :], normed)
        dx[...] = jnp.zeros_like(dx)

    attend_backward(q_in, k_in, v_in, do_in, lse, delta, closed, dq, dkv)
    spread_back(
        normed, dkv, wk, wv, dx, dw_project, dw_project,
        pl.ds(pl.multiple_of(D + step * QUAD, QUAD), QUAD),
        pl.ds(pl.multiple_of(2 * D + step * QUAD, QUAD), QUAD),
    )
    store_tiles(
        dw_project,
        pl.ds(pl.multiple_of(step * QUAD, QUAD), QUAD),
        transposed(dq[...], normed[0:ROWS, :]),
    )
    dx[0:ROWS, :] += against(dq[...], wq[...])

    @pl.when(step == QUADS - 1)
    def _():
        gain_sum, shift_sum = finish_pages(pages, dx, keep, send)
        small[...] = jnp.concatenate([gain_sum, shift_sum, jnp.zeros((6, D), F32)], axis=0)


def norm_back_kernel(index, added, *refs):
    pages = refs[:DOCS]
    gain, mine, other = refs[DOCS : DOCS + 3]
    rest = refs[DOCS + 3 :]
    for place, page in enumerate(pages):
        rows = slice(place * PAGE, (place + 1) * PAGE)
        scaled, inverse = standardize(page[...].astype(F32))
        upstream = mine[rows, :].astype(F32) + other[rows, :].astype(F32)
        grad = norm_back(upstream, scaled, inverse, gain[index : index + 1, :])
        if added:
            grad = grad + rest[0][rows, :]
        rest[-1][place] = grad.astype(BF16)


def whole(shape):
    return pl.BlockSpec(shape, lambda step: (0,) * len(shape))


def columns(rows, offset=0):
    return pl.BlockSpec((rows, QUAD), lambda step: (0, offset + step))


def stat_rows():
    return pl.BlockSpec((8, ROWS), lambda step: (step, 0))


def shaped(shape, kind):
    return jax.ShapeDtypeStruct(shape, kind)


def call(kernel, name, steps, ins, outs, scratch, flops, byte_count):
    in_specs, operands = zip(*ins)
    out_specs, out_shapes = zip(*outs)
    return pl.pallas_call(
        kernel,
        grid=(steps,),
        in_specs=list(in_specs),
        out_specs=list(out_specs),
        out_shape=list(out_shapes),
        scratch_shapes=scratch,
        name=name,
        compiler_params=pltpu.CompilerParams(vmem_limit_bytes=VMEM_LIMIT),
        cost_estimate=pl.CostEstimate(flops=flops, bytes_accessed=byte_count, transcendentals=0),
    )(*operands)


def page_inputs(pages):
    return [(whole((PAGE, D)), page) for page in pages]


def self_forward(pages, gain, shift, closed, project):
    keys = len(pages) * PAGE
    return call(
        functools.partial(self_forward_kernel, len(pages)),
        "self_forward",
        QUADS,
        page_inputs(pages)
        + [
            (whole(gain.shape), gain),
            (whole(shift.shape), shift),
            (whole(closed.shape), closed),
            (columns(D), project),
            (columns(D, QUADS), project),
            (columns(D, 2 * QUADS), project),
        ],
        [
            (columns(ROWS), shaped((ROWS, D), F32)),
            (stat_rows(), shaped((8 * QUADS, ROWS), F32)),
            (columns(ROWS), shaped((ROWS, D), BF16)),
            (columns(keys), shaped((keys, D), BF16)),
            (columns(keys), shaped((keys, D), BF16)),
        ],
        [pltpu.VMEM((keys, D), BF16)],
        6 * 10**9,
        12 * 10**6,
    )


def cross_forward(texts, pages, self_out, w_self, w_gate, gain, shift, closed, w_query, w_pairs):
    keys = len(pages) * PAGE
    return call(
        functools.partial(cross_forward_kernel, len(pages)),
        "cross_forward",
        QUADS,
        page_inputs(texts)
        + page_inputs(pages)
        + [
            (whole(self_out.shape), self_out),
            (whole(w_self.shape), w_self),
            (whole(w_gate.shape), w_gate),
            (whole(gain.shape), gain),
            (whole(shift.shape), shift),
            (whole(closed.shape), closed),
            (columns(D), w_query),
            (columns(D), w_pairs),
            (columns(D, QUADS), w_pairs),
        ],
        [
            (whole((ROWS, D)), shaped((ROWS, D), F32)),
            (whole((ROWS, PAIR)), shaped((ROWS, PAIR), F32)),
            (columns(ROWS), shaped((ROWS, D), F32)),
            (stat_rows(), shaped((8 * QUADS, ROWS), F32)),
            (columns(ROWS), shaped((ROWS, D), BF16)),
            (columns(keys), shaped((keys, D), BF16)),
            (columns(keys), shaped((keys, D), BF16)),
        ],
        [pltpu.VMEM((keys, D), BF16), pltpu.VMEM((ROWS, D), BF16)],
        7 * 10**9,
        14 * 10**6,
    )


def forward_back(
    hidden, raw, gate, cots, w_out, gain, shift, w_expand, b_expand, w_reduce, b_reduce, cuts, far_cuts
):
    steps = FF // D
    far = FF // far_cuts
    if far >= D:
        far_spec = pl.BlockSpec((1, D, D), lambda step: (step * D // far, 0, (step * D % far) // D))
    else:
        far_spec = pl.BlockSpec((D // far, D, far), lambda step: (step, 0, 0))
    return call(
        functools.partial(forward_back_kernel, steps),
        "forward_back",
        steps,
        [
            (whole((ROWS, D)), hidden),
            (whole((ROWS, D)), raw),
            (whole((ROWS, PAIR)), gate),
        ]
        + page_inputs(cots)
        + [
            (whole((D, D)), w_out),
            (whole(gain.shape), gain),
            (whole(shift.shape), shift),
            (pl.BlockSpec((D, D), lambda step: (0, step)), w_expand),
            (pl.BlockSpec((1, D), lambda step: (0, step)), b_expand),
            (pl.BlockSpec((D, D), lambda step: (step, 0)), w_reduce),
            (whole((1, D)), b_reduce),
        ],
        [
            (whole((ROWS, D)), shaped((ROWS, D), BF16)),
            (
                pl.BlockSpec((cuts, D, D // cuts), lambda step: (0, step, 0)),
                shaped((cuts, FF, D // cuts), BF16),
            ),
            (far_spec, shaped((far_cuts, D, far), BF16)),
            (whole((cuts, D, D // cuts)), shaped((cuts, D, D // cuts), BF16)),
            (whole((ROWS, D)), shaped((ROWS, D), F32)),
            (whole((ROWS, D)), shaped((ROWS, D), BF16)),
            (whole((8 * QUADS, ROWS)), shaped((8 * QUADS, ROWS), F32)),
            (whole((ROWS, PAIR)), shaped((ROWS, PAIR), F32)),
            (pl.BlockSpec((1, D), lambda step: (0, step)), shaped((1, FF), F32)),
            (whole((8, D)), shaped((8, D), F32)),
        ],
        [
            pltpu.VMEM((ROWS, D), BF16),
            pltpu.VMEM((ROWS, D), F32),
            pltpu.VMEM((ROWS, D), BF16),
            pltpu.VMEM((ROWS, D), BF16),
            pltpu.VMEM((ROWS, D), F32),
            pltpu.VMEM((ROWS, D), F32),
        ],
        8 * 10**9,
        25 * 10**6,
    )


def back_scratch(keys, dq_columns):
    return [
        pltpu.VMEM((keys, D), BF16),
        pltpu.VMEM((keys, 2 * QUAD), BF16),
        pltpu.VMEM((keys, D), F32),
        pltpu.VMEM((ROWS, dq_columns), BF16),
    ]


def cross_back(
    pages, gain, shift, closed, q, k, v, grad_out, lse, delta, w_pairs,
    w_query, w_gate, w_self, hidden, self_out, grad_mixed, grad_logit, cuts,
):
    keys = len(pages) * PAGE
    half = keys // 2
    return call(
        functools.partial(cross_back_kernel, len(pages)),
        "cross_back",
        QUADS,
        page_inputs(pages)
        + [
            (whole(gain.shape), gain),
            (whole(shift.shape), shift),
            (whole(closed.shape), closed),
            (columns(ROWS), q),
            (columns(keys), k),
            (columns(keys), v),
            (columns(ROWS), grad_out),
            (stat_rows(), lse),
            (stat_rows(), delta),
            (columns(D), w_pairs),
            (columns(D, QUADS), w_pairs),
            (whole((D, D)), w_query),
            (whole((D, PAIR)), w_gate),
            (whole((D, D)), w_self),
            (whole((ROWS, D)), hidden),
            (whole((ROWS, D)), self_out),
            (whole((ROWS, D)), grad_mixed),
            (whole((ROWS, PAIR)), grad_logit),
        ],
        [
            (whole((half, D)), shaped((half, D), BF16)),
            (whole((half, D)), shaped((half, D), BF16)),
            (whole((cuts, 2 * D, D // cuts)), shaped((cuts, 2 * D, D // cuts), BF16)),
            (whole((cuts, D, D // cuts)), shaped((cuts, D, D // cuts), BF16)),
            (whole((cuts, D, D // cuts)), shaped((cuts, D, D // cuts), BF16)),
            (whole((16, D)), shaped((16, D), F32)),
            (whole((ROWS, D)), shaped((ROWS, D), F32)),
            (whole((ROWS, D)), shaped((ROWS, D), BF16)),
            (whole((8 * QUADS, ROWS)), shaped((8 * QUADS, ROWS), F32)),
            (whole((8, D)), shaped((8, D), F32)),
        ],
        back_scratch(keys, D),
        12 * 10**9,
        20 * 10**6,
    )


def self_back(pages, gain, shift, closed, q, k, v, grad_out, lse, delta, project, cuts):
    keys = len(pages) * PAGE
    half = keys // 2
    return call(
        functools.partial(self_back_kernel, len(pages)),
        "self_back",
        QUADS,
        page_inputs(pages)
        + [
            (whole(gain.shape), gain),
            (whole(shift.shape), shift),
            (whole(closed.shape), closed),
            (columns(ROWS), q),
            (columns(keys), k),
            (columns(keys), v),
            (columns(ROWS), grad_out),
            (stat_rows(), lse),
            (stat_rows(), delta),
            (columns(D), project),
            (columns(D, QUADS), project),
            (columns(D, 2 * QUADS), project),
        ],
        [
            (whole((half, D)), shaped((half, D), BF16)),
            (whole((half, D)), shaped((half, D), BF16)),
            (whole((cuts, 3 * D, D // cuts)), shaped((cuts, 3 * D, D // cuts), BF16)),
            (whole((8, D)), shaped((8, D), F32)),
        ],
        back_scratch(keys, QUAD),
        11 * 10**9,
        17 * 10**6,
    )


def final_norm(index, pages, gain, mine, other, added):
    ins = page_inputs(pages) + [
        (whole(gain.shape), gain),
        (whole((ROWS, D)), mine),
        (whole((ROWS, D)), other),
    ]
    if added is not None:
        ins.append((whole((ROWS, D)), added))
    (result,) = call(
        functools.partial(norm_back_kernel, index, added is not None),
        "final_norm",
        1,
        ins,
        [(whole((DOCS, PAGE, D)), shaped((DOCS, PAGE, D), BF16))],
        [],
        10**7,
        3 * 10**6,
    )
    return result


class Layout:
    def __init__(self):
        self.wide = lax.axis_size("wide")
        self.blk = lax.axis_size("blk")
        self.part = self.blk // 4
        self.w = lax.axis_index("wide")
        self.b = lax.axis_index("blk")
        self.turn = lax.rem(self.b // self.part, 2)
        self.bits = {}
        for bit in range(self.wide.bit_length() - 1):
            self.bits["w", bit] = (self.w >> bit) & 1
        for bit in range(self.blk.bit_length() - 1):
            self.bits["b", bit] = (self.b >> bit) & 1

    def exchange(self, value, move):
        pairs = []
        for w in range(self.wide):
            for b in range(self.blk):
                to_w, to_b = move(w, b)
                pairs.append((w * self.blk + b, to_w * self.blk + to_b))
        return lax.ppermute(value, AXES, pairs)

    def flip(self, value, name):
        axis, bit = name
        if axis == "w":
            return self.exchange(value, lambda w, b: (w ^ (1 << bit), b))
        return self.exchange(value, lambda w, b: (w, b ^ (1 << bit)))

    def swap(self, value, turn):
        def move(w, b):
            quarter, rest = divmod(b, self.part)
            return (w - w % 2 + quarter // 2, (2 * (w % 2) + ((quarter % 2) ^ turn)) * self.part + rest)

        return self.exchange(value, move)

    def to_group(self, value):
        return [
            self.swap(
                lax.dynamic_index_in_dim(value, self.turn ^ turn, 0, keepdims=False), turn
            )
            for turn in range(DOCS)
        ]

    def from_group(self, pages):
        first, second = (self.swap(page, turn) for turn, page in enumerate(pages))
        flag = self.turn == 0
        return jnp.stack([jnp.where(flag, first, second), jnp.where(flag, second, first)])

    def group_bits(self):
        return [("b", bit) for bit in range(self.part.bit_length() - 1)] + [("w", 0)]

    def gather(self, page):
        pages = [page]
        for name in self.group_bits():
            pages = pages + [self.flip(item, name) for item in pages]
        return pages

    def group_sum(self, keep, send):
        names = self.group_bits()
        for name in reversed(names):
            got = self.flip(send, name)
            if name == names[0]:
                return keep, got
            half = keep.shape[0] // 2
            keep, send = (keep[:half] + got[:half]), (keep[half:] + got[half:])

    def reduce_scatter(self, grads, order):
        wide_names = [("w", bit) for bit in range(self.wide.bit_length() - 2, 0, -1)]
        blk_names = [("b", bit) for bit in range(self.blk.bit_length() - 2, -1, -1)]
        names = wide_names + blk_names + [("w", 0)]
        parts = [
            grad.reshape((2,) * len(names) + (grad.shape[1] // (2 * self.blk), grad.shape[2]))
            for grad in grads
        ]
        for name in order:
            axis = names.index(name)
            names.remove(name)
            bit = self.bits[name]

            def pick(index):
                picked = [
                    lax.dynamic_index_in_dim(part, index, axis, keepdims=False) for part in parts
                ]
                return picked[0] if len(picked) == 1 else jnp.concatenate(picked, axis=-2)

            parts = [pick(bit) + self.flip(pick(1 - bit), name)]
        return parts[0]

    def finish(self, piece):
        rows, lanes = piece.shape
        halves = jnp.stack([piece[:, : lanes // 2], piece[:, lanes // 2 :]])
        bit = self.bits["w", 0]
        mine = lax.dynamic_index_in_dim(halves, bit, 0, keepdims=False)
        other = self.flip(lax.dynamic_index_in_dim(halves, 1 - bit, 0, keepdims=False), ("w", 0))
        flag = bit == 0
        return jnp.stack([jnp.where(flag, mine, other), jnp.where(flag, other, mine)])

    def tiles(self, piece, counts):
        both = self.finish(piece)
        results = []
        start = 0
        for count in counts:
            part = both[:, start : start + count, :]
            start += count
            results.append(jnp.transpose(part.reshape(-1, part.shape[-1])).astype(F32))
        return results

    def all_sum(self, value):
        for name in self.bits:
            value = value + self.flip(value, name)
        return value


def cut_lanes(grad, cuts):
    if grad.shape[0] == cuts:
        return grad
    _, rows, lanes = grad.shape
    return jnp.transpose(grad.reshape(rows, cuts, lanes // cuts), (1, 0, 2))


def body(
    text_blocks,
    image_blocks,
    cotangent,
    text_mask,
    page_regions,
    doc_pages,
    self_project,
    self_output,
    cross_query,
    cross_pairs,
    cross_output,
    gate_weight,
    expand_weight,
    expand_bias,
    reduce_weight,
    reduce_bias,
    norm_gain,
    norm_bias,
):
    lay = Layout()
    blk_count = lay.blk
    wide_half = lay.wide // 2
    cuts = wide_half if (D // wide_half) % PAIR == 0 else 1
    far_cuts = wide_half if (FF // wide_half) % PAIR == 0 else 1

    offsets = jnp.arange(PAGE, dtype=jnp.int32)
    living = (lay.b < doc_pages)[:, None]
    text_open = living & ((text_mask > 0) | (offsets[None, :] == 0))
    image_open = living & (offsets[None, :] < page_regions)
    closed_here = jnp.where(
        jnp.concatenate([text_open, image_open], axis=1), 0.0, NEGATIVE
    ).astype(BF16)

    text_own = lay.to_group(text_blocks)
    text_sets = [lay.gather(page) for page in text_own]
    text_pages = [page for pair in zip(*text_sets) for page in pair]

    masks = jnp.stack(lay.to_group(closed_here))
    for name in lay.group_bits():
        masks = jnp.concatenate([masks, lay.flip(masks, name)], axis=0)
    keys = masks.shape[0] * PAGE
    first_lane = jnp.arange(PAIR)[None, :] == 0

    def closed_column(part):
        return jnp.where(first_lane, part.reshape(keys, 1), 0.0).astype(BF16)

    text_closed = closed_column(masks[:, :PAGE])
    image_closed = closed_column(masks[:, PAGE:])

    image_own = lay.to_group(image_blocks)
    image_sets = [lay.gather(page) for page in image_own]
    image_pages = [page for pair in zip(*image_sets) for page in pair]
    cots = lay.to_group(cotangent)

    gate_wide = jnp.pad(gate_weight, ((0, 0), (0, PAIR - H)))

    self_out, self_lse, self_q, self_k, self_v = self_forward(
        text_pages, norm_gain, norm_bias, text_closed, self_project
    )
    hidden, gate, raw, cross_lse, cross_q, cross_k, cross_v = cross_forward(
        text_own, image_pages, self_out, self_output, gate_wide, norm_gain, norm_bias,
        image_closed, cross_query, cross_pairs,
    )
    (
        joined, d_expand, d_reduce, d_cross_output, grad_mixed, grad_raw, cross_delta, grad_logit,
        d_expand_bias, small_last,
    ) = forward_back(
        hidden, raw, gate, cots, cross_output, norm_gain, norm_bias, expand_weight,
        expand_bias.reshape(1, FF), reduce_weight, reduce_bias.reshape(1, D), cuts, far_cuts,
    )
    wide_bits = [("w", bit) for bit in range(1, lay.wide.bit_length() - 1)]
    low_blk = [("b", 0)]
    high_blk = [("b", bit) for bit in range(1, blk_count.bit_length() - 1)]
    core = [("w", 0)]
    expand_piece = lay.reduce_scatter([cut_lanes(d_expand, wide_half)], core + wide_bits + high_blk + low_blk)
    reduce_piece = lay.reduce_scatter([cut_lanes(d_reduce, wide_half)], core + low_blk + high_blk + wide_bits)
    joined_blocks = lay.from_group([joined[:PAGE], joined[PAGE:]])

    (
        image_keep, image_send, d_pairs, d_query, d_self_output, d_gate, grad_hidden, self_do,
        self_delta, small_cross,
    ) = cross_back(
        image_pages, norm_gain, norm_bias, image_closed, cross_q, cross_k, cross_v, grad_raw,
        cross_lse, cross_delta, cross_pairs, cross_query, gate_wide, self_output, hidden, self_out,
        grad_mixed, grad_logit, cuts,
    )
    cross_piece = lay.reduce_scatter(
        [cut_lanes(item, wide_half) for item in (d_pairs, d_query, d_cross_output, d_self_output)],
        core + wide_bits + low_blk + high_blk,
    )
    image_mine, image_other = lay.group_sum(image_keep, image_send)
    image_back = final_norm(2, image_own, norm_gain, image_mine, image_other, None)
    image_grad = lay.from_group([image_back[0], image_back[1]])
    small_first = lay.all_sum(
        jnp.concatenate([d_gate, d_expand_bias.reshape(-1, D), small_last[:4], small_cross[:4]], axis=0)
    )

    text_keep, text_send, d_project, small_self = self_back(
        text_pages, norm_gain, norm_bias, text_closed, self_q, self_k, self_v, self_do,
        self_lse, self_delta, self_project, cuts,
    )
    text_mine, text_other = lay.group_sum(text_keep, text_send)
    text_back = final_norm(0, text_own, norm_gain, text_mine, text_other, grad_hidden)
    text_grad = lay.from_group([text_back[0], text_back[1]])
    project_piece = lay.reduce_scatter(
        [cut_lanes(d_project, wide_half)], core + low_blk + wide_bits + high_blk
    )
    small_second = lay.all_sum(small_self)

    share = 2 * blk_count
    (grad_expand_weight,) = lay.tiles(expand_piece, [FF // share])
    (grad_reduce_weight,) = lay.tiles(reduce_piece, [D // share])
    grad_cross_pairs, grad_cross_query, grad_cross_output, grad_self_output = lay.tiles(
        cross_piece, [2 * D // share, D // share, D // share, D // share]
    )
    (grad_self_project,) = lay.tiles(project_piece, [3 * D // share])
    grad_gate_weight = jnp.transpose(small_first[:H])
    at_bias = 16
    at_last = at_bias + FF // D
    at_cross = at_last + 4
    return (
        joined_blocks,
        text_grad,
        image_grad,
        grad_self_project,
        grad_self_output,
        grad_cross_query,
        grad_cross_pairs,
        grad_cross_output,
        grad_expand_weight,
        grad_reduce_weight,
        grad_gate_weight,
        small_first[at_bias:at_last].reshape(FF),
        small_first[at_last],
        jnp.stack(
            [
                small_second[0],
                small_first[at_cross],
                small_first[at_cross + 2],
                small_first[at_last + 1],
            ]
        ),
        jnp.stack(
            [
                small_second[1],
                small_first[at_cross + 1],
                small_first[at_cross + 3],
                small_first[at_last + 2],
            ]
        ),
    )


def solution(mesh):
    rows = P("wide", "blk", None)
    return jax.shard_map(
        body,
        mesh=mesh,
        in_specs=(rows,) * 3 + (P("wide", "blk"),) * 2 + (P("wide"),) + (P(),) * 12,
        out_specs=(rows,) * 3 + (P("wide", "blk"),) * 7 + (P(),) * 5,
        check_vma=False,
    )
```

time: 1650 us -> 390 us (0.24)
  waiting for transfers between devices: 1200 us -> 130 us
  local copies, waits for them, and re-layouts: 219 us -> 35.4 us
  matrix products: 115 us -> 0 us
  Pallas kernels: 0 us -> 107 us
  starting transfers between devices: 1.14 us -> 83.7 us
  blocking collectives: 32.8 us -> 0 us
  other arithmetic: 47 us -> 25.3 us
    reduce_scatter x9 -> x0, waiting for transfers between devices: 932 us -> none  [the longest x7 831 us: body(): lax.psum_scatter(ordered, ('wide', 'blk'), scatter_dimension=0, tiled=True)]
    all_gather x2 -> x0, waiting for transfers between devices: 143 us -> none  [the longest x1 71.9 us: body(): lax.all_gather(image_pairs, 'blk', axis=1, tiled=True)]
    ppermute x0 -> x66, waiting for transfers between devices: none -> 130 us  [exchange(): return lax.ppermute(value, AXES, pairs)]
    psum x1 -> x0, waiting for transfers between devices: 130 us -> none  [body(): lax.psum((grad_gate_weight, grad_expand_bias, grad_reduce_bias, jnp.stack...]
    dot_general x52 -> x0, matrix products: 115 us -> none  [the longest x7 27.7 us: transposed(): lax.dot_general(left, right, (((0,), (0,)), ((), ())), preferred_element_...]
    pallas_call x0 -> x7, Pallas kernels: none -> 107 us  [call(): pl.pallas_call(kernel, grid=(steps,), in_specs=list(in_specs), out_specs=...]
    ppermute x0 -> x66, starting transfers between devices: none -> 83.7 us  [exchange(): return lax.ppermute(value, AXES, pairs)]
    dynamic_update_slice x12 -> x0, local copies, waits for them, and re-layouts: 74.3 us -> none  [the longest x4 40.4 us: forward_fold(): lax.map(forward_per_doc, (queries, carried[0], carried[1], carried[2], ke...]
  transfers between devices with their start and end apart: 12 -> 66, of which waited for: 11 -> 24; matrix products, arithmetic and copies ran while one was open for 12% -> 13% of each run, Pallas kernels for 0% -> 23%
where the time goes in v1:
time: 390 us; the launch traced here: 384 us
  waiting for transfers between devices  130 us (33%)
  Pallas kernels  107 us (27%)
  starting transfers between devices  83.7 us (21%)
  local copies, waits for them, and re-layouts  35.4 us (9%)
  other arithmetic  25.3 us (6%)
    ppermute x66, waiting for transfers between devices, exchange(): return lax.ppermute(value, AXES, pairs)  130 us
    pallas_call x7, Pallas kernels, call(): pl.pallas_call(kernel, grid=(steps,), in_specs=list(in_specs), out_specs=...  107 us
    ppermute x66, starting transfers between devices, exchange(): return lax.ppermute(value, AXES, pairs)  83.7 us
    squeeze x22, local copies, waits for them, and re-layouts, pick(): lax.dynamic_index_in_dim(part, index, axis, keepdims=False)  15.3 us
    add x20, other arithmetic, reduce_scatter(): parts = [pick(bit) + self.flip(pick(1 - bit), name)]  12.2 us
  transfers between devices with their start and end apart: 66, of which 24 were waited for; matrix products, arithmetic and copies ran while one was open for 13% of the time, Pallas kernels for 23%

profile of v1, /device:TPU:1, one launch (start us, length us, event | category | flops | bytes accessed | tf_op | source)
XLA Modules:
  0.0 383.7 jit_solution(10110104432407222813)
XLA Ops:
  2.2 5.6 %collective-permute-start.16 = (bf16[256]{0:T(256)(128)(2,1)S(1)}, bf16[256]{0:T(256)(128)(2,1)S(1)}, u32[]{:S(2)}, u32[]{:S(2)}) collective-permute-start(bf16[256]{0:T(256)(128)(2,1)S(1)} %get-tuple-element.147), channel_id=1, source_target_pairs={{0,0},{1,1},{2,2},{3,3},{4,8},{5,9},{6,10},{7,11},{8,4},{9,5},{10,... | collective-permute-start | bytes 1544 | tf_op jit(solution)/shard_map/ppermute | solution.py:689
  9.9 2.6 collective-permute-start.1
  12.5 1.9 collective-permute-start
  15.5 1.9 collective-permute-start.3
  17.4 2.8 collective-permute-start.2
  20.3 1.3 collective-permute-start.18
  27.0 3.1 collective-permute-done.2.refs_2_.refs_0_
  32.7 2.9 collective-permute-done.10.refs_2_
  35.6 1.3 collective-permute-start.14
  38.1 3.7 collective-permute-start.21
  41.7 2.3 collective-permute-done.4.refs_4_.refs_2_
  45.7 13.3 %self_forward.1 = (f32[256,768]{1,0:T(8,128)}, f32[24,256]{1,0:T(8,128)}, bf16[256,768]{1,0:T(8,128)(2,1)}, bf16[1024,768]{1,0:T(8,128)(2,1)}, bf16[1024,768]{1,0:T(8,128)(2,1)}) custom-call(bf16[128,768]{1,0:T(8,128)(2,1)} %copy-done.21, bf16[128,768]{1,0:T(8,128)(2,1)} %copy-done.20, bf16[128,768]{1,0:T(8,128)(2,1)} %copy-done.29, ...), custom_call_target="tpu_custom_call" | custom-call | flops 6000000000 | bytes 12000000 | tf_op jit(solution)/shard_map/self_forward/pallas_call | solution.py:421
  59.0 5.1 %collective-permute-start.20 = (bf16[128,768]{1,0:T(8,128)(2,1)S(1)}, bf16[128,768]{1,0:T(8,128)(2,1)S(1)}, u32[]{:S(2)}, u32[]{:S(2)}) collective-permute-start(bf16[128,768]{1,0:T(8,128)(2,1)S(1)} %get-tuple-element.174), channel_id=1, source_target_pairs={{0,0},{1,1},{2,2},{3,3},{4,8},{5,9},{6,10},{7,11},{8,4},{9,5},{10,... | collective-permute-start | bytes 589832 | tf_op jit(solution)/shard_map/ppermute | solution.py:689
  64.9 14.9 %cross_forward.1 = (f32[256,768]{1,0:T(8,128)}, f32[256,128]{1,0:T(8,128)}, f32[256,768]{1,0:T(8,128)}, f32[24,256]{1,0:T(8,128)}, bf16[256,768]{1,0:T(8,128)(2,...) custom-call(bf16[128,768]{1,0:T(8,128)(2,1)} %copy-done.21, bf16[128,768]{1,0:T(8,128)(2,1)} %copy-done.20, ...), custom_call_target="tpu_custom_call" | custom-call | flops 7000000000 | bytes 14000000 | tf_op jit(solution)/shard_map/cross_forward/pallas_call | solution.py:421
  80.6 18.0 %forward_back.1 = (bf16[256,768]{1,0:T(8,128)(2,1)}, bf16[2,3072,384]{2,1,0:T(8,128)(2,1)}, bf16[2,768,1536]{2,1,0:T(8,128)(2,1)}, bf16[2,768,384]{2,1,0:T(8,128...) custom-call(f32[256,768]{1,0:T(8,128)} %get-tuple-element.52.hidden., ...), custom_call_target="tpu_custom_call" | custom-call | flops 8000000000 | bytes 25000000 | tf_op jit(solution)/shard_map/forward_back/pallas_call | solution.py:421
  100.1 1.4 reduce.9
  102.2 2.4 collective-permute-start.22
  104.7 29.4 %cross_back.1 = (bf16[512,768]{1,0:T(8,128)(2,1)}, bf16[512,768]{1,0:T(8,128)(2,1)}, bf16[2,1536,384]{2,1,0:T(8,128)(2,1)}, bf16[2,768,384]{2,1,0:T(8,128)(2,1)}...) custom-call(bf16[128,768]{1,0:T(8,128)(2,1)} %copy-done.19, ...), custom_call_target="tpu_custom_call" | custom-call | flops 12000000000 | bytes 20000000 | tf_op jit(solution)/shard_map/cross_back/pallas_call | solution.py:421
  134.8 25.9 %self_back.1 = (bf16[512,768]{1,0:T(8,128)(2,1)}, bf16[512,768]{1,0:T(8,128)(2,1)}, bf16[2,2304,384]{2,1,0:T(8,128)(2,1)}, f32[8,768]{1,0:T(8,128)}) custom-call(bf16[128,768]{1,0:T(8,128)(2,1)} %copy-done.21, bf16[128,768]{1,0:T(8,128)(2,1)} %copy-done.20, bf16[128,768]{1,0:T(8,128)(2,1)} %copy-done.29, bf16[128,768]{1,0:T(8,128)(2,1)} %copy-done.28, ...), custom_call_target="tpu_custom_call" | custom-call | flops 11000000512 | bytes 17000000 | tf_op jit(solution)/shard_map/self_back/pallas_call | solution.py:421
  161.5 2.9 dynamic-slice_bitcast_fusion.2
  164.8 3.4 dynamic-slice_bitcast_fusion
  168.2 1.3 dynamic-slice_bitcast_fusion.7
  169.5 1.3 collective-permute-start.62
  176.0 1.3 collective-permute-start.57
  177.3 1.7 pad_maximum_fusion
  179.1 2.4 collective-permute-start.65
  181.5 1.3 collective-permute-start.58
  182.8 1.7 dynamic-slice_bitcast_fusion.1
  184.4 5.2 %collective-permute-start.23 = (bf16[128,768]{1,0:T(8,128)(2,1)S(1)}, bf16[128,768]{1,0:T(8,128)(2,1)S(1)}, u32[]{:S(2)}, u32[]{:S(2)}) collective-permute-start(bf16[128,768]{1,0:T(8,128)(2,1)S(1)} %get-tuple-element.172), channel_id=1, source_target_pairs={{0,2},{1,3},{2,0},{3,1},{4,10},{5,11},{6,8},{7,9},{8,6},{9,7},{10,... | collective-permute-start | bytes 589832 | tf_op jit(solution)/shard_map/ppermute | solution.py:689
  190.3 3.6 collective-permute-done.23
  193.9 1.5 collective-permute-start.59
  195.4 2.0 collective-permute-done.59
  198.3 3.6 collective-permute-done.60
  201.9 5.2 %collective-permute-start.44 = (bf16[2,2,2,2,192,384]{5,4,3,2,1,0:T(8,128)(2,1)}, bf16[2,2,2,2,192,384]{5,4,3,2,1,0:T(8,128)(2,1)}, u32[]{:S(2)}, u32[]{:S(2)}) collective-permute-start(bf16[2,2,2,2,192,384]{5,4,3,2,1,0:T(8,128)(2,1)} %dynamic-slice_bitcast_fusion.1), channel_id=1, source_target_pairs={{0,8},{1,9},{2,10},{3,11},{4,12},{5,13},{6,14},{7,15},{8,0},{9,1},... | collective-permute-start | bytes 7077896 | tf_op jit(solution)/shard_map/ppermute | solution.py:689
  212.3 6.5 %collective-permute-done.25.refs_4_ = bf16[256,768]{1,0:T(8,128)(2,1)S(1)} collective-permute-done((bf16[256,768]{1,0:T(8,128)(2,1)S(1)}, bf16[256,768]{1,0:T(8,128)(2,1)S(1)}, u32[]{:S(2)}, u32[]{:S(2)}) %collective-permute-start.25) | collective-permute-done | bytes 393248 | tf_op jit(solution)/shard_map/ppermute | solution.py:689
  219.5 3.0 final_norm.2
  222.5 1.8 slice_bitcast_fusion.3
  224.3 3.1 collective-permute-start.26
  227.5 2.4 collective-permute-start.27
  229.9 2.6 final_norm.3
  232.5 1.9 bitcast_add_fusion.2
  235.5 3.5 collective-permute-start.30
  239.0 1.7 collective-permute-start.31
  241.4 6.2 %collective-permute-done.30 = bf16[128,768]{1,0:T(8,128)(2,1)S(1)} collective-permute-done((bf16[128,768]{1,0:T(8,128)(2,1)S(1)}, bf16[128,768]{1,0:T(8,128)(2,1)S(1)}, u32[]{:S(2)}, u32[]{:S(2)}) %collective-permute-start.30) | collective-permute-done | bytes 196640 | tf_op jit(solution)/shard_map/ppermute | solution.py:689
  250.3 5.0 %collective-permute-done.33 = bf16[2,2,2,144,384]{4,3,2,1,0:T(8,128)(2,1)S(1)} collective-permute-done((bf16[2,2,2,144,384]{4,3,2,1,0:T(8,128)(2,1)S(1)}, bf16[2,2,2,144,384]{4,3,2,1,0:T(8,128)(2,1)S(1)}, u32[]{:S(2)}, u32[]{:S(2)}) %collective-permute-start.33) | collective-permute-done | bytes 884768 | tf_op jit(solution)/shard_map/ppermute | solution.py:689
  256.1 2.3 bitcast_add_fusion
  259.2 8.0 %collective-permute-done.34 = bf16[2,2,144,384]{3,2,1,0:T(8,128)(2,1)S(1)} collective-permute-done((bf16[2,2,144,384]{3,2,1,0:T(8,128)(2,1)S(1)}, bf16[2,2,144,384]{3,2,1,0:T(8,128)(2,1)S(1)}, u32[]{:S(2)}, u32[]{:S(2)}) %collective-permute-start.34) | collective-permute-done | bytes 442400 | tf_op jit(solution)/shard_map/ppermute | solution.py:689
  267.5 1.9 bitcast_add_fusion.1
  271.6 1.9 collective-permute-done.35
  274.5 6.6 %collective-permute-done.36 = bf16[144,384]{1,0:T(8,128)(2,1)S(1)} collective-permute-done((bf16[144,384]{1,0:T(8,128)(2,1)S(1)}, bf16[144,384]{1,0:T(8,128)(2,1)S(1)}, u32[]{:S(2)}, u32[]{:S(2)}) %collective-permute-start.36) | collective-permute-done | bytes 110624 | tf_op jit(solution)/shard_map/ppermute | solution.py:689
  281.2 1.4 collective-permute-start.37
  282.6 1.3 dynamic-slice_bitcast_fusion.3
  284.5 1.9 collective-permute-done.51
  289.4 8.2 %collective-permute-done.45 = bf16[2,2,2,192,384]{4,3,2,1,0:T(8,128)(2,1)} collective-permute-done((bf16[2,2,2,192,384]{4,3,2,1,0:T(8,128)(2,1)}, bf16[2,2,2,192,384]{4,3,2,1,0:T(8,128)(2,1)}, u32[]{:S(2)}, u32[]{:S(2)}) %collective-permute-start.45) | collective-permute-done | bytes 1179680 | tf_op jit(solution)/shard_map/ppermute | solution.py:689
  297.6 1.8 bitcast_add_fusion.5
  300.6 2.5 collective-permute-done.52
  304.4 16.9 %collective-permute-done.46 = bf16[2,2,192,384]{3,2,1,0:T(8,128)(2,1)S(1)} collective-permute-done((bf16[2,2,192,384]{3,2,1,0:T(8,128)(2,1)S(1)}, bf16[2,2,192,384]{3,2,1,0:T(8,128)(2,1)S(1)}, u32[]{:S(2)}, u32[]{:S(2)}) %collective-permute-start.46) | collective-permute-done | bytes 589856 | tf_op jit(solution)/shard_map/ppermute | solution.py:689
  321.7 14.7 %collective-permute-done.47 = bf16[2,192,384]{2,1,0:T(8,128)(2,1)S(1)} collective-permute-done((bf16[2,192,384]{2,1,0:T(8,128)(2,1)S(1)}, bf16[2,192,384]{2,1,0:T(8,128)(2,1)S(1)}, u32[]{:S(2)}, u32[]{:S(2)}) %collective-permute-start.47) | collective-permute-done | bytes 294944 | tf_op jit(solution)/shard_map/ppermute | solution.py:689
  336.6 1.5 bitcast_add_fusion.3
  338.2 1.5 collective-permute-start.40
  341.7 2.3 collective-permute-start.49
  344.1 13.2 %collective-permute-done.40 = bf16[2,2,240,384]{3,2,1,0:T(8,128)(2,1)S(1)} collective-permute-done((bf16[2,2,240,384]{3,2,1,0:T(8,128)(2,1)S(1)}, bf16[2,2,240,384]{3,2,1,0:T(8,128)(2,1)S(1)}, u32[]{:S(2)}, u32[]{:S(2)}) %collective-permute-start.40) | collective-permute-done | bytes 737312 | tf_op jit(solution)/shard_map/ppermute | solution.py:689
  357.7 8.6 %collective-permute-done.41 = bf16[2,240,384]{2,1,0:T(8,128)(2,1)S(1)} collective-permute-done((bf16[2,240,384]{2,1,0:T(8,128)(2,1)S(1)}, bf16[2,240,384]{2,1,0:T(8,128)(2,1)S(1)}, u32[]{:S(2)}, u32[]{:S(2)}) %collective-permute-start.41) | collective-permute-done | bytes 368672 | tf_op jit(solution)/shard_map/ppermute | solution.py:689
  366.5 10.9 %collective-permute-done.42 = bf16[240,384]{1,0:T(8,128)(2,1)S(1)} collective-permute-done((bf16[240,384]{1,0:T(8,128)(2,1)S(1)}, bf16[240,384]{1,0:T(8,128)(2,1)S(1)}, u32[]{:S(2)}, u32[]{:S(2)}) %collective-permute-start.42) | collective-permute-done | bytes 184352 | tf_op jit(solution)/shard_map/ppermute | solution.py:689
  (295 shorter events, 58.5 us)
Async XLA Ops:
  2.2 15.2 %collective-permute-start.16 = (bf16[256]{0:T(256)(128)(2,1)S(1)}, bf16[256]{0:T(256)(128)(2,1)S(1)}, u32[]{:S(2)}, u32[]{:S(2)}) collective-permute-start(bf16[256]{0:T(256)(128)(2,1)S(1)} %get-tuple-element.147), channel_id=1, source_target_pairs={{0,0},{1,1},{2,2},{3,3},{4,8},{5,9},{6,10},{7,11},{8,4},{9,5},{10,... | collective-permute-start | bytes 1544 | tf_op jit(solution)/shard_map/ppermute | solution.py:689
  7.8 12.4 %collective-permute-start.17 = (bf16[256]{0:T(256)(128)(2,1)S(1)}, bf16[256]{0:T(256)(128)(2,1)S(1)}, u32[]{:S(2)}, u32[]{:S(2)}) collective-permute-start(bf16[256]{0:T(256)(128)(2,1)S(1)} %get-tuple-element.148), channel_id=1, source_target_pairs={{0,2},{1,3},{2,0},{3,1},{4,10},{5,11},{6,8},{7,9},{8,6},{9,7},{10,... | collective-permute-start | bytes 1544 | tf_op jit(solution)/shard_map/ppermute | solution.py:689
  9.9 14.5 %collective-permute-start.1 = (bf16[128,768]{1,0:T(8,128)(2,1)S(1)}, bf16[128,768]{1,0:T(8,128)(2,1)S(1)}, u32[]{:S(2)}, u32[]{:S(2)}) collective-permute-start(bf16[128,768]{1,0:T(8,128)(2,1)S(1)} %get-tuple-element.177), channel_id=1, source_target_pairs={{0,2},{1,3},{2,0},{3,1},{4,10},{5,11},{6,8},{7,9},{8,6},{9,7},{10,... | collective-permute-start | bytes 589832 | tf_op jit(solution)/shard_map/ppermute | solution.py:689
  12.5 13.7 %collective-permute-start = (bf16[128,768]{1,0:T(8,128)(2,1)S(1)}, bf16[128,768]{1,0:T(8,128)(2,1)S(1)}, u32[]{:S(2)}, u32[]{:S(2)}) collective-permute-start(bf16[128,768]{1,0:T(8,128)(2,1)S(1)} %get-tuple-element.178), channel_id=1, source_target_pairs={{0,0},{1,1},{2,2},{3,3},{4,8},{5,9},{6,10},{7,11},{8,4},{9,5},{10,... | collective-permute-start | bytes 589832 | tf_op jit(solution)/shard_map/ppermute | solution.py:689
  15.5 10.9 %collective-permute-start.3 = (bf16[128,768]{1,0:T(8,128)(2,1)S(1)}, bf16[128,768]{1,0:T(8,128)(2,1)S(1)}, u32[]{:S(2)}, u32[]{:S(2)}) collective-permute-start(bf16[128,768]{1,0:T(8,128)(2,1)S(1)} %get-tuple-element.175), channel_id=1, source_target_pairs={{0,2},{1,3},{2,0},{3,1},{4,10},{5,11},{6,8},{7,9},{8,6},{9,7},{10,... | collective-permute-start | bytes 589832 | tf_op jit(solution)/shard_map/ppermute | solution.py:689
  17.4 12.7 %collective-permute-start.2 = (bf16[128,768]{1,0:T(8,128)(2,1)S(1)}, bf16[128,768]{1,0:T(8,128)(2,1)S(1)}, u32[]{:S(2)}, u32[]{:S(2)}) collective-permute-start(bf16[128,768]{1,0:T(8,128)(2,1)S(1)} %get-tuple-element.176), channel_id=1, source_target_pairs={{0,0},{1,1},{2,2},{3,3},{4,8},{5,9},{6,10},{7,11},{8,4},{9,5},{10,... | collective-permute-start | bytes 589832 | tf_op jit(solution)/shard_map/ppermute | solution.py:689
  24.4 6.9 %collective-permute-start.13 = (bf16[128,768]{1,0:T(8,128)(2,1)S(1)}, bf16[128,768]{1,0:T(8,128)(2,1)S(1)}, u32[]{:S(2)}, u32[]{:S(2)}) collective-permute-start(bf16[128,768]{1,0:T(8,128)(2,1)S(1)} %collective-permute-done.1.refs_1_), channel_id=1, source_target_pairs={{0,8},{1,9},{2,10},{3,11},{4,12},{5,13},{6,14},{7,15},{8,0},{9,1},... | collective-permute-start | bytes 589832 | tf_op jit(solution)/shard_map/ppermute | solution.py:689
  24.9 6.7 %collective-permute-start.11 = (bf16[128,768]{1,0:T(8,128)(2,1)S(1)}, bf16[128,768]{1,0:T(8,128)(2,1)S(1)}, u32[]{:S(2)}, u32[]{:S(2)}) collective-permute-start(bf16[128,768]{1,0:T(8,128)(2,1)S(1)} %collective-permute-done.1.refs_1_), channel_id=1, source_target_pairs={{0,1},{1,0},{2,3},{3,2},{4,5},{5,4},{6,7},{7,6},{8,9},{9,8},{10,11... | collective-permute-start | bytes 589832 | tf_op jit(solution)/shard_map/ppermute | solution.py:689
  26.2 9.5 %collective-permute-start.10 = (bf16[128,768]{1,0:T(8,128)(2,1)S(1)}, bf16[128,768]{1,0:T(8,128)(2,1)S(1)}, u32[]{:S(2)}, u32[]{:S(2)}) collective-permute-start(bf16[128,768]{1,0:T(8,128)(2,1)S(1)} %collective-permute-done.refs_0_), channel_id=1, source_target_pairs={{0,1},{1,0},{2,3},{3,2},{4,5},{5,4},{6,7},{7,6},{8,9},{9,8},{10,11... | collective-permute-start | bytes 589832 | tf_op jit(solution)/shard_map/ppermute | solution.py:689
  26.4 11.6 %collective-permute-start.12 = (bf16[128,768]{1,0:T(8,128)(2,1)S(1)}, bf16[128,768]{1,0:T(8,128)(2,1)S(1)}, u32[]{:S(2)}, u32[]{:S(2)}) collective-permute-start(bf16[128,768]{1,0:T(8,128)(2,1)S(1)} %collective-permute-done.refs_0_), channel_id=1, source_target_pairs={{0,8},{1,9},{2,10},{3,11},{4,12},{5,13},{6,14},{7,15},{8,0},{9,1},... | collective-permute-start | bytes 589832 | tf_op jit(solution)/shard_map/ppermute | solution.py:689
  30.1 11.6 %collective-permute-start.5 = (bf16[128,768]{1,0:T(8,128)(2,1)S(1)}, bf16[128,768]{1,0:T(8,128)(2,1)S(1)}, u32[]{:S(2)}, u32[]{:S(2)}) collective-permute-start(bf16[128,768]{1,0:T(8,128)(2,1)S(1)} %collective-permute-done.3.refs_3_.refs_1_), channel_id=1, source_target_pairs={{0,1},{1,0},{2,3},{3,2},{4,5},{5,4},{6,7},{7,6},{8,9},{9,8},{10,11... | collective-permute-start | bytes 589832 | tf_op jit(solution)/shard_map/ppermute | solution.py:689
  31.3 12.7 %collective-permute-start.4 = (bf16[128,768]{1,0:T(8,128)(2,1)S(1)}, bf16[128,768]{1,0:T(8,128)(2,1)S(1)}, u32[]{:S(2)}, u32[]{:S(2)}) collective-permute-start(bf16[128,768]{1,0:T(8,128)(2,1)S(1)} %collective-permute-done.2.refs_2_.refs_0_), channel_id=1, source_target_pairs={{0,1},{1,0},{2,3},{3,2},{4,5},{5,4},{6,7},{7,6},{8,9},{9,8},{10,11... | collective-permute-start | bytes 589832 | tf_op jit(solution)/shard_map/ppermute | solution.py:689
  31.6 13.3 %collective-permute-start.15 = (bf16[128,768]{1,0:T(8,128)(2,1)S(1)}, bf16[128,768]{1,0:T(8,128)(2,1)S(1)}, u32[]{:S(2)}, u32[]{:S(2)}) collective-permute-start(bf16[128,768]{1,0:T(8,128)(2,1)S(1)} %collective-permute-done.11.refs_3_), channel_id=1, source_target_pairs={{0,8},{1,9},{2,10},{3,11},{4,12},{5,13},{6,14},{7,15},{8,0},{9,1},... | collective-permute-start | bytes 589832 | tf_op jit(solution)/shard_map/ppermute | solution.py:689
  35.6 9.4 %collective-permute-start.14 = (bf16[128,768]{1,0:T(8,128)(2,1)S(1)}, bf16[128,768]{1,0:T(8,128)(2,1)S(1)}, u32[]{:S(2)}, u32[]{:S(2)}) collective-permute-start(bf16[128,768]{1,0:T(8,128)(2,1)S(1)} %collective-permute-done.10.refs_2_), channel_id=1, source_target_pairs={{0,8},{1,9},{2,10},{3,11},{4,12},{5,13},{6,14},{7,15},{8,0},{9,1},... | collective-permute-start | bytes 589832 | tf_op jit(solution)/shard_map/ppermute | solution.py:689
  38.1 41.8 %collective-permute-start.21 = (bf16[128,768]{1,0:T(8,128)(2,1)S(1)}, bf16[128,768]{1,0:T(8,128)(2,1)S(1)}, u32[]{:S(2)}, u32[]{:S(2)}) collective-permute-start(bf16[128,768]{1,0:T(8,128)(2,1)S(1)} %get-tuple-element.173), channel_id=1, source_target_pairs={{0,2},{1,3},{2,0},{3,1},{4,10},{5,11},{6,8},{7,9},{8,6},{9,7},{10,... | collective-permute-start | bytes 589832 | tf_op jit(solution)/shard_map/ppermute | solution.py:689
  41.7 17.3 %collective-permute-start.7 = (bf16[128,768]{1,0:T(8,128)(2,1)S(1)}, bf16[128,768]{1,0:T(8,128)(2,1)S(1)}, u32[]{:S(2)}, u32[]{:S(2)}) collective-permute-start(bf16[128,768]{1,0:T(8,128)(2,1)S(1)} %collective-permute-done.3.refs_3_.refs_1_), channel_id=1, source_target_pairs={{0,8},{1,9},{2,10},{3,11},{4,12},{5,13},{6,14},{7,15},{8,0},{9,1},... | collective-permute-start | bytes 589832 | tf_op jit(solution)/shard_map/ppermute | solution.py:689
  44.0 20.0 %collective-permute-start.6 = (bf16[128,768]{1,0:T(8,128)(2,1)S(1)}, bf16[128,768]{1,0:T(8,128)(2,1)S(1)}, u32[]{:S(2)}, u32[]{:S(2)}) collective-permute-start(bf16[128,768]{1,0:T(8,128)(2,1)S(1)} %collective-permute-done.2.refs_2_.refs_0_), channel_id=1, source_target_pairs={{0,8},{1,9},{2,10},{3,11},{4,12},{5,13},{6,14},{7,15},{8,0},{9,1},... | collective-permute-start | bytes 589832 | tf_op jit(solution)/shard_map/ppermute | solution.py:689
  44.9 19.2 %collective-permute-start.9 = (bf16[128,768]{1,0:T(8,128)(2,1)S(1)}, bf16[128,768]{1,0:T(8,128)(2,1)S(1)}, u32[]{:S(2)}, u32[]{:S(2)}) collective-permute-start(bf16[128,768]{1,0:T(8,128)(2,1)S(1)} %collective-permute-done.5.refs_5_.refs_3_), channel_id=1, source_target_pairs={{0,8},{1,9},{2,10},{3,11},{4,12},{5,13},{6,14},{7,15},{8,0},{9,1},... | collective-permute-start | bytes 589832 | tf_op jit(solution)/shard_map/ppermute | solution.py:689
  45.0 19.1 %collective-permute-start.8 = (bf16[128,768]{1,0:T(8,128)(2,1)S(1)}, bf16[128,768]{1,0:T(8,128)(2,1)S(1)}, u32[]{:S(2)}, u32[]{:S(2)}) collective-permute-start(bf16[128,768]{1,0:T(8,128)(2,1)S(1)} %collective-permute-done.4.refs_4_.refs_2_), channel_id=1, source_target_pairs={{0,8},{1,9},{2,10},{3,11},{4,12},{5,13},{6,14},{7,15},{8,0},{9,1},... | collective-permute-start | bytes 589832 | tf_op jit(solution)/shard_map/ppermute | solution.py:689
  59.0 20.8 %collective-permute-start.20 = (bf16[128,768]{1,0:T(8,128)(2,1)S(1)}, bf16[128,768]{1,0:T(8,128)(2,1)S(1)}, u32[]{:S(2)}, u32[]{:S(2)}) collective-permute-start(bf16[128,768]{1,0:T(8,128)(2,1)S(1)} %get-tuple-element.174), channel_id=1, source_target_pairs={{0,0},{1,1},{2,2},{3,3},{4,8},{5,9},{6,10},{7,11},{8,4},{9,5},{10,... | collective-permute-start | bytes 589832 | tf_op jit(solution)/shard_map/ppermute | solution.py:689
  102.2 87.5 %collective-permute-start.22 = (bf16[128,768]{1,0:T(8,128)(2,1)S(1)}, bf16[128,768]{1,0:T(8,128)(2,1)S(1)}, u32[]{:S(2)}, u32[]{:S(2)}) collective-permute-start(bf16[128,768]{1,0:T(8,128)(2,1)S(1)} %get-tuple-element.171), channel_id=1, source_target_pairs={{0,0},{1,1},{2,2},{3,3},{4,8},{5,9},{6,10},{7,11},{8,4},{9,5},{10,... | collective-permute-start | bytes 589832 | tf_op jit(solution)/shard_map/ppermute | solution.py:689
  160.7 8.8 %collective-permute-start.61 = (f32[8,768]{1,0:T(8,128)}, f32[8,768]{1,0:T(8,128)S(1)}, u32[]{:S(2)}, u32[]{:S(2)}) collective-permute-start(f32[8,768]{1,0:T(8,128)} %get-tuple-element.86), channel_id=1, source_target_pairs={{0,8},{1,9},{2,10},{3,11},{4,12},{5,13},{6,14},{7,15},{8,0},{9,1},... | collective-permute-start | bytes 73736 | tf_op jit(solution)/shard_map/ppermute | solution.py:689
  160.8 15.2 %collective-permute-start.56 = (f32[28,768]{1,0:T(8,128)S(1)}, f32[28,768]{1,0:T(8,128)S(1)}, u32[]{:S(2)}, u32[]{:S(2)}) collective-permute-start(f32[28,768]{1,0:T(8,128)S(1)} %pad_maximum_fusion.8), channel_id=1, source_target_pairs={{0,8},{1,9},{2,10},{3,11},{4,12},{5,13},{6,14},{7,15},{8,0},{9,1},... | collective-permute-start | bytes 258056 | tf_op jit(solution)/shard_map/ppermute | solution.py:689
  161.4 45.8 %collective-permute-start.24 = (bf16[512,768]{1,0:T(8,128)(2,1)}, bf16[512,768]{1,0:T(8,128)(2,1)S(1)}, u32[]{:S(2)}, u32[]{:S(2)}) collective-permute-start(bf16[512,768]{1,0:T(8,128)(2,1)} %get-tuple-element.71), channel_id=1, source_target_pairs={{0,8},{1,9},{2,10},{3,11},{4,12},{5,13},{6,14},{7,15},{8,0},{9,1},... | collective-permute-start | bytes 2359304 | tf_op jit(solution)/shard_map/ppermute | solution.py:689
  164.4 68.1 %collective-permute-start.32 = (bf16[2,2,2,2,144,384]{5,4,3,2,1,0:T(8,128)(2,1)}, bf16[2,2,2,2,144,384]{5,4,3,2,1,0:T(8,128)(2,1)}, u32[]{:S(2)}, u32[]{:S(2)}) collective-permute-start(bf16[2,2,2,2,144,384]{5,4,3,2,1,0:T(8,128)(2,1)} %dynamic-slice_bitcast_fusion.2), channel_id=1, source_target_pairs={{0,8},{1,9},{2,10},{3,11},{4,12},{5,13},{6,14},{7,15},{8,0},{9,1},... | collective-permute-start | bytes 5308424 | tf_op jit(solution)/shard_map/ppermute | solution.py:689
  169.5 2.8 collective-permute-start.62
  172.3 2.7 collective-permute-start.63
  174.9 4.1 %collective-permute-start.64 = (f32[8,768]{1,0:T(8,128)S(1)}, f32[8,768]{1,0:T(8,128)S(1)}, u32[]{:S(2)}, u32[]{:S(2)}) collective-permute-start(f32[8,768]{1,0:T(8,128)S(1)} %add.266), channel_id=1, source_target_pairs={{0,2},{1,3},{2,0},{3,1},{4,6},{5,7},{6,4},{7,5},{8,10},{9,11},{10,... | collective-permute-start | bytes 73736 | tf_op jit(solution)/shard_map/ppermute | solution.py:689
  176.0 5.4 %collective-permute-start.57 = (f32[28,768]{1,0:T(8,128)S(1)}, f32[28,768]{1,0:T(8,128)S(1)}, u32[]{:S(2)}, u32[]{:S(2)}) collective-permute-start(f32[28,768]{1,0:T(8,128)S(1)} %fusion.19), channel_id=1, source_target_pairs={{0,16},{1,17},{2,18},{3,19},{4,20},{5,21},{6,22},{7,23},{8,24},{9,... | collective-permute-start | bytes 258056 | tf_op jit(solution)/shard_map/ppermute | solution.py:689
  179.1 5.4 %collective-permute-start.65 = (f32[8,768]{1,0:T(8,128)S(1)}, f32[8,768]{1,0:T(8,128)S(1)}, u32[]{:S(2)}, u32[]{:S(2)}) collective-permute-start(f32[8,768]{1,0:T(8,128)S(1)} %add.267), channel_id=1, source_target_pairs={{0,4},{1,5},{2,6},{3,7},{4,0},{5,1},{6,2},{7,3},{8,12},{9,13},{10,... | collective-permute-start | bytes 73736 | tf_op jit(solution)/shard_map/ppermute | solution.py:689
  181.5 8.1 %collective-permute-start.58 = (f32[28,768]{1,0:T(8,128)S(1)}, f32[28,768]{1,0:T(8,128)S(1)}, u32[]{:S(2)}, u32[]{:S(2)}) collective-permute-start(f32[28,768]{1,0:T(8,128)S(1)} %add.260), channel_id=1, source_target_pairs={{0,1},{1,0},{2,3},{3,2},{4,5},{5,4},{6,7},{7,6},{8,9},{9,8},{10,11... | collective-permute-start | bytes 258056 | tf_op jit(solution)/shard_map/ppermute | solution.py:689
  184.4 9.5 %collective-permute-start.23 = (bf16[128,768]{1,0:T(8,128)(2,1)S(1)}, bf16[128,768]{1,0:T(8,128)(2,1)S(1)}, u32[]{:S(2)}, u32[]{:S(2)}) collective-permute-start(bf16[128,768]{1,0:T(8,128)(2,1)S(1)} %get-tuple-element.172), channel_id=1, source_target_pairs={{0,2},{1,3},{2,0},{3,1},{4,10},{5,11},{6,8},{7,9},{8,6},{9,7},{10,... | collective-permute-start | bytes 589832 | tf_op jit(solution)/shard_map/ppermute | solution.py:689
  189.6 19.1 %collective-permute-start.28 = (bf16[512,768]{1,0:T(8,128)(2,1)S(1)}, bf16[512,768]{1,0:T(8,128)(2,1)S(1)}, u32[]{:S(2)}, u32[]{:S(2)}) collective-permute-start(bf16[512,768]{1,0:T(8,128)(2,1)S(1)} %copy-done.26), channel_id=1, source_target_pairs={{0,8},{1,9},{2,10},{3,11},{4,12},{5,13},{6,14},{7,15},{8,0},{9,1},... | collective-permute-start | bytes 2359304 | tf_op jit(solution)/shard_map/ppermute | solution.py:689
  189.8 66.3 %collective-permute-start.50 = (bf16[2,2,2,2,48,1536]{5,4,3,2,1,0:T(8,128)(2,1)}, bf16[2,2,2,2,48,1536]{5,4,3,2,1,0:T(8,128)(2,1)}, u32[]{:S(2)}, u32[]{:S(2)}) collective-permute-start(bf16[2,2,2,2,48,1536]{5,4,3,2,1,0:T(8,128)(2,1)} %dynamic-slice_bitcast_fusion), channel_id=1, source_target_pairs={{0,8},{1,9},{2,10},{3,11},{4,12},{5,13},{6,14},{7,15},{8,0},{9,1},... | collective-permute-start | bytes 7077896 | tf_op jit(solution)/shard_map/ppermute | solution.py:689
  193.9 3.5 collective-permute-start.59
  197.4 4.4 %collective-permute-start.60 = (f32[28,768]{1,0:T(8,128)S(1)}, f32[28,768]{1,0:T(8,128)S(1)}, u32[]{:S(2)}, u32[]{:S(2)}) collective-permute-start(f32[28,768]{1,0:T(8,128)S(1)} %add.262), channel_id=1, source_target_pairs={{0,4},{1,5},{2,6},{3,7},{4,0},{5,1},{6,2},{7,3},{8,12},{9,13},{10,... | collective-permute-start | bytes 258056 | tf_op jit(solution)/shard_map/ppermute | solution.py:689
  201.9 65.6 %collective-permute-start.44 = (bf16[2,2,2,2,192,384]{5,4,3,2,1,0:T(8,128)(2,1)}, bf16[2,2,2,2,192,384]{5,4,3,2,1,0:T(8,128)(2,1)}, u32[]{:S(2)}, u32[]{:S(2)}) collective-permute-start(bf16[2,2,2,2,192,384]{5,4,3,2,1,0:T(8,128)(2,1)} %dynamic-slice_bitcast_fusion.1), channel_id=1, source_target_pairs={{0,8},{1,9},{2,10},{3,11},{4,12},{5,13},{6,14},{7,15},{8,0},{9,1},... | collective-permute-start | bytes 7077896 | tf_op jit(solution)/shard_map/ppermute | solution.py:689
  208.0 10.7 %collective-permute-start.25 = (bf16[256,768]{1,0:T(8,128)(2,1)S(1)}, bf16[256,768]{1,0:T(8,128)(2,1)S(1)}, u32[]{:S(2)}, u32[]{:S(2)}) collective-permute-start(bf16[256,768]{1,0:T(8,128)(2,1)S(1)} %get-tuple-element.153), channel_id=1, source_target_pairs={{0,1},{1,0},{2,3},{3,2},{4,5},{5,4},{6,7},{7,6},{8,9},{9,8},{10,11... | collective-permute-start | bytes 1179656 | tf_op jit(solution)/shard_map/ppermute | solution.py:689
  209.7 17.8 %collective-permute-start.29 = (bf16[256,768]{1,0:T(8,128)(2,1)}, bf16[256,768]{1,0:T(8,128)(2,1)}, u32[]{:S(2)}, u32[]{:S(2)}) collective-permute-start(bf16[256,768]{1,0:T(8,128)(2,1)} %get-tuple-element.151), channel_id=1, source_target_pairs={{0,1},{1,0},{2,3},{3,2},{4,5},{5,4},{6,7},{7,6},{8,9},{9,8},{10,11... | collective-permute-start | bytes 1179656 | tf_op jit(solution)/shard_map/ppermute | solution.py:689
  224.3 11.2 %collective-permute-start.26 = (bf16[128,768]{1,0:T(8,128)(2,1)}, bf16[128,768]{1,0:T(8,128)(2,1)}, u32[]{:S(2)}, u32[]{:S(2)}) collective-permute-start(bf16[128,768]{1,0:T(8,128)(2,1)} %get-tuple-element.167), channel_id=1, source_target_pairs={{0,0},{1,1},{2,2},{3,3},{4,8},{5,9},{6,10},{7,11},{8,4},{9,5},{10,... | collective-permute-start | bytes 589832 | tf_op jit(solution)/shard_map/ppermute | solution.py:689
  227.5 11.5 %collective-permute-start.27 = (bf16[128,768]{1,0:T(8,128)(2,1)}, bf16[128,768]{1,0:T(8,128)(2,1)}, u32[]{:S(2)}, u32[]{:S(2)}) collective-permute-start(bf16[128,768]{1,0:T(8,128)(2,1)} %get-tuple-element.168), channel_id=1, source_target_pairs={{0,2},{1,3},{2,0},{3,1},{4,10},{5,11},{6,8},{7,9},{8,6},{9,7},{10,... | collective-permute-start | bytes 589832 | tf_op jit(solution)/shard_map/ppermute | solution.py:689
  234.5 20.8 %collective-permute-start.33 = (bf16[2,2,2,144,384]{4,3,2,1,0:T(8,128)(2,1)S(1)}, bf16[2,2,2,144,384]{4,3,2,1,0:T(8,128)(2,1)S(1)}, u32[]{:S(2)}, u32[]{:S(2)}) collective-permute-start(bf16[2,2,2,144,384]{4,3,2,1,0:T(8,128)(2,1)S(1)} %dynamic-slice_bitcast_fusion.8), channel_id=1, source_target_pairs={{0,1},{1,0},{2,3},{3,2},{4,5},{5,4},{6,7},{7,6},{8,9},{9,8},{10,11... | collective-permute-start | bytes 2654216 | tf_op jit(solution)/shard_map/ppermute | solution.py:689
  235.5 12.1 %collective-permute-start.30 = (bf16[128,768]{1,0:T(8,128)(2,1)S(1)}, bf16[128,768]{1,0:T(8,128)(2,1)S(1)}, u32[]{:S(2)}, u32[]{:S(2)}) collective-permute-start(bf16[128,768]{1,0:T(8,128)(2,1)S(1)} %get-tuple-element.163), channel_id=1, source_target_pairs={{0,0},{1,1},{2,2},{3,3},{4,8},{5,9},{6,10},{7,11},{8,4},{9,5},{10,... | collective-permute-start | bytes 589832 | tf_op jit(solution)/shard_map/ppermute | solution.py:689
  239.0 8.6 %collective-permute-start.31 = (bf16[128,768]{1,0:T(8,128)(2,1)S(1)}, bf16[128,768]{1,0:T(8,128)(2,1)S(1)}, u32[]{:S(2)}, u32[]{:S(2)}) collective-permute-start(bf16[128,768]{1,0:T(8,128)(2,1)S(1)} %get-tuple-element.164), channel_id=1, source_target_pairs={{0,2},{1,3},{2,0},{3,1},{4,10},{5,11},{6,8},{7,9},{8,6},{9,7},{10,... | collective-permute-start | bytes 589832 | tf_op jit(solution)/shard_map/ppermute | solution.py:689
  247.6 26.0 %collective-permute-start.38 = (bf16[2,2,2,2,240,384]{5,4,3,2,1,0:T(8,128)(2,1)S(1)}, bf16[2,2,2,2,240,384]{5,4,3,2,1,0:T(8,128)(2,1)S(1)}, u32[]{:S(2)}, u32[]{:S(2)}) collective-permute-start(bf16[2,2,2,2,240,384]{5,4,3,2,1,0:T(8,128)(2,1)S(1)} %copy-done.5), channel_id=1, source_target_pairs={{0,8},{1,9},{2,10},{3,11},{4,12},{5,13},{6,14},{7,15},{8,0},{9,1},... | collective-permute-start | bytes 8847368 | tf_op jit(solution)/shard_map/ppermute | solution.py:689
  255.4 11.8 %collective-permute-start.34 = (bf16[2,2,144,384]{3,2,1,0:T(8,128)(2,1)S(1)}, bf16[2,2,144,384]{3,2,1,0:T(8,128)(2,1)S(1)}, u32[]{:S(2)}, u32[]{:S(2)}) collective-permute-start(bf16[2,2,144,384]{3,2,1,0:T(8,128)(2,1)S(1)} %dynamic-slice_bitcast_fusion.18), channel_id=1, source_target_pairs={{0,16},{1,17},{2,18},{3,19},{4,20},{5,21},{6,22},{7,23},{8,24},{9,... | collective-permute-start | bytes 1327112 | tf_op jit(solution)/shard_map/ppermute | solution.py:689
  258.5 27.9 %collective-permute-start.51 = (bf16[2,2,2,48,1536]{4,3,2,1,0:T(8,128)(2,1)S(1)}, bf16[2,2,2,48,1536]{4,3,2,1,0:T(8,128)(2,1)S(1)}, u32[]{:S(2)}, u32[]{:S(2)}) collective-permute-start(bf16[2,2,2,48,1536]{4,3,2,1,0:T(8,128)(2,1)S(1)} %dynamic-slice_bitcast_fusion.4), channel_id=1, source_target_pairs={{0,1},{1,0},{2,3},{3,2},{4,5},{5,4},{6,7},{7,6},{8,9},{9,8},{10,11... | collective-permute-start | bytes 3538952 | tf_op jit(solution)/shard_map/ppermute | solution.py:689
  267.3 6.2 %collective-permute-start.35 = (bf16[2,144,384]{2,1,0:T(8,128)(2,1)S(1)}, bf16[2,144,384]{2,1,0:T(8,128)(2,1)S(1)}, u32[]{:S(2)}, u32[]{:S(2)}) collective-permute-start(bf16[2,144,384]{2,1,0:T(8,128)(2,1)S(1)} %dynamic-slice_bitcast_fusion.22), channel_id=1, source_target_pairs={{0,2},{1,3},{2,0},{3,1},{4,6},{5,7},{6,4},{7,5},{8,10},{9,11},{10,... | collective-permute-start | bytes 663560 | tf_op jit(solution)/shard_map/ppermute | solution.py:689
  270.7 27.0 %collective-permute-start.45 = (bf16[2,2,2,192,384]{4,3,2,1,0:T(8,128)(2,1)}, bf16[2,2,2,192,384]{4,3,2,1,0:T(8,128)(2,1)}, u32[]{:S(2)}, u32[]{:S(2)}) collective-permute-start(bf16[2,2,2,192,384]{4,3,2,1,0:T(8,128)(2,1)} %dynamic-slice_bitcast_fusion.5), channel_id=1, source_target_pairs={{0,16},{1,17},{2,18},{3,19},{4,20},{5,21},{6,22},{7,23},{8,24},{9,... | collective-permute-start | bytes 3538952 | tf_op jit(solution)/shard_map/ppermute | solution.py:689
  273.6 7.5 %collective-permute-start.36 = (bf16[144,384]{1,0:T(8,128)(2,1)S(1)}, bf16[144,384]{1,0:T(8,128)(2,1)S(1)}, u32[]{:S(2)}, u32[]{:S(2)}) collective-permute-start(bf16[144,384]{1,0:T(8,128)(2,1)S(1)} %dynamic-slice_bitcast_fusion.32), channel_id=1, source_target_pairs={{0,4},{1,5},{2,6},{3,7},{4,0},{5,1},{6,2},{7,3},{8,12},{9,13},{10,... | collective-permute-start | bytes 331784 | tf_op jit(solution)/shard_map/ppermute | solution.py:689
  281.2 3.2 collective-permute-start.37
  283.9 52.6 %collective-permute-start.39 = (bf16[2,2,2,240,384]{4,3,2,1,0:T(8,128)(2,1)}, bf16[2,2,2,240,384]{4,3,2,1,0:T(8,128)(2,1)}, u32[]{:S(2)}, u32[]{:S(2)}) collective-permute-start(bf16[2,2,2,240,384]{4,3,2,1,0:T(8,128)(2,1)} %dynamic-slice_bitcast_fusion.3), channel_id=1, source_target_pairs={{0,16},{1,17},{2,18},{3,19},{4,20},{5,21},{6,22},{7,23},{8,24},{9,... | collective-permute-start | bytes 4423688 | tf_op jit(solution)/shard_map/ppermute | solution.py:689
  288.5 14.7 %collective-permute-start.52 = (bf16[2,2,48,1536]{3,2,1,0:T(8,128)(2,1)}, bf16[2,2,48,1536]{3,2,1,0:T(8,128)(2,1)}, u32[]{:S(2)}, u32[]{:S(2)}) collective-permute-start(bf16[2,2,48,1536]{3,2,1,0:T(8,128)(2,1)} %dynamic-slice_bitcast_fusion.10), channel_id=1, source_target_pairs={{0,2},{1,3},{2,0},{3,1},{4,6},{5,7},{6,4},{7,5},{8,10},{9,11},{10,... | collective-permute-start | bytes 1769480 | tf_op jit(solution)/shard_map/ppermute | solution.py:689
  299.4 21.8 %collective-permute-start.46 = (bf16[2,2,192,384]{3,2,1,0:T(8,128)(2,1)S(1)}, bf16[2,2,192,384]{3,2,1,0:T(8,128)(2,1)S(1)}, u32[]{:S(2)}, u32[]{:S(2)}) collective-permute-start(bf16[2,2,192,384]{3,2,1,0:T(8,128)(2,1)S(1)} %dynamic-slice_bitcast_fusion.11), channel_id=1, source_target_pairs={{0,2},{1,3},{2,0},{3,1},{4,6},{5,7},{6,4},{7,5},{8,10},{9,11},{10,... | collective-permute-start | bytes 1769480 | tf_op jit(solution)/shard_map/ppermute | solution.py:689
  304.3 17.2 %collective-permute-start.53 = (bf16[2,48,1536]{2,1,0:T(8,128)(2,1)S(1)}, bf16[2,48,1536]{2,1,0:T(8,128)(2,1)S(1)}, u32[]{:S(2)}, u32[]{:S(2)}) collective-permute-start(bf16[2,48,1536]{2,1,0:T(8,128)(2,1)S(1)} %dynamic-slice_bitcast_fusion.20), channel_id=1, source_target_pairs={{0,4},{1,5},{2,6},{3,7},{4,0},{5,1},{6,2},{7,3},{8,12},{9,13},{10,... | collective-permute-start | bytes 884744 | tf_op jit(solution)/shard_map/ppermute | solution.py:689
  321.4 14.9 %collective-permute-start.47 = (bf16[2,192,384]{2,1,0:T(8,128)(2,1)S(1)}, bf16[2,192,384]{2,1,0:T(8,128)(2,1)S(1)}, u32[]{:S(2)}, u32[]{:S(2)}) collective-permute-start(bf16[2,192,384]{2,1,0:T(8,128)(2,1)S(1)} %dynamic-slice_bitcast_fusion.21), channel_id=1, source_target_pairs={{0,4},{1,5},{2,6},{3,7},{4,0},{5,1},{6,2},{7,3},{8,12},{9,13},{10,... | collective-permute-start | bytes 884744 | tf_op jit(solution)/shard_map/ppermute | solution.py:689
  321.6 18.1 %collective-permute-start.54 = (bf16[48,1536]{1,0:T(8,128)(2,1)S(1)}, bf16[48,1536]{1,0:T(8,128)(2,1)S(1)}, u32[]{:S(2)}, u32[]{:S(2)}) collective-permute-start(bf16[48,1536]{1,0:T(8,128)(2,1)S(1)} %dynamic-slice_bitcast_fusion.30), channel_id=1, source_target_pairs={{0,16},{1,17},{2,18},{3,19},{4,20},{5,21},{6,22},{7,23},{8,24},{9,... | collective-permute-start | bytes 442376 | tf_op jit(solution)/shard_map/ppermute | solution.py:689
  336.5 5.0 %collective-permute-start.48 = (bf16[192,384]{1,0:T(8,128)(2,1)S(1)}, bf16[192,384]{1,0:T(8,128)(2,1)S(1)}, u32[]{:S(2)}, u32[]{:S(2)}) collective-permute-start(bf16[192,384]{1,0:T(8,128)(2,1)S(1)} %dynamic-slice_bitcast_fusion.31), channel_id=1, source_target_pairs={{0,1},{1,0},{2,3},{3,2},{4,5},{5,4},{6,7},{7,6},{8,9},{9,8},{10,11... | collective-permute-start | bytes 442376 | tf_op jit(solution)/shard_map/ppermute | solution.py:689
  338.2 19.1 %collective-permute-start.40 = (bf16[2,2,240,384]{3,2,1,0:T(8,128)(2,1)S(1)}, bf16[2,2,240,384]{3,2,1,0:T(8,128)(2,1)S(1)}, u32[]{:S(2)}, u32[]{:S(2)}) collective-permute-start(bf16[2,2,240,384]{3,2,1,0:T(8,128)(2,1)S(1)} %dynamic-slice_bitcast_fusion.9), channel_id=1, source_target_pairs={{0,1},{1,0},{2,3},{3,2},{4,5},{5,4},{6,7},{7,6},{8,9},{9,8},{10,11... | collective-permute-start | bytes 2211848 | tf_op jit(solution)/shard_map/ppermute | solution.py:689
  339.8 4.2 %collective-permute-start.55 = (bf16[48,768]{1,0:T(8,128)(2,1)S(1)}, bf16[48,768]{1,0:T(8,128)(2,1)S(1)}, u32[]{:S(2)}, u32[]{:S(2)}) collective-permute-start(bf16[48,768]{1,0:T(8,128)(2,1)S(1)} %fusion.9), channel_id=1, source_target_pairs={{0,8},{1,9},{2,10},{3,11},{4,12},{5,13},{6,14},{7,15},{8,0},{9,1},... | collective-permute-start | bytes 221192 | tf_op jit(solution)/shard_map/ppermute | solution.py:689
  341.7 15.9 %collective-permute-start.49 = (bf16[192,192]{1,0:T(8,128)(2,1)S(1)}, bf16[192,192]{1,0:T(8,128)(2,1)S(1)}, u32[]{:S(2)}, u32[]{:S(2)}) collective-permute-start(bf16[192,192]{1,0:T(8,128)(2,1)S(1)} %fusion.5), channel_id=1, source_target_pairs={{0,8},{1,9},{2,10},{3,11},{4,12},{5,13},{6,14},{7,15},{8,0},{9,1},... | collective-permute-start | bytes 221192 | tf_op jit(solution)/shard_map/ppermute | solution.py:689
  357.5 8.8 %collective-permute-start.41 = (bf16[2,240,384]{2,1,0:T(8,128)(2,1)S(1)}, bf16[2,240,384]{2,1,0:T(8,128)(2,1)S(1)}, u32[]{:S(2)}, u32[]{:S(2)}) collective-permute-start(bf16[2,240,384]{2,1,0:T(8,128)(2,1)S(1)} %dynamic-slice_bitcast_fusion.19), channel_id=1, source_target_pairs={{0,2},{1,3},{2,0},{3,1},{4,6},{5,7},{6,4},{7,5},{8,10},{9,11},{10,... | collective-permute-start | bytes 1105928 | tf_op jit(solution)/shard_map/ppermute | solution.py:689
  366.3 11.0 %collective-permute-start.42 = (bf16[240,384]{1,0:T(8,128)(2,1)S(1)}, bf16[240,384]{1,0:T(8,128)(2,1)S(1)}, u32[]{:S(2)}, u32[]{:S(2)}) collective-permute-start(bf16[240,384]{1,0:T(8,128)(2,1)S(1)} %dynamic-slice_bitcast_fusion.29), channel_id=1, source_target_pairs={{0,4},{1,5},{2,6},{3,7},{4,0},{5,1},{6,2},{7,3},{8,12},{9,13},{10,... | collective-permute-start | bytes 552968 | tf_op jit(solution)/shard_map/ppermute | solution.py:689
  377.6 2.6 collective-permute-start.43
  (49 other events, 493.6 us)

commit v2 on v1

--- a/solution.py
+++ b/solution.py
@@ -385,18 +385,345 @@
         small[...] = jnp.concatenate([gain_sum, shift_sum, jnp.zeros((6, D), F32)], axis=0)
 
 
-def norm_back_kernel(index, added, *refs):
-    pages = refs[:DOCS]
-    gain, mine, other = refs[DOCS : DOCS + 3]
-    rest = refs[DOCS + 3 :]
-    for place, page in enumerate(pages):
-        rows = slice(place * PAGE, (place + 1) * PAGE)
-        scaled, inverse = standardize(page[...].astype(F32))
-        upstream = mine[rows, :].astype(F32) + other[rows, :].astype(F32)
-        grad = norm_back(upstream, scaled, inverse, gain[index : index + 1, :])
-        if added:
-            grad = grad + rest[0][rows, :]
-        rest[-1][place] = grad.astype(BF16)
+class Places:
+    def __init__(self, wide, blk):
+        self.wide = wide
+        self.blk = blk
+        self.part = blk // 4
+        self.w = lax.axis_index("wide")
+        self.b = lax.axis_index("blk")
+        self.quarter = self.b // self.part
+        self.turn = self.quarter % 2
+
+    def bit(self, name):
+        axis, bit = name
+        return ((self.w if axis == "w" else self.b) // (1 << bit)) % 2
+
+    def flip(self, name):
+        axis, bit = name
+        step = (1 << bit) * (1 - 2 * self.bit(name))
+        return (self.w + step, self.b) if axis == "w" else (self.w, self.b + step)
+
+    def swap(self, turn):
+        core = self.w % 2
+        turned = self.turn if turn == 0 else 1 - self.turn
+        return (
+            self.w - core + self.quarter // 2,
+            (2 * core + turned) * self.part + self.b % self.part,
+        )
+
+    def swap_stays(self):
+        return self.w % 2 == self.quarter // 2
+
+
+def bit_names(wide, blk):
+    return [("w", bit) for bit in range(wide.bit_length() - 1)] + [
+        ("b", bit) for bit in range(blk.bit_length() - 1)
+    ]
+
+
+def group_bits(blk):
+    return [("b", bit) for bit in range((blk // 4).bit_length() - 1)] + [("w", 0)]
+
+
+def tile_bits(wide, blk):
+    return (
+        [("w", bit) for bit in range(wide.bit_length() - 2, 0, -1)]
+        + [("b", bit) for bit in range(blk.bit_length() - 2, -1, -1)]
+        + [("w", 0)]
+    )
+
+
+def remote(source, target, send, receive, device):
+    return pltpu.make_async_remote_copy(
+        src_ref=source,
+        dst_ref=target,
+        send_sem=send,
+        recv_sem=receive,
+        device_id=device,
+        device_id_type=pl.DeviceIdType.MESH,
+    )
+
+
+def greet(places, names, swaps):
+    barrier = pltpu.get_barrier_semaphore()
+    for name in names:
+        pl.semaphore_signal(
+            barrier, inc=1, device_id=places.flip(name), device_id_type=pl.DeviceIdType.MESH
+        )
+    count = len(names)
+    if swaps:
+        pl.semaphore_signal(
+            barrier, inc=1, device_id=places.swap(1), device_id_type=pl.DeviceIdType.MESH
+        )
+
+        @pl.when(jnp.logical_not(places.swap_stays()))
+        def _():
+            pl.semaphore_signal(
+                barrier, inc=1, device_id=places.swap(0), device_id_type=pl.DeviceIdType.MESH
+            )
+
+        count = count + 2 - places.swap_stays().astype(jnp.int32)
+    pl.semaphore_wait(barrier, count)
+
+
+class Scatter:
+    def __init__(self, places, names, order, grad, own, got, ends, sends, receives, local):
+        self.places = places
+        self.grad = grad
+        self.own = own
+        self.got = got
+        self.ends = ends
+        self.sends = sends
+        self.receives = receives
+        self.local = local
+        self.order = order
+        self.axes = []
+        left = list(names)
+        for name in order:
+            self.axes.append(left.index(name))
+            left.remove(name)
+        self.stages = len(order)
+
+    def cut(self, ref, stage, index):
+        axis = self.axes[stage]
+        return ref.at[(slice(None),) * axis + (index,)]
+
+    def copy(self, stage):
+        place = self.places
+        if stage == self.stages:
+            source, target, name = self.ends.at[0], self.ends.at[1], ("w", 0)
+        else:
+            name = self.order[stage]
+            source = self.grad if stage == 0 else self.got[stage - 1]
+            source = self.cut(source, stage, 1 - place.bit(name))
+            target = self.got[stage]
+        return remote(
+            source, target, self.sends.at[stage], self.receives.at[stage], place.flip(name)
+        )
+
+    def fetch(self):
+        kept = self.cut(self.grad, 0, self.places.bit(self.order[0]))
+        return pltpu.make_async_copy(kept, self.own, self.local)
+
+    def start(self):
+        self.copy(0).start()
+        self.fetch().start()
+
+    def add(self, stage):
+        self.copy(stage).wait_recv()
+        target = self.got[stage]
+        if stage == 0:
+            self.fetch().wait()
+            source = self.own
+        else:
+            source = self.cut(self.got[stage - 1], stage, self.places.bit(self.order[stage]))
+        lead = len(target.shape) - 2
+        if lead == 0:
+            target[...] = target[...] + source[...]
+        else:
+
+            def block(index, carry):
+                at = tuple((index // (1 << (lead - 1 - axis))) % 2 for axis in range(lead))
+                target[at] = target[at] + source[at]
+                return carry
+
+            lax.fori_loop(0, 1 << lead, block, 0)
+        if stage + 1 == self.stages:
+            lanes = target.shape[-1] // 2
+            piece = target[...]
+            second = self.places.bit(("w", 0)) == 1
+            self.ends[0] = jnp.where(second, piece[:, :lanes], piece[:, lanes:])
+        self.copy(stage + 1).start()
+
+    def end(self, out):
+        self.copy(self.stages).wait_recv()
+        lanes = out.shape[-1]
+        piece = self.got[-1][...]
+        other = self.ends[1]
+        second = self.places.bit(("w", 0)) == 1
+        mine = jnp.where(second, piece[:, lanes:], piece[:, :lanes])
+        out[0] = jnp.where(second, other, mine)
+        out[1] = jnp.where(second, mine, other)
+        for stage in range(self.stages + 1):
+            self.copy(stage).wait_send()
+
+
+class Rows:
+    def __init__(self, places, names, keep, send, sums, got, home, landed, sends, receives):
+        self.places = places
+        self.names = list(reversed(names))
+        self.keep = keep
+        self.send = send
+        self.sums = sums
+        self.got = got
+        self.home = home
+        self.landed = landed
+        self.sends = sends
+        self.receives = receives
+
+    def copy(self, stage):
+        source = self.send if stage == 0 else self.sums
+        rows = self.got[stage].shape[0]
+        if stage > 0:
+            source = source.at[pl.ds(rows, rows)]
+        return remote(
+            source, self.got[stage], self.sends.at[stage], self.receives.at[stage],
+            self.places.flip(self.names[stage]),
+        )
+
+    def start(self):
+        self.copy(0).start()
+
+    def add(self, stage):
+        self.copy(stage).wait_recv()
+        if stage > 0:
+            self.copy(stage).wait_send()
+        source = self.keep if stage == 0 else self.sums
+        rows = self.got[stage].shape[0]
+
+        def block(index, carry):
+            at = pl.ds(pl.multiple_of(index * PAGE, PAGE), PAGE)
+            self.sums[at, :] = source[at, :] + self.got[stage][at, :]
+            return carry
+
+        lax.fori_loop(0, rows // PAGE, block, 0)
+        if stage + 1 < len(self.names):
+            self.copy(stage + 1).start()
+
+    def norm(self, pages, gain, added):
+        for turn, page in enumerate(pages):
+            rows = slice(turn * PAGE, (turn + 1) * PAGE)
+            scaled, inverse = standardize(page[...].astype(F32))
+            grad = norm_back(self.sums[rows, :].astype(F32), scaled, inverse, gain)
+            if added is not None:
+                grad = grad + added[rows, :]
+            self.home[turn] = grad.astype(BF16)
+            self.go(turn, True)
+
+    def back(self, turn):
+        stage = len(self.names) + turn
+        return remote(
+            self.home.at[turn], self.landed.at[self.places.turn], self.sends.at[stage],
+            self.receives.at[stage], self.places.swap(turn),
+        )
+
+    def go(self, turn, begin):
+        def carry():
+            copy = self.back(turn)
+            copy.start() if begin else copy.wait()
+
+        if turn > 0:
+            carry()
+            return
+        stays = self.places.swap_stays()
+        pl.when(jnp.logical_not(stays))(carry)
+        if begin:
+
+            @pl.when(stays)
+            def _():
+                self.landed[self.places.turn] = self.home[turn]
+
+    def end(self, out):
+        for turn in range(DOCS):
+            self.go(turn, False)
+        self.copy(0).wait_send()
+        out[...] = self.landed[...]
+
+
+class Total:
+    def __init__(self, places, names, mine, got, sends, receives):
+        self.places = places
+        self.names = names
+        self.mine = mine
+        self.got = got
+        self.sends = sends
+        self.receives = receives
+
+    def copy(self, stage):
+        return remote(
+            self.mine.at[stage], self.got.at[stage], self.sends.at[stage], self.receives.at[stage],
+            self.places.flip(self.names[stage]),
+        )
+
+    def start(self):
+        self.copy(0).start()
+
+    def add(self, stage, out):
+        self.copy(stage).wait()
+        value = self.mine[stage] + self.got[stage]
+        if stage + 1 < len(self.names):
+            self.mine[stage + 1] = value
+            self.copy(stage + 1).start()
+        else:
+            out[...] = value
+
+
+def exchange_kernel(wide, blk, orders, *refs):
+    count = len(orders)
+    grads, refs = refs[:count], refs[count:]
+    (
+        text_keep, text_send, image_keep, image_send, text0, text1, image0, image1,
+        grad_hidden, gain, small,
+    ), refs = refs[:11], refs[11:]
+    (text_out, image_out, small_out), refs = refs[:3], refs[3:]
+    outs, refs = refs[:count], refs[count:]
+    places = Places(wide, blk)
+    names = bit_names(wide, blk)
+    stages = len(names)
+    groups = group_bits(blk)
+    scatters = []
+    for index, order in enumerate(orders):
+        own, got, ends, sends, receives, local = (
+            refs[0], refs[1 : 1 + stages], refs[1 + stages], refs[2 + stages], refs[3 + stages],
+            refs[4 + stages],
+        )
+        refs = refs[5 + stages :]
+        scatters.append(
+            Scatter(
+                places, tile_bits(wide, blk), order, grads[index], own, got, ends, sends,
+                receives, local,
+            )
+        )
+    streams = []
+    for keep, send in ((text_keep, text_send), (image_keep, image_send)):
+        sums, got, home, landed, sends, receives = (
+            refs[0], refs[1 : 1 + len(groups)], refs[1 + len(groups)], refs[2 + len(groups)],
+            refs[3 + len(groups)], refs[4 + len(groups)],
+        )
+        refs = refs[5 + len(groups) :]
+        streams.append(
+            Rows(places, groups, keep, send, sums, got, home, landed, sends, receives)
+        )
+    text, image = streams
+    total = Total(places, names, *refs)
+
+    greet(places, names, True)
+    total.mine[0] = small[...]
+    text.start()
+    image.start()
+    total.start()
+    for scatter in scatters:
+        scatter.start()
+    for stage in range(len(groups)):
+        text.add(stage)
+        image.add(stage)
+        if stage == 0:
+            scatters[0].add(0)
+            scatters[1].add(0)
+    total.add(0, small_out)
+    text.norm((text0, text1), gain[0:1, :], grad_hidden)
+    image.norm((image0, image1), gain[2:3, :], None)
+    for scatter in scatters[2:]:
+        scatter.add(0)
+    for stage in range(1, stages):
+        total.add(stage, small_out)
+        for scatter in scatters:
+            scatter.add(stage)
+    for scatter, out in zip(scatters, outs):
+        scatter.end(out)
+    text.end(text_out)
+    image.end(image_out)
 
 
 def whole(shape):
@@ -645,25 +972,45 @@
     )
 
 
-def final_norm(index, pages, gain, mine, other, added):
-    ins = page_inputs(pages) + [
-        (whole(gain.shape), gain),
-        (whole((ROWS, D)), mine),
-        (whole((ROWS, D)), other),
-    ]
-    if added is not None:
-        ins.append((whole((ROWS, D)), added))
-    (result,) = call(
-        functools.partial(norm_back_kernel, index, added is not None),
-        "final_norm",
-        1,
-        ins,
-        [(whole((DOCS, PAGE, D)), shaped((DOCS, PAGE, D), BF16))],
-        [],
-        10**7,
-        3 * 10**6,
-    )
-    return result
+def exchange(wide, blk, orders, grads, keeps, texts, images, grad_hidden, gain, small):
+    names = bit_names(wide, blk)
+    stages = len(names)
+    groups = group_bits(blk)
+    vmem = pl.BlockSpec(memory_space=pltpu.VMEM)
+    scratch = []
+    results = []
+    for grad in grads:
+        *lead, rows, lanes = grad.shape
+        scratch.append(pltpu.VMEM((*lead[1:], rows, lanes), BF16))
+        for stage in range(stages):
+            scratch.append(pltpu.VMEM((*lead[stage + 1 :], rows, lanes), BF16))
+        scratch.append(pltpu.VMEM((2, rows, lanes // 2), BF16))
+        scratch += [pltpu.SemaphoreType.DMA((stages + 1,))] * 2 + [pltpu.SemaphoreType.DMA]
+        results.append(shaped((2, rows, lanes // 2), BF16))
+    for keep, _ in keeps:
+        rows = keep.shape[0]
+        scratch.append(pltpu.VMEM((rows, D), BF16))
+        for stage in range(len(groups)):
+            scratch.append(pltpu.VMEM((rows >> stage, D), BF16))
+        scratch += [pltpu.VMEM((DOCS, PAGE, D), BF16)] * 2
+        scratch += [pltpu.SemaphoreType.DMA((len(groups) + DOCS,))] * 2
+    scratch += [pltpu.VMEM((stages, *small.shape), F32)] * 2
+    scratch += [pltpu.SemaphoreType.DMA((stages,))] * 2
+    stream = shaped((DOCS, PAGE, D), BF16)
+    operands = [*grads, *keeps[0], *keeps[1], *texts, *images, grad_hidden, gain, small]
+    return pl.pallas_call(
+        functools.partial(exchange_kernel, wide, blk, orders),
+        in_specs=[pl.BlockSpec(memory_space=pl.ANY)] * len(grads)
+        + [vmem] * (len(operands) - len(grads)),
+        out_specs=[vmem] * (3 + len(grads)),
+        out_shape=[stream, stream, shaped(small.shape, F32), *results],
+        scratch_shapes=scratch,
+        name="exchange",
+        compiler_params=pltpu.CompilerParams(
+            vmem_limit_bytes=VMEM_LIMIT, collective_id=0, has_side_effects=True
+        ),
+        cost_estimate=pl.CostEstimate(flops=10**7, bytes_accessed=4 * 10**8, transcendentals=0),
+    )(*operands)
 
 
 class Layout:
@@ -723,67 +1070,14 @@
             pages = pages + [self.flip(item, name) for item in pages]
         return pages
 
-    def group_sum(self, keep, send):
-        names = self.group_bits()
-        for name in reversed(names):
-            got = self.flip(send, name)
-            if name == names[0]:
-                return keep, got
-            half = keep.shape[0] // 2
-            keep, send = (keep[:half] + got[:half]), (keep[half:] + got[half:])
-
-    def reduce_scatter(self, grads, order):
-        wide_names = [("w", bit) for bit in range(self.wide.bit_length() - 2, 0, -1)]
-        blk_names = [("b", bit) for bit in range(self.blk.bit_length() - 2, -1, -1)]
-        names = wide_names + blk_names + [("w", 0)]
-        parts = [
-            grad.reshape((2,) * len(names) + (grad.shape[1] // (2 * self.blk), grad.shape[2]))
-            for grad in grads
-        ]
-        for name in order:
-            axis = names.index(name)
-            names.remove(name)
-            bit = self.bits[name]
-
-            def pick(index):
-                picked = [
-                    lax.dynamic_index_in_dim(part, index, axis, keepdims=False) for part in parts
-                ]
-                return picked[0] if len(picked) == 1 else jnp.concatenate(picked, axis=-2)
-
-            parts = [pick(bit) + self.flip(pick(1 - bit), name)]
-        return parts[0]
-
-    def finish(self, piece):
-        rows, lanes = piece.shape
-        halves = jnp.stack([piece[:, : lanes // 2], piece[:, lanes // 2 :]])
-        bit = self.bits["w", 0]
-        mine = lax.dynamic_index_in_dim(halves, bit, 0, keepdims=False)
-        other = self.flip(lax.dynamic_index_in_dim(halves, 1 - bit, 0, keepdims=False), ("w", 0))
-        flag = bit == 0
-        return jnp.stack([jnp.where(flag, mine, other), jnp.where(flag, other, mine)])
-
-    def tiles(self, piece, counts):
-        both = self.finish(piece)
-        results = []
-        start = 0
-        for count in counts:
-            part = both[:, start : start + count, :]
-            start += count
-            results.append(jnp.transpose(part.reshape(-1, part.shape[-1])).astype(F32))
-        return results
-
-    def all_sum(self, value):
-        for name in self.bits:
-            value = value + self.flip(value, name)
-        return value
-
-
-def cut_lanes(grad, cuts):
-    if grad.shape[0] == cuts:
-        return grad
-    _, rows, lanes = grad.shape
-    return jnp.transpose(grad.reshape(rows, cuts, lanes // cuts), (1, 0, 2))
+
+def tiled(grad, wide, blk):
+    cuts = wide // 2
+    if grad.shape[0] != cuts:
+        _, rows, lanes = grad.shape
+        grad = jnp.transpose(grad.reshape(rows, cuts, lanes // cuts), (1, 0, 2))
+    names = tile_bits(wide, blk)
+    return grad.reshape((2,) * len(names) + (grad.shape[1] // (2 * blk), grad.shape[2]))
 
 
 def body(
@@ -857,12 +1151,6 @@
         hidden, raw, gate, cots, cross_output, norm_gain, norm_bias, expand_weight,
         expand_bias.reshape(1, FF), reduce_weight, reduce_bias.reshape(1, D), cuts, far_cuts,
     )
-    wide_bits = [("w", bit) for bit in range(1, lay.wide.bit_length() - 1)]
-    low_blk = [("b", 0)]
-    high_blk = [("b", bit) for bit in range(1, blk_count.bit_length() - 1)]
-    core = [("w", 0)]
-    expand_piece = lay.reduce_scatter([cut_lanes(d_expand, wide_half)], core + wide_bits + high_blk + low_blk)
-    reduce_piece = lay.reduce_scatter([cut_lanes(d_reduce, wide_half)], core + low_blk + high_blk + wide_bits)
     joined_blocks = lay.from_group([joined[:PAGE], joined[PAGE:]])
 
     (
@@ -873,40 +1161,49 @@
         cross_lse, cross_delta, cross_pairs, cross_query, gate_wide, self_output, hidden, self_out,
         grad_mixed, grad_logit, cuts,
     )
-    cross_piece = lay.reduce_scatter(
-        [cut_lanes(item, wide_half) for item in (d_pairs, d_query, d_cross_output, d_self_output)],
-        core + wide_bits + low_blk + high_blk,
-    )
-    image_mine, image_other = lay.group_sum(image_keep, image_send)
-    image_back = final_norm(2, image_own, norm_gain, image_mine, image_other, None)
-    image_grad = lay.from_group([image_back[0], image_back[1]])
-    small_first = lay.all_sum(
-        jnp.concatenate([d_gate, d_expand_bias.reshape(-1, D), small_last[:4], small_cross[:4]], axis=0)
-    )
-
     text_keep, text_send, d_project, small_self = self_back(
         text_pages, norm_gain, norm_bias, text_closed, self_q, self_k, self_v, self_do,
         self_lse, self_delta, self_project, cuts,
     )
-    text_mine, text_other = lay.group_sum(text_keep, text_send)
-    text_back = final_norm(0, text_own, norm_gain, text_mine, text_other, grad_hidden)
-    text_grad = lay.from_group([text_back[0], text_back[1]])
-    project_piece = lay.reduce_scatter(
-        [cut_lanes(d_project, wide_half)], core + low_blk + wide_bits + high_blk
-    )
-    small_second = lay.all_sum(small_self)
-
-    share = 2 * blk_count
-    (grad_expand_weight,) = lay.tiles(expand_piece, [FF // share])
-    (grad_reduce_weight,) = lay.tiles(reduce_piece, [D // share])
-    grad_cross_pairs, grad_cross_query, grad_cross_output, grad_self_output = lay.tiles(
-        cross_piece, [2 * D // share, D // share, D // share, D // share]
-    )
-    (grad_self_project,) = lay.tiles(project_piece, [3 * D // share])
-    grad_gate_weight = jnp.transpose(small_first[:H])
+    core = [("w", 0)]
+    wide_bits = [("w", bit) for bit in range(1, lay.wide.bit_length() - 1)]
+    low_blk = [("b", 0)]
+    high_blk = [("b", bit) for bit in range(1, blk_count.bit_length() - 1)]
+    plan = [
+        (d_expand, core + wide_bits + high_blk + low_blk),
+        (d_reduce, core + low_blk + high_blk + wide_bits),
+        (d_project, core + wide_bits + low_blk + high_blk),
+        (d_pairs, core + low_blk + wide_bits + high_blk),
+        (d_query, core + low_blk + high_blk + wide_bits),
+        (d_cross_output, core + wide_bits + high_blk + low_blk),
+        (d_self_output, core + low_blk + wide_bits + high_blk),
+    ]
+    small = jnp.concatenate(
+        [d_gate, d_expand_bias.reshape(-1, D), small_last[:4], small_cross[:4], small_self[:4]],
+        axis=0,
+    )
+    text_grad, image_grad, sums, *pieces = exchange(
+        lay.wide,
+        lay.blk,
+        [order for _, order in plan],
+        [tiled(grad, lay.wide, lay.blk) for grad, _ in plan],
+        ((text_keep, text_send), (image_keep, image_send)),
+        text_own,
+        image_own,
+        grad_hidden,
+        norm_gain,
+        small,
+    )
+    (
+        grad_expand_weight, grad_reduce_weight, grad_self_project, grad_cross_pairs,
+        grad_cross_query, grad_cross_output, grad_self_output,
+    ) = [
+        jnp.transpose(piece.reshape(-1, piece.shape[-1])).astype(F32) for piece in pieces
+    ]
     at_bias = 16
     at_last = at_bias + FF // D
     at_cross = at_last + 4
+    at_self = at_cross + 4
     return (
         joined_blocks,
         text_grad,
@@ -918,25 +1215,11 @@
         grad_cross_output,
         grad_expand_weight,
         grad_reduce_weight,
-        grad_gate_weight,
-        small_first[at_bias:at_last].reshape(FF),
-        small_first[at_last],
-        jnp.stack(
-            [
-                small_second[0],
-                small_first[at_cross],
-                small_first[at_cross + 2],
-                small_first[at_last + 1],
-            ]
-        ),
-        jnp.stack(
-            [
-                small_second[1],
-                small_first[at_cross + 1],
-                small_first[at_cross + 3],
-                small_first[at_last + 2],
-            ]
-        ),
+        jnp.transpose(sums[:H]),
+        sums[at_bias:at_last].reshape(FF),
+        sums[at_last],
+        jnp.stack([sums[at_self], sums[at_cross], sums[at_cross + 2], sums[at_last + 1]]),
+        jnp.stack([sums[at_self + 1], sums[at_cross + 1], sums[at_cross + 3], sums[at_last + 2]]),
     )
 
 

time: 390 us -> 310 us (0.79)
  Pallas kernels: 107 us -> 231 us
  waiting for transfers between devices: 130 us -> 10.2 us
  starting transfers between devices: 83.7 us -> 33.9 us
  other arithmetic: 25.3 us -> 8.04 us
  local copies, waits for them, and re-layouts: 35.4 us -> 19.2 us
    pallas_call x0 -> x1, Pallas kernels: none -> 129 us  [exchange(): pl.pallas_call(functools.partial(exchange_kernel, wide, blk, orders), in_...]
    ppermute x66 -> x24, waiting for transfers between devices: 130 us -> 10.2 us  [exchange(): return lax.ppermute(value, AXES, pairs)]
    ppermute x66 -> x24, starting transfers between devices: 83.7 us -> 33.9 us  [exchange(): return lax.ppermute(value, AXES, pairs)]
    squeeze x24 -> x0, local copies, waits for them, and re-layouts: 17.1 us -> none  [the longest x22 15.3 us: pick(): lax.dynamic_index_in_dim(part, index, axis, keepdims=False)]
    add x32 -> x0, other arithmetic: 14.1 us -> none  [the longest x20 12.2 us: reduce_scatter(): parts = [pick(bit) + self.flip(pick(1 - bit), name)]]
    pallas_call x7 -> x5, Pallas kernels: 107 us -> 102 us  [call(): pl.pallas_call(kernel, grid=(steps,), in_specs=list(in_specs), out_specs=...]
    unnamed x100 -> x65, local copies, waits for them, and re-layouts: 7.69 us -> 3.5 us
  transfers between devices with their start and end apart: 66 -> 24, of which waited for: 24 -> 4; matrix products, arithmetic and copies ran while one was open for 13% -> 5% of each run, Pallas kernels for 23% -> 9%
where the time goes in v2:
time: 310 us; the launch traced here: 304 us
  Pallas kernels  231 us (75%)
  starting transfers between devices  33.9 us (11%)
  local copies, waits for them, and re-layouts  19.2 us (6%)
  waiting for transfers between devices  10.2 us (3%)
  other arithmetic  8.04 us (3%)
    pallas_call x1, Pallas kernels, exchange(): pl.pallas_call(functools.partial(exchange_kernel, wide, blk, orders), in_...  129 us
    pallas_call x5, Pallas kernels, call(): pl.pallas_call(kernel, grid=(steps,), in_specs=list(in_specs), out_specs=...  102 us
    ppermute x24, starting transfers between devices, exchange(): return lax.ppermute(value, AXES, pairs)  33.9 us
    ppermute x24, waiting for transfers between devices, exchange(): return lax.ppermute(value, AXES, pairs)  10.2 us
  transfers between devices with their start and end apart: 24, of which 4 were waited for; matrix products, arithmetic and copies ran while one was open for 5% of the time, Pallas kernels for 9%

profile of v2, /device:TPU:1, one launch (start us, length us, event | category | flops | bytes accessed | tf_op | source)
XLA Modules:
  0.0 304.0 jit_solution(8408238313345825642)
XLA Ops:
  0.7 0.7 broadcast_compare_fusion
  1.4 0.8 or_and_fusion
  2.2 5.6 %collective-permute-start.16 = (bf16[256]{0:T(256)(128)(2,1)S(1)}, bf16[256]{0:T(256)(128)(2,1)S(1)}, u32[]{:S(2)}, u32[]{:S(2)}) collective-permute-start(bf16[256]{0:T(256)(128)(2,1)S(1)} %get-tuple-element.107), channel_id=1, source_target_pairs={{0,0},{1,1},{2,2},{3,3},{4,8},{5,9},{6,10},{7,11},{8,4},{9,5},{10,... | collective-permute-start | bytes 1544 | tf_op jit(solution)/shard_map/ppermute | solution.py:1036
  7.8 1.1 collective-permute-start.17
  8.9 1.0 dynamic-slice_bitcast_fusion.4
  10.0 2.6 collective-permute-start.1
  12.5 1.9 collective-permute-start
  14.5 1.3 collective-permute-start.18
  15.8 1.0 dynamic-slice_bitcast_fusion.2
  16.9 2.2 collective-permute-start.3
  19.0 2.7 collective-permute-start.2
  21.9 0.6 reshape.95.b_reduce
  22.5 0.2 copy.33
  22.7 0.7 pad.4.refs_12_.refs_20_
  23.5 0.5 collective-permute-start.13
  24.0 0.3 collective-permute-start.11
  24.3 0.2 collective-permute-done.refs_0_.refs_11_
  24.4 1.0 collective-permute-start.10
  25.5 0.6 collective-permute-start.12
  26.1 4.6 %collective-permute-done.2.refs_2_.refs_0_.refs_13_ = bf16[128,768]{1,0:T(8,128)(2,1)S(1)} collective-permute-done((bf16[128,768]{1,0:T(8,128)(2,1)S(1)}, bf16[128,768]{1,0:T(8,128)(2,1)S(1)}, u32[]{:S(2)}, u32[]{:S(2)}) %collective-permute-start.2) | collective-permute-done | bytes 196640 | tf_op jit(solution)/shard_map/ppermute | solution.py:1036
  30.8 0.6 collective-permute-start.5
  31.4 0.9 collective-permute-start.4
  32.3 2.4 collective-permute-done.10.refs_2_
  34.7 1.3 collective-permute-start.14
  36.0 1.1 broadcast_select_fusion
  37.1 2.6 collective-permute-start.21
  39.8 0.4 collective-permute-start.7
  40.2 2.9 collective-permute-done.4.refs_4_.refs_2_
  43.1 0.8 collective-permute-start.6
  44.1 0.4 collective-permute-start.8
  44.5 0.1 copy-done.22
  44.7 13.3 %self_forward.1 = (f32[256,768]{1,0:T(8,128)}, f32[24,256]{1,0:T(8,128)}, bf16[256,768]{1,0:T(8,128)(2,1)}, bf16[1024,768]{1,0:T(8,128)(2,1)}, bf16[1024,768]{1,0:T(8,128)(2,1)}) custom-call(bf16[128,768]{1,0:T(8,128)(2,1)} %copy-done.5, bf16[128,768]{1,0:T(8,128)(2,1)} %copy-done.4, bf16[128,768]{1,0:T(8,128)(2,1)} %copy-done.20, ...), custom_call_target="tpu_custom_call" | custom-call | flops 6000000000 | bytes 12000000 | tf_op jit(solution)/shard_map/self_forward/pallas_call | solution.py:748
  58.1 3.9 %collective-permute-start.20 = (bf16[128,768]{1,0:T(8,128)(2,1)S(1)}, bf16[128,768]{1,0:T(8,128)(2,1)S(1)}, u32[]{:S(2)}, u32[]{:S(2)}) collective-permute-start(bf16[128,768]{1,0:T(8,128)(2,1)S(1)} %get-tuple-element.114), channel_id=1, source_target_pairs={{0,0},{1,1},{2,2},{3,3},{4,8},{5,9},{6,10},{7,11},{8,4},{9,5},{10,... | collective-permute-start | bytes 589832 | tf_op jit(solution)/shard_map/ppermute | solution.py:1036
  62.0 0.6 copy-done.27
  62.9 14.9 %cross_forward.1 = (f32[256,768]{1,0:T(8,128)}, f32[256,128]{1,0:T(8,128)}, f32[256,768]{1,0:T(8,128)}, f32[24,256]{1,0:T(8,128)}, bf16[256,768]{1,0:T(8,128)(2,...) custom-call(bf16[128,768]{1,0:T(8,128)(2,1)} %copy-done.5, bf16[128,768]{1,0:T(8,128)(2,1)} %copy-done.4, ...), custom_call_target="tpu_custom_call" | custom-call | flops 7000000000 | bytes 14000000 | tf_op jit(solution)/shard_map/cross_forward/pallas_call | solution.py:748
  77.8 0.7 copy-done.30
  78.5 18.0 %forward_back.1 = (bf16[256,768]{1,0:T(8,128)(2,1)}, bf16[2,3072,384]{2,1,0:T(8,128)(2,1)}, bf16[2,768,1536]{2,1,0:T(8,128)(2,1)}, bf16[2,768,384]{2,1,0:T(8,128...) custom-call(f32[256,768]{1,0:T(8,128)} %get-tuple-element.62.hidden., ...), custom_call_target="tpu_custom_call" | custom-call | flops 8000000000 | bytes 25000000 | tf_op jit(solution)/shard_map/forward_back/pallas_call | solution.py:748
  96.5 0.5 broadcast.21
  97.0 1.4 reduce.9
  98.4 0.7 slice.58
  99.1 29.5 %cross_back.1 = (bf16[512,768]{1,0:T(8,128)(2,1)}, bf16[512,768]{1,0:T(8,128)(2,1)}, bf16[2,1536,384]{2,1,0:T(8,128)(2,1)}, bf16[2,768,384]{2,1,0:T(8,128)(2,1)}...) custom-call(bf16[128,768]{1,0:T(8,128)(2,1)} %copy-done.7, ...), custom_call_target="tpu_custom_call" | custom-call | flops 12000000000 | bytes 20000000 | tf_op jit(solution)/shard_map/cross_back/pallas_call | solution.py:748
  128.7 26.0 %self_back.1 = (bf16[512,768]{1,0:T(8,128)(2,1)}, bf16[512,768]{1,0:T(8,128)(2,1)}, bf16[2,2304,384]{2,1,0:T(8,128)(2,1)}, f32[8,768]{1,0:T(8,128)}) custom-call(bf16[128,768]{1,0:T(8,128)(2,1)} %copy-done.5, bf16[128,768]{1,0:T(8,128)(2,1)} %copy-done.4, bf16[128,768]{1,0:T(8,128)(2,1)} %copy-done.20, bf16[128,768]{1,0:T(8,128)(2,1)} %copy-done.19, ...), custom_call_target="tpu_custom_call" | custom-call | flops 11000000512 | bytes 17000000 | tf_op jit(solution)/shard_map/self_back/pallas_call | solution.py:748
  154.7 0.7 slice.60
  155.4 1.9 concatenate.17.refs_17_
  157.3 129.3 %exchange.1 = (bf16[2,128,768]{2,1,0:T(8,128)(2,1)}, bf16[2,128,768]{2,1,0:T(8,128)(2,1)}, f32[32,768]{1,0:T(8,128)}, bf16[2,192,192]{2,1,0:T(8,128)(2,1)}, bf16...) custom-call(bf16[2,2,2,2,2,192,384]{6,5,4,3,2,1,0:T(8,128)(2,1)} %bi, ...), custom_call_target="tpu_custom_call" | custom-call | flops 10000000 | bytes 400000000 | tf_op jit(solution)/shard_map/exchange/pallas_call | solution.py:1001
  286.6 0.8 slice.62
  287.4 1.6 fusion.4
  289.0 2.1 collective-permute-start.22
  291.1 0.9 collective-permute-start.23
  292.0 0.6 reshape.104
  292.6 0.8 bitcast_convert_fusion.5
  293.4 0.7 copy.35
  294.2 0.9 bitcast_convert_fusion.2
  295.1 0.8 copy.37
  295.9 0.7 copy.38
  296.7 0.7 copy.36
  297.4 0.9 copy.34
  298.3 0.7 convert_bitcast_fusion
  299.1 0.9 copy.39
  300.0 0.6 pad_maximum_fusion.1
  300.6 0.6 slice_bitcast_fusion
  301.3 0.8 pad_maximum_fusion
  302.1 0.7 copy.42
  302.8 0.7 copy.43
  (99 shorter events, 0.9 us)
Async XLA Ops:
  0.6 21.2 %copy-start = (bf16[2,128,768]{2,1,0:T(8,128)(2,1)S(1)}, bf16[2,128,768]{2,1,0:T(8,128)(2,1)}, u32[]{:S(2)}) copy-start(bf16[2,128,768]{2,1,0:T(8,128)(2,1)} %param.20) | copy-start | bytes 1179652
  0.7 21.3 %copy-start.17 = (f32[768]{0:T(1024)S(1)}, f32[768]{0:T(1024)}, u32[]{:S(2)}) copy-start(f32[768]{0:T(1024)} %param.33) | copy-start | bytes 9220
  0.7 21.9 %copy-start.15 = (bf16[768,12]{0,1:T(8,128)(2,1)S(1)}, bf16[768,12]{0,1:T(8,128)(2,1)}, u32[]{:S(2)}) copy-start(bf16[768,12]{0,1:T(8,128)(2,1)} %param.29) | copy-start | bytes 55300
  2.2 12.3 %collective-permute-start.16 = (bf16[256]{0:T(256)(128)(2,1)S(1)}, bf16[256]{0:T(256)(128)(2,1)S(1)}, u32[]{:S(2)}, u32[]{:S(2)}) collective-permute-start(bf16[256]{0:T(256)(128)(2,1)S(1)} %get-tuple-element.107), channel_id=1, source_target_pairs={{0,0},{1,1},{2,2},{3,3},{4,8},{5,9},{6,10},{7,11},{8,4},{9,5},{10,... | collective-permute-start | bytes 1544 | tf_op jit(solution)/shard_map/ppermute | solution.py:1036
  7.8 6.7 %collective-permute-start.17 = (bf16[256]{0:T(256)(128)(2,1)S(1)}, bf16[256]{0:T(256)(128)(2,1)S(1)}, u32[]{:S(2)}, u32[]{:S(2)}) collective-permute-start(bf16[256]{0:T(256)(128)(2,1)S(1)} %get-tuple-element.108), channel_id=1, source_target_pairs={{0,2},{1,3},{2,0},{3,1},{4,10},{5,11},{6,8},{7,9},{8,6},{9,7},{10,... | collective-permute-start | bytes 1544 | tf_op jit(solution)/shard_map/ppermute | solution.py:1036
  10.0 13.5 %collective-permute-start.1 = (bf16[128,768]{1,0:T(8,128)(2,1)S(1)}, bf16[128,768]{1,0:T(8,128)(2,1)S(1)}, u32[]{:S(2)}, u32[]{:S(2)}) collective-permute-start(bf16[128,768]{1,0:T(8,128)(2,1)S(1)} %get-tuple-element.117), channel_id=1, source_target_pairs={{0,2},{1,3},{2,0},{3,1},{4,10},{5,11},{6,8},{7,9},{8,6},{9,7},{10,... | collective-permute-start | bytes 589832 | tf_op jit(solution)/shard_map/ppermute | solution.py:1036
  12.5 11.9 %collective-permute-start = (bf16[128,768]{1,0:T(8,128)(2,1)S(1)}, bf16[128,768]{1,0:T(8,128)(2,1)S(1)}, u32[]{:S(2)}, u32[]{:S(2)}) collective-permute-start(bf16[128,768]{1,0:T(8,128)(2,1)S(1)} %get-tuple-element.118), channel_id=1, source_target_pairs={{0,0},{1,1},{2,2},{3,3},{4,8},{5,9},{6,10},{7,11},{8,4},{9,5},{10,... | collective-permute-start | bytes 589832 | tf_op jit(solution)/shard_map/ppermute | solution.py:1036
  14.5 7.2 %collective-permute-start.18 = (bf16[2,256]{1,0:T(2,128)(2,1)S(1)}, bf16[2,256]{1,0:T(2,128)(2,1)S(1)}, u32[]{:S(2)}, u32[]{:S(2)}) collective-permute-start(bf16[2,256]{1,0:T(2,128)(2,1)S(1)} %pad_maximum_fusion.5), channel_id=1, source_target_pairs={{0,1},{1,0},{2,3},{3,2},{4,5},{5,4},{6,7},{7,6},{8,9},{9,8},{10,11... | collective-permute-start | bytes 3080 | tf_op jit(solution)/shard_map/ppermute | solution.py:1036
  16.9 8.6 %collective-permute-start.3 = (bf16[128,768]{1,0:T(8,128)(2,1)S(1)}, bf16[128,768]{1,0:T(8,128)(2,1)S(1)}, u32[]{:S(2)}, u32[]{:S(2)}) collective-permute-start(bf16[128,768]{1,0:T(8,128)(2,1)S(1)} %get-tuple-element.115), channel_id=1, source_target_pairs={{0,2},{1,3},{2,0},{3,1},{4,10},{5,11},{6,8},{7,9},{8,6},{9,7},{10,... | collective-permute-start | bytes 589832 | tf_op jit(solution)/shard_map/ppermute | solution.py:1036
  19.0 11.7 %collective-permute-start.2 = (bf16[128,768]{1,0:T(8,128)(2,1)S(1)}, bf16[128,768]{1,0:T(8,128)(2,1)S(1)}, u32[]{:S(2)}, u32[]{:S(2)}) collective-permute-start(bf16[128,768]{1,0:T(8,128)(2,1)S(1)} %get-tuple-element.116), channel_id=1, source_target_pairs={{0,0},{1,1},{2,2},{3,3},{4,8},{5,9},{6,10},{7,11},{8,4},{9,5},{10,... | collective-permute-start | bytes 589832 | tf_op jit(solution)/shard_map/ppermute | solution.py:1036
  21.8 1.6 collective-permute-start.19
  23.4 21.1 %copy-start.4 = (bf16[128,768]{1,0:T(8,128)(2,1)}, bf16[128,768]{1,0:T(8,128)(2,1)S(1)}, u32[]{:S(2)}) copy-start(bf16[128,768]{1,0:T(8,128)(2,1)S(1)} %collective-permute-done.1.refs_1_.refs_12_) | copy-start | bytes 589828
  23.5 7.9 %collective-permute-start.13 = (bf16[128,768]{1,0:T(8,128)(2,1)S(1)}, bf16[128,768]{1,0:T(8,128)(2,1)S(1)}, u32[]{:S(2)}, u32[]{:S(2)}) collective-permute-start(bf16[128,768]{1,0:T(8,128)(2,1)S(1)} %collective-permute-done.1.refs_1_.refs_12_), channel_id=1, source_target_pairs={{0,8},{1,9},{2,10},{3,11},{4,12},{5,13},{6,14},{7,15},{8,0},{9,1},... | collective-permute-start | bytes 589832 | tf_op jit(solution)/shard_map/ppermute | solution.py:1036
  24.0 8.2 %collective-permute-start.11 = (bf16[128,768]{1,0:T(8,128)(2,1)S(1)}, bf16[128,768]{1,0:T(8,128)(2,1)S(1)}, u32[]{:S(2)}, u32[]{:S(2)}) collective-permute-start(bf16[128,768]{1,0:T(8,128)(2,1)S(1)} %collective-permute-done.1.refs_1_.refs_12_), channel_id=1, source_target_pairs={{0,1},{1,0},{2,3},{3,2},{4,5},{5,4},{6,7},{7,6},{8,9},{9,8},{10,11... | collective-permute-start | bytes 589832 | tf_op jit(solution)/shard_map/ppermute | solution.py:1036
  24.4 20.1 %copy-start.5 = (bf16[128,768]{1,0:T(8,128)(2,1)}, bf16[128,768]{1,0:T(8,128)(2,1)S(1)}, u32[]{:S(2)}) copy-start(bf16[128,768]{1,0:T(8,128)(2,1)S(1)} %collective-permute-done.refs_0_.refs_11_) | copy-start | bytes 589828
  24.4 10.2 %collective-permute-start.10 = (bf16[128,768]{1,0:T(8,128)(2,1)S(1)}, bf16[128,768]{1,0:T(8,128)(2,1)S(1)}, u32[]{:S(2)}, u32[]{:S(2)}) collective-permute-start(bf16[128,768]{1,0:T(8,128)(2,1)S(1)} %collective-permute-done.refs_0_.refs_11_), channel_id=1, source_target_pairs={{0,1},{1,0},{2,3},{3,2},{4,5},{5,4},{6,7},{7,6},{8,9},{9,8},{10,11... | collective-permute-start | bytes 589832 | tf_op jit(solution)/shard_map/ppermute | solution.py:1036
  25.5 32.5 %copy-start.6 = (bf16[128,768]{1,0:T(8,128)(2,1)}, bf16[128,768]{1,0:T(8,128)(2,1)S(1)}, u32[]{:S(2)}) copy-start(bf16[128,768]{1,0:T(8,128)(2,1)S(1)} %collective-permute-done.3.refs_3_.refs_1_.refs_14_) | copy-start | bytes 589828
  25.5 11.6 %collective-permute-start.12 = (bf16[128,768]{1,0:T(8,128)(2,1)S(1)}, bf16[128,768]{1,0:T(8,128)(2,1)S(1)}, u32[]{:S(2)}, u32[]{:S(2)}) collective-permute-start(bf16[128,768]{1,0:T(8,128)(2,1)S(1)} %collective-permute-done.refs_0_.refs_11_), channel_id=1, source_target_pairs={{0,8},{1,9},{2,10},{3,11},{4,12},{5,13},{6,14},{7,15},{8,0},{9,1},... | collective-permute-start | bytes 589832 | tf_op jit(solution)/shard_map/ppermute | solution.py:1036
  30.8 27.3 %copy-start.7 = (bf16[128,768]{1,0:T(8,128)(2,1)}, bf16[128,768]{1,0:T(8,128)(2,1)S(1)}, u32[]{:S(2)}) copy-start(bf16[128,768]{1,0:T(8,128)(2,1)S(1)} %collective-permute-done.2.refs_2_.refs_0_.refs_13_) | copy-start | bytes 589828
  30.8 9.0 %collective-permute-start.5 = (bf16[128,768]{1,0:T(8,128)(2,1)S(1)}, bf16[128,768]{1,0:T(8,128)(2,1)S(1)}, u32[]{:S(2)}, u32[]{:S(2)}) collective-permute-start(bf16[128,768]{1,0:T(8,128)(2,1)S(1)} %collective-permute-done.3.refs_3_.refs_1_.refs_14_), channel_id=1, source_target_pairs={{0,1},{1,0},{2,3},{3,2},{4,5},{5,4},{6,7},{7,6},{8,9},{9,8},{10,11... | collective-permute-start | bytes 589832 | tf_op jit(solution)/shard_map/ppermute | solution.py:1036
  31.4 13.1 %copy-start.18 = (bf16[128,768]{1,0:T(8,128)(2,1)}, bf16[128,768]{1,0:T(8,128)(2,1)S(1)}, u32[]{:S(2)}) copy-start(bf16[128,768]{1,0:T(8,128)(2,1)S(1)} %collective-permute-done.13.refs_5_) | copy-start | bytes 589828
  31.4 11.7 %collective-permute-start.4 = (bf16[128,768]{1,0:T(8,128)(2,1)S(1)}, bf16[128,768]{1,0:T(8,128)(2,1)S(1)}, u32[]{:S(2)}, u32[]{:S(2)}) collective-permute-start(bf16[128,768]{1,0:T(8,128)(2,1)S(1)} %collective-permute-done.2.refs_2_.refs_0_.refs_13_), channel_id=1, source_target_pairs={{0,1},{1,0},{2,3},{3,2},{4,5},{5,4},{6,7},{7,6},{8,9},{9,8},{10,11... | collective-permute-start | bytes 589832 | tf_op jit(solution)/shard_map/ppermute | solution.py:1036
  32.2 12.3 %copy-start.19 = (bf16[128,768]{1,0:T(8,128)(2,1)}, bf16[128,768]{1,0:T(8,128)(2,1)S(1)}, u32[]{:S(2)}) copy-start(bf16[128,768]{1,0:T(8,128)(2,1)S(1)} %collective-permute-done.11.refs_3_) | copy-start | bytes 589828
  32.2 11.7 %collective-permute-start.15 = (bf16[128,768]{1,0:T(8,128)(2,1)S(1)}, bf16[128,768]{1,0:T(8,128)(2,1)S(1)}, u32[]{:S(2)}, u32[]{:S(2)}) collective-permute-start(bf16[128,768]{1,0:T(8,128)(2,1)S(1)} %collective-permute-done.11.refs_3_), channel_id=1, source_target_pairs={{0,8},{1,9},{2,10},{3,11},{4,12},{5,13},{6,14},{7,15},{8,0},{9,1},... | collective-permute-start | bytes 589832 | tf_op jit(solution)/shard_map/ppermute | solution.py:1036
  34.7 9.8 %copy-start.20 = (bf16[128,768]{1,0:T(8,128)(2,1)}, bf16[128,768]{1,0:T(8,128)(2,1)S(1)}, u32[]{:S(2)}) copy-start(bf16[128,768]{1,0:T(8,128)(2,1)S(1)} %collective-permute-done.10.refs_2_) | copy-start | bytes 589828
  34.7 9.4 %collective-permute-start.14 = (bf16[128,768]{1,0:T(8,128)(2,1)S(1)}, bf16[128,768]{1,0:T(8,128)(2,1)S(1)}, u32[]{:S(2)}, u32[]{:S(2)}) collective-permute-start(bf16[128,768]{1,0:T(8,128)(2,1)S(1)} %collective-permute-done.10.refs_2_), channel_id=1, source_target_pairs={{0,8},{1,9},{2,10},{3,11},{4,12},{5,13},{6,14},{7,15},{8,0},{9,1},... | collective-permute-start | bytes 589832 | tf_op jit(solution)/shard_map/ppermute | solution.py:1036
  37.1 7.4 %copy-start.21 = (bf16[128,768]{1,0:T(8,128)(2,1)}, bf16[128,768]{1,0:T(8,128)(2,1)S(1)}, u32[]{:S(2)}) copy-start(bf16[128,768]{1,0:T(8,128)(2,1)S(1)} %collective-permute-done.12.refs_4_) | copy-start | bytes 589828
  37.1 40.6 %collective-permute-start.21 = (bf16[128,768]{1,0:T(8,128)(2,1)S(1)}, bf16[128,768]{1,0:T(8,128)(2,1)}, u32[]{:S(2)}, u32[]{:S(2)}) collective-permute-start(bf16[128,768]{1,0:T(8,128)(2,1)S(1)} %get-tuple-element.113), channel_id=1, source_target_pairs={{0,2},{1,3},{2,0},{3,1},{4,10},{5,11},{6,8},{7,9},{8,6},{9,7},{10,... | collective-permute-start | bytes 589832 | tf_op jit(solution)/shard_map/ppermute | solution.py:1036
  39.8 18.3 %copy-start.24 = (bf16[128,768]{1,0:T(8,128)(2,1)}, bf16[128,768]{1,0:T(8,128)(2,1)S(1)}, u32[]{:S(2)}) copy-start(bf16[128,768]{1,0:T(8,128)(2,1)S(1)} %collective-permute-done.5.refs_5_.refs_3_) | copy-start | bytes 589828
  39.8 18.3 %collective-permute-start.7 = (bf16[128,768]{1,0:T(8,128)(2,1)S(1)}, bf16[128,768]{1,0:T(8,128)(2,1)S(1)}, u32[]{:S(2)}, u32[]{:S(2)}) collective-permute-start(bf16[128,768]{1,0:T(8,128)(2,1)S(1)} %collective-permute-done.3.refs_3_.refs_1_.refs_14_), channel_id=1, source_target_pairs={{0,8},{1,9},{2,10},{3,11},{4,12},{5,13},{6,14},{7,15},{8,0},{9,1},... | collective-permute-start | bytes 589832 | tf_op jit(solution)/shard_map/ppermute | solution.py:1036
  43.1 14.9 %copy-start.25 = (bf16[128,768]{1,0:T(8,128)(2,1)}, bf16[128,768]{1,0:T(8,128)(2,1)S(1)}, u32[]{:S(2)}) copy-start(bf16[128,768]{1,0:T(8,128)(2,1)S(1)} %collective-permute-done.4.refs_4_.refs_2_) | copy-start | bytes 589828
  43.1 18.8 %collective-permute-start.6 = (bf16[128,768]{1,0:T(8,128)(2,1)S(1)}, bf16[128,768]{1,0:T(8,128)(2,1)S(1)}, u32[]{:S(2)}, u32[]{:S(2)}) collective-permute-start(bf16[128,768]{1,0:T(8,128)(2,1)S(1)} %collective-permute-done.2.refs_2_.refs_0_.refs_13_), channel_id=1, source_target_pairs={{0,8},{1,9},{2,10},{3,11},{4,12},{5,13},{6,14},{7,15},{8,0},{9,1},... | collective-permute-start | bytes 589832 | tf_op jit(solution)/shard_map/ppermute | solution.py:1036
  44.0 0.7 copy-start.22
  44.0 18.0 %collective-permute-start.9 = (bf16[128,768]{1,0:T(8,128)(2,1)S(1)}, bf16[128,768]{1,0:T(8,128)(2,1)S(1)}, u32[]{:S(2)}, u32[]{:S(2)}) collective-permute-start(bf16[128,768]{1,0:T(8,128)(2,1)S(1)} %collective-permute-done.5.refs_5_.refs_3_), channel_id=1, source_target_pairs={{0,8},{1,9},{2,10},{3,11},{4,12},{5,13},{6,14},{7,15},{8,0},{9,1},... | collective-permute-start | bytes 589832 | tf_op jit(solution)/shard_map/ppermute | solution.py:1036
  44.1 0.7 copy-start.23
  44.1 17.9 %collective-permute-start.8 = (bf16[128,768]{1,0:T(8,128)(2,1)S(1)}, bf16[128,768]{1,0:T(8,128)(2,1)S(1)}, u32[]{:S(2)}, u32[]{:S(2)}) collective-permute-start(bf16[128,768]{1,0:T(8,128)(2,1)S(1)} %collective-permute-done.4.refs_4_.refs_2_), channel_id=1, source_target_pairs={{0,8},{1,9},{2,10},{3,11},{4,12},{5,13},{6,14},{7,15},{8,0},{9,1},... | collective-permute-start | bytes 589832 | tf_op jit(solution)/shard_map/ppermute | solution.py:1036
  58.1 4.0 %copy-start.26 = (bf16[128,768]{1,0:T(8,128)(2,1)}, bf16[128,768]{1,0:T(8,128)(2,1)S(1)}, u32[]{:S(2)}) copy-start(bf16[128,768]{1,0:T(8,128)(2,1)S(1)} %collective-permute-done.7.refs_7_.refs_5_) | copy-start | bytes 589828
  58.1 19.7 %collective-permute-start.20 = (bf16[128,768]{1,0:T(8,128)(2,1)S(1)}, bf16[128,768]{1,0:T(8,128)(2,1)S(1)}, u32[]{:S(2)}, u32[]{:S(2)}) collective-permute-start(bf16[128,768]{1,0:T(8,128)(2,1)S(1)} %get-tuple-element.114), channel_id=1, source_target_pairs={{0,0},{1,1},{2,2},{3,3},{4,8},{5,9},{6,10},{7,11},{8,4},{9,5},{10,... | collective-permute-start | bytes 589832 | tf_op jit(solution)/shard_map/ppermute | solution.py:1036
  62.0 0.7 copy-start.27
  62.0 0.8 copy-start.28
  62.0 0.9 copy-start.29
  77.8 0.7 copy-start.30
  128.6 26.8 %copy-start.16 = (f32[8,768]{1,0:T(8,128)S(1)}, f32[8,768]{1,0:T(8,128)}, u32[]{:S(2)}) copy-start(f32[8,768]{1,0:T(8,128)} %get-tuple-element.95) | copy-start | bytes 73732
  128.6 26.8 %copy-start.14 = (f32[16,768]{1,0:T(8,128)S(1)}, f32[16,768]{1,0:T(8,128)}, u32[]{:S(2)}) copy-start(f32[16,768]{1,0:T(8,128)} %get-tuple-element.92) | copy-start | bytes 147460
  157.3 131.7 %copy-start.1 = (bf16[256,768]{1,0:T(8,128)(2,1)S(1)}, bf16[256,768]{1,0:T(8,128)(2,1)}, u32[]{:S(2)}) copy-start(bf16[256,768]{1,0:T(8,128)(2,1)} %get-tuple-element.65) | copy-start | bytes 1179652
  286.6 9.3 %copy-start.12 = (bf16[2,48,192]{2,1,0:T(8,128)(2,1)S(1)}, bf16[2,48,192]{2,1,0:T(8,128)(2,1)}, u32[]{:S(2)}) copy-start(bf16[2,48,192]{2,1,0:T(8,128)(2,1)} %get-tuple-element.101) | copy-start | bytes 110596
  286.6 9.3 %copy-start.13 = (bf16[2,48,192]{2,1,0:T(8,128)(2,1)S(1)}, bf16[2,48,192]{2,1,0:T(8,128)(2,1)}, u32[]{:S(2)}) copy-start(bf16[2,48,192]{2,1,0:T(8,128)(2,1)} %get-tuple-element.103) | copy-start | bytes 110596
  286.6 10.8 %copy-start.10 = (bf16[2,144,192]{2,1,0:T(8,128)(2,1)S(1)}, bf16[2,144,192]{2,1,0:T(8,128)(2,1)}, u32[]{:S(2)}) copy-start(bf16[2,144,192]{2,1,0:T(8,128)(2,1)} %get-tuple-element.99) | copy-start | bytes 331780
  289.0 9.3 %copy-start.9 = (bf16[2,48,768]{2,1,0:T(8,128)(2,1)S(1)}, bf16[2,48,768]{2,1,0:T(8,128)(2,1)}, u32[]{:S(2)}) copy-start(bf16[2,48,768]{2,1,0:T(8,128)(2,1)} %get-tuple-element.105) | copy-start | bytes 442372
  289.0 12.2 %collective-permute-start.22 = (bf16[128,768]{1,0:T(8,128)(2,1)S(1)}, bf16[128,768]{1,0:T(8,128)(2,1)S(1)}, u32[]{:S(2)}, u32[]{:S(2)}) collective-permute-start(bf16[128,768]{1,0:T(8,128)(2,1)S(1)} %get-tuple-element.111), channel_id=1, source_target_pairs={{0,0},{1,1},{2,2},{3,3},{4,8},{5,9},{6,10},{7,11},{8,4},{9,5},{10,... | collective-permute-start | bytes 589832 | tf_op jit(solution)/shard_map/ppermute | solution.py:1036
  291.1 10.1 %collective-permute-start.23 = (bf16[128,768]{1,0:T(8,128)(2,1)S(1)}, bf16[128,768]{1,0:T(8,128)(2,1)S(1)}, u32[]{:S(2)}, u32[]{:S(2)}) collective-permute-start(bf16[128,768]{1,0:T(8,128)(2,1)S(1)} %get-tuple-element.112), channel_id=1, source_target_pairs={{0,2},{1,3},{2,0},{3,1},{4,10},{5,11},{6,8},{7,9},{8,6},{9,7},{10,... | collective-permute-start | bytes 589832 | tf_op jit(solution)/shard_map/ppermute | solution.py:1036
  292.6 6.5 %copy-start.8 = (bf16[2,192,192]{2,1,0:T(8,128)(2,1)S(1)}, bf16[2,192,192]{2,1,0:T(8,128)(2,1)}, u32[]{:S(2)}) copy-start(bf16[2,192,192]{2,1,0:T(8,128)(2,1)} %get-tuple-element.104) | copy-start | bytes 442372
  295.9 4.7 %copy-start.11 = (f32[32,768]{1,0:T(8,128)S(1)}, f32[32,768]{1,0:T(8,128)}, u32[]{:S(2)}) copy-start(f32[32,768]{1,0:T(8,128)} %get-tuple-element.106) | copy-start | bytes 294916
  299.0 3.0 copy-start.3
  299.1 3.7 %copy-start.2 = (bf16[2,128,768]{2,1,0:T(8,128)(2,1)S(1)}, bf16[2,128,768]{2,1,0:T(8,128)(2,1)}, u32[]{:S(2)}) copy-start(bf16[2,128,768]{2,1,0:T(8,128)(2,1)} %get-tuple-element.155) | copy-start | bytes 1179652

commit v3 on v2

v3 whole, which is shorter than its diff:
```python
import functools
from typing import NamedTuple

import jax
import jax.numpy as jnp
from jax import lax
from jax.experimental import pallas as pl
from jax.experimental.pallas import tpu as pltpu
from jax.sharding import PartitionSpec as P

D = 768
H = 12
HD = 64
FF = 3072
PAGE = 128
DOCS = 2
ROWS = DOCS * PAGE
QUAD = 256
QUADS = D // QUAD
PAIR = 128
IMAGE = 112
EXTRA = 16
EPSILON = 1e-05
NEGATIVE = -1e30
HIGHEST = lax.Precision.HIGHEST
BF16 = jnp.bfloat16
F32 = jnp.float32
VMEM_LIMIT = 60 * 1024 * 1024


def product(left, right):
    return jnp.dot(left, right, preferred_element_type=F32)


def against(left, right, precision=None):
    return lax.dot_general(
        left, right, (((1,), (1,)), ((), ())), preferred_element_type=F32, precision=precision
    )


def transposed(left, right, precision=None):
    return lax.dot_general(
        left, right, (((0,), (0,)), ((), ())), preferred_element_type=F32, precision=precision
    )


def standardize(values):
    centred = values - jnp.mean(values, axis=-1, keepdims=True)
    inverse = lax.rsqrt(jnp.mean(centred * centred, axis=-1, keepdims=True) + EPSILON)
    return centred * inverse, inverse


def norm_back(upstream, scaled, inverse, gains):
    weighted = upstream * gains
    return inverse * (
        weighted
        - jnp.mean(weighted, axis=-1, keepdims=True)
        - scaled * jnp.mean(weighted * scaled, axis=-1, keepdims=True)
    )


def column_sum(values):
    return jnp.sum(values, axis=0, keepdims=True)


def normalize_page(page, index, gain, shift, normed):
    rows = page.shape[0]
    scaled, _ = standardize(page[...].astype(F32))
    normed[index * rows : (index + 1) * rows, :] = (scaled * gain + shift).astype(BF16)


def normalize_pages(pages, gain, shift, normed):
    for index in range(pages.shape[0]):
        normalize_page(pages.at[index], index, gain, shift, normed)


def lane_index(rows):
    return lax.broadcasted_iota(jnp.int32, (rows, PAIR), 1)


def side_masks(rows):
    lanes = lane_index(rows)
    return [(lanes < HD).astype(BF16), (lanes >= HD).astype(BF16)]


def attend_forward(q_ref, k_ref, v_ref, closed_ref, out_ref, lse_ref):
    lanes = lane_index(ROWS)
    masks = side_masks(ROWS)
    first_lane = (lanes == 0).astype(BF16)
    stats = jnp.zeros((ROWS, PAIR), F32)
    for pair in range(QUAD // PAIR):
        cols = slice(pair * PAIR, (pair + 1) * PAIR)
        keys = jnp.concatenate([k_ref[:, cols], closed_ref[...]], axis=1)
        values = v_ref[:, cols]
        queries = q_ref[:, cols]
        results = []
        for side in range(2):
            query = jnp.concatenate([queries * masks[side], first_lane], axis=1)
            scores = against(query, keys)
            top = jnp.max(scores, axis=1, keepdims=True)
            weights = jnp.exp(scores - top)
            total = jnp.sum(weights, axis=1, keepdims=True)
            results.append(product(weights.astype(BF16), values) / total)
            stats = jnp.where(lanes == pair * 2 + side, top + jnp.log(total), stats)
        out_ref[:, cols] = jnp.where(lanes < HD, results[0], results[1])
    lse_ref[...] = jnp.transpose(stats)[:8, :]


def attend_backward(q_ref, k_ref, v_ref, do_ref, lse_ref, delta_ref, closed_ref, dq_ref, dkv_ref, hook):
    lanes = lane_index(ROWS)
    masks = side_masks(ROWS)
    first_lane = (lanes == 0).astype(BF16)
    for pair in range(QUAD // PAIR):
        cols = slice(pair * PAIR, (pair + 1) * PAIR)
        key_part = k_ref[:, cols]
        keys = jnp.concatenate([key_part, closed_ref[...]], axis=1)
        values = v_ref[:, cols]
        dq_parts = []
        dk = None
        dv = None
        for side in range(2):
            row = pair * 2 + side
            query = q_ref[:, cols] * masks[side]
            grad_out = do_ref[:, cols] * masks[side]
            scores = against(keys, jnp.concatenate([query, first_lane], axis=1))
            weights = jnp.exp(scores - lse_ref[row : row + 1, :])
            grad_weights = against(values, grad_out)
            grad_scores = (weights * (grad_weights - delta_ref[row : row + 1, :])).astype(BF16)
            dv_part = product(weights.astype(BF16), grad_out)
            dk_part = product(grad_scores, query)
            dv = dv_part if dv is None else dv + dv_part
            dk = dk_part if dk is None else dk + dk_part
            dq_parts.append(transposed(grad_scores, key_part))
        dq_ref[:, cols] = (jnp.where(lanes < HD, dq_parts[0], dq_parts[1]) * HD ** (-0.5)).astype(
            BF16
        )
        dkv_ref[:, cols] = dk.astype(BF16)
        dkv_ref[:, QUAD + pair * PAIR : QUAD + (pair + 1) * PAIR] = dv.astype(BF16)
        if pair == 0:
            hook()


def head_sums(values):
    sums = []
    lanes = lane_index(values.shape[0])
    for pair in range(H // 2):
        part = values[:, pair * PAIR : (pair + 1) * PAIR]
        sums.append(jnp.sum(jnp.where(lanes < HD, part, 0.0), axis=1, keepdims=True))
        sums.append(jnp.sum(jnp.where(lanes >= HD, part, 0.0), axis=1, keepdims=True))
    return sums


def head_rows(sums):
    lanes = lane_index(ROWS)
    stats = jnp.zeros((ROWS, PAIR), F32)
    for head, value in enumerate(sums):
        stats = jnp.where(lanes == (head // 4) * 8 + head % 4, value, stats)
    return jnp.transpose(stats)[: 8 * QUADS, :]


def spread_heads(gates):
    lanes = lane_index(gates.shape[0])
    parts = []
    for pair in range(H // 2):
        parts.append(
            jnp.where(lanes < HD, gates[:, 2 * pair : 2 * pair + 1], gates[:, 2 * pair + 1 : 2 * pair + 2])
        )
    return jnp.concatenate(parts, axis=1)


def store_tiles(out_ref, rows, value):
    cuts = out_ref.shape[0]
    lanes = out_ref.shape[2]
    for cut in range(cuts):
        out_ref[cut, rows, :] = value[:, cut * lanes : (cut + 1) * lanes].astype(BF16)


class Gather:
    def __init__(self, places, names, packed, landed, waits):
        self.places = places
        self.names = names
        self.packed = packed
        self.landed = landed
        self.sends, self.receives = waits

    @staticmethod
    def waits(names):
        count = DOCS << len(names)
        return [pltpu.SemaphoreType.DMA((count,))] * 2

    def swap(self, turn):
        doc = self.places.turn if turn == 0 else 1 - self.places.turn
        return remote(
            self.packed.at[doc], self.landed.at[turn], self.sends.at[turn], self.receives.at[turn],
            self.places.swap(turn),
        )

    def start(self):
        stays = self.places.swap_stays()
        pl.when(jnp.logical_not(stays))(lambda: self.swap(0).start())
        self.swap(1).start()

        @pl.when(stays)
        def _():
            self.landed[0] = self.packed[self.places.turn]

    def copy(self, block, turn):
        stage = block.bit_length() - 1
        source = (block - (1 << stage)) * DOCS + turn
        at = block * DOCS + turn
        return remote(
            self.landed.at[source], self.landed.at[at], self.sends.at[at], self.receives.at[at],
            self.places.flip(self.names[stage]),
        )

    def arrive(self, block, turn):
        if block > 0:
            self.copy(block, turn).wait_recv()
        elif turn > 0:
            self.swap(turn).wait_recv()
        else:
            stays = self.places.swap_stays()
            pl.when(jnp.logical_not(stays))(lambda: self.swap(0).wait_recv())
        for stage in range(block.bit_length(), len(self.names)):
            self.copy(block + (1 << stage), turn).start()

    def end(self):
        stays = self.places.swap_stays()
        pl.when(jnp.logical_not(stays))(lambda: self.swap(0).wait_send())
        self.swap(1).wait_send()
        for block in range(1, 1 << len(self.names)):
            for turn in range(DOCS):
                self.copy(block, turn).wait_send()


def closed_rows(is_open):
    row = jnp.where(is_open, 0.0, NEGATIVE)
    wide = jnp.concatenate([row, jnp.zeros((1, D - PAGE), F32)], axis=1)
    return jnp.broadcast_to(wide, (EXTRA, D)).astype(BF16)


def closed_column(rows):
    row = rows[0:1, 0:PAGE].astype(F32)
    turned = jnp.transpose(jnp.broadcast_to(row, (PAGE, PAGE)))
    return jnp.where(lane_index(PAGE) == 0, turned, 0.0).astype(BF16)


def self_forward_kernel(
    wide, blk,
    regions, doc_pages, text_in, image_in, cot_in, mask, gain, shift, wq, wk, wv,
    out, lse, q_out, k_out, v_out, text_out, image_out, cot_out, text_closed, image_closed,
    normed, text_packed, image_packed, text_landed, image_landed, cot_landed,
    text_sends, text_receives, image_sends, image_receives, cot_sends, cot_receives, local,
):
    step = pl.program_id(0)
    places = Places(wide, blk)
    groups = group_bits(blk)
    blocks = 1 << len(groups)
    text = Gather(places, groups, text_packed, text_landed, (text_sends, text_receives))
    image = Gather(places, groups, image_packed, image_landed, (image_sends, image_receives))
    cot = Gather(places, [], cot_in, cot_landed, (cot_sends, cot_receives))
    outward = [
        pltpu.make_async_copy(text_landed.at[:, pl.ds(0, PAGE)], text_out, local.at[0]),
        pltpu.make_async_copy(image_landed.at[:, pl.ds(0, IMAGE)], image_out, local.at[1]),
        pltpu.make_async_copy(cot_landed, cot_out, local.at[2]),
    ]

    @pl.when(step == 0)
    def _():
        offsets = lax.broadcasted_iota(jnp.int32, (1, PAGE), 1)
        for doc in range(DOCS):
            text_packed[doc, 0:PAGE, :] = text_in[doc]
            living = places.b < doc_pages[doc]
            is_open = ((mask[doc : doc + 1, :] > 0) | (offsets == 0)) & living
            text_packed[doc, PAGE : PAGE + EXTRA, :] = closed_rows(is_open)
        greet(places, groups, True)
        text.start()
        for doc in range(DOCS):
            image_packed[doc, 0:IMAGE, :] = image_in[doc, 0:IMAGE, :]
            living = places.b < doc_pages[doc]
            is_open = (offsets < regions[doc, 0]) & living
            image_packed[doc, IMAGE : IMAGE + EXTRA, :] = closed_rows(is_open)
        text.arrive(0, 0)
        text.arrive(0, 1)
        image.start()

        def take(block, turn):
            index = block * DOCS + turn
            page = text_landed.at[index, pl.ds(0, PAGE)]
            normalize_page(page, index, gain[0:1, :], shift[0:1, :], normed)
            text_closed[index * PAGE : (index + 1) * PAGE, :] = closed_column(
                text_landed[index, PAGE : PAGE + EXTRA, :]
            )

        for turn in range(DOCS):
            take(0, turn)
        for block in range(1, blocks):
            for turn in range(DOCS):
                text.arrive(block, turn)
            if block == 1:
                image.arrive(0, 0)
                image.arrive(0, 1)
                cot.start()
            for turn in range(DOCS):
                take(block, turn)

    @pl.when(step == 1)
    def _():
        outward[0].start()
        for block in range(1, blocks // 2):
            for turn in range(DOCS):
                image.arrive(block, turn)

    q_out[...] = (product(normed[0:ROWS, :], wq[...]).astype(BF16) * HD ** (-0.5)).astype(BF16)
    k_out[...] = product(normed[...], wk[...]).astype(BF16)
    v_out[...] = product(normed[...], wv[...]).astype(BF16)
    attend_forward(q_out, k_out, v_out, text_closed, out, lse)

    @pl.when(step == QUADS - 1)
    def _():
        for turn in range(DOCS):
            cot.arrive(0, turn)
        outward[2].start()
        for block in range(max(1, blocks // 2), blocks):
            for turn in range(DOCS):
                image.arrive(block, turn)
        outward[1].start()
        for index in range(blocks * DOCS):
            column = closed_column(image_landed[index, IMAGE : IMAGE + EXTRA, :])
            image_closed[index * IMAGE : (index + 1) * IMAGE, :] = column[0:IMAGE, :]
        for stream in (text, image, cot):
            stream.end()
        for copy in outward:
            copy.wait()


def cross_forward_kernel(
    text, pages, self_out, w_self, w_gate, gain, shift, closed, wq, wk, wv,
    hidden, gate, out, lse, q_out, k_out, v_out,
    normed, cross, gates,
):
    @pl.when(pl.program_id(0) == 0)
    def _():
        normalize_pages(pages, gain[2:3, :], shift[2:3, :], normed)
        branch = product(self_out[...].astype(BF16), w_self[...])
        for index in range(DOCS):
            rows = slice(index * PAGE, (index + 1) * PAGE)
            hidden[rows, :] = text[index].astype(F32) + branch[rows, :]
        scaled, _ = standardize(hidden[...])
        cross[...] = (scaled * gain[1:2, :] + shift[1:2, :]).astype(BF16)
        gates[...] = jnp.zeros_like(gates)
        gates[0:H, :] = w_gate[...]
        gate[...] = jax.nn.sigmoid(against(cross[...], gates[...]))

    q_out[...] = (product(cross[...], wq[...]).astype(BF16) * HD ** (-0.5)).astype(BF16)
    k_out[...] = product(normed[...], wk[...]).astype(BF16)
    v_out[...] = product(normed[...], wv[...]).astype(BF16)
    attend_forward(q_out, k_out, v_out, closed, out, lse)


def expand_part(wide, blk, step):
    few = (slice(None),) * (wide.bit_length() - 2)
    rest = (slice(None),) * (blk.bit_length() - 3)
    return few + (step // 2, step % 2) + rest, (slice(None), slice(None))


def reduce_part(wide, blk, step):
    cuts = wide.bit_length() - 2
    rest = (slice(None),) * (blk.bit_length() - 1)
    if cuts >= 2:
        lead = (step // 2, step % 2) + (slice(None),) * (cuts - 2) + rest
        return lead, (slice(None), slice(None))
    lanes = pl.ds(pl.multiple_of((step % 2) * D, D), D)
    return (step // 2,) + rest, (slice(None), lanes)


def put_expand(out, value, step, wide, blk):
    cuts, bits = wide.bit_length() - 2, blk.bit_length() - 1
    rows, lanes = out.shape[-2:]
    for cut in range(1 << cuts):
        for part in range(D // rows):
            at = bits_of(cut, cuts) + (step // 2, step % 2) + bits_of(part, bits - 1)
            out[at] = value[part * rows : (part + 1) * rows, cut * lanes : (cut + 1) * lanes]


def put_reduce(out, value, step, wide, blk):
    cuts, bits = wide.bit_length() - 2, blk.bit_length() - 1
    rows, lanes = out.shape[-2:]
    for part in range(D // rows):
        place = bits_of(part, bits + 1)
        piece = value[part * rows : (part + 1) * rows, :]
        if cuts >= 2:
            for cut in range(D // lanes):
                at = (step // 2, step % 2) + bits_of(cut, cuts - 2) + place
                out[at] = piece[:, cut * lanes : (cut + 1) * lanes]
        else:
            out[(step // 2,) + place + (slice(None), pl.ds(pl.multiple_of((step % 2) * D, D), D))] = piece


def forward_back_kernel(
    steps, wide, blk,
    hidden, raw, gate, cots, w_out, gain, shift, w_expand, b_expand, w_reduce, b_reduce,
    joined, expand_out, reduce_out, d_out, grad_mixed, grad_raw, delta, grad_logit, small,
    gated, mixed, final, upstream, joined_sum, back_sum,
    expand_all, reduce_all, expand_got, reduce_got, sends, receives, local,
):
    step = pl.program_id(0)
    places = Places(wide, blk)
    core = ("w", 0)

    def copies(at):
        found = []
        for index, (part, grad, got) in enumerate(
            ((expand_part, expand_all, expand_got), (reduce_part, reduce_all, reduce_got))
        ):
            lead, tail = part(wide, blk, at)
            found.append(
                remote(
                    grad.at[lead + (1 - places.bit(core),) + tail],
                    got.at[lead + tail],
                    sends.at[index, at],
                    receives.at[index, at],
                    places.flip(core),
                )
            )
        return found

    @pl.when(step == 0)
    def _():
        greet(places, [core], False)
        upstream[0:PAGE, :] = cots[0]
        upstream[PAGE:ROWS, :] = cots[1]
        small[...] = jnp.zeros_like(small)
        gated[...] = (spread_heads(gate[...]) * raw[...]).astype(BF16)
        rows = hidden[...] + product(gated[...], w_out[...])
        mixed[...] = rows
        scaled, _ = standardize(rows)
        final[...] = (scaled * gain[3:4, :] + shift[3:4, :]).astype(BF16)
        joined_sum[...] = rows + b_reduce[...]
        back_sum[...] = jnp.zeros_like(back_sum)

    inner = product(final[...], w_expand[...]) + b_expand[...]
    squared = inner * inner
    root = (2.0 / jnp.pi) ** 0.5
    curve = jnp.tanh(root * inner * (1.0 + 0.044715 * squared))
    half = 0.5 * (1.0 + curve)
    active = (inner * half).astype(BF16)
    slope = half + 0.5 * inner * (1.0 - curve * curve) * (root * (1.0 + 3.0 * 0.044715 * squared))
    joined_sum[...] += product(active, w_reduce[...])
    grad_active = against(upstream[...], w_reduce[...]).astype(BF16)
    grad_inner = (grad_active.astype(F32) * slope).astype(BF16)
    small[pl.ds(8 + step, 1), :] = column_sum(grad_inner.astype(F32))
    back_sum[...] += against(grad_inner, w_expand[...])
    put_expand(expand_all, transposed(grad_inner, final[...]).astype(BF16), step, wide, blk)
    put_reduce(reduce_all, transposed(upstream[...], active).astype(BF16), step, wide, blk)
    for copy in copies(step):
        copy.start()

    @pl.when(step == steps - 1)
    def _():
        total = joined_sum[...].astype(BF16)
        joined[0] = total[:PAGE]
        joined[1] = total[PAGE:]
        scaled, inverse = standardize(mixed[...])
        back = back_sum[...]
        cotangent = upstream[...].astype(F32)
        grad = cotangent + norm_back(back, scaled, inverse, gain[3:4, :])
        grad_mixed[...] = grad
        branch = grad.astype(BF16)
        store_tiles(d_out, slice(None), transposed(branch, gated[...]))
        grad_gated = against(branch, w_out[...]).astype(BF16).astype(F32)
        gates = gate[...]
        lanes = lane_index(ROWS)
        logit = jnp.zeros((ROWS, PAIR), F32)
        for head, value in enumerate(head_sums(grad_gated * raw[...])):
            logit = jnp.where(lanes == head, value, logit)
        grad_logit[...] = logit * gates * (1.0 - gates)
        rounded = (spread_heads(gates) * grad_gated).astype(BF16)
        grad_raw[...] = rounded
        delta[...] = head_rows(head_sums(rounded.astype(F32) * raw[...]))
        small[0:1, :] = column_sum(cotangent)
        small[1:2, :] = column_sum(back * scaled)
        small[2:3, :] = column_sum(back)
        for at in range(steps):
            for copy in copies(at):
                copy.wait_recv()
        moves = []
        for index, (grad, got, out) in enumerate(
            ((expand_all, expand_got, expand_out), (reduce_all, reduce_got, reduce_out))
        ):
            lead = len(got.shape) - 2
            add_blocks(got, grad.at[(slice(None),) * lead + (places.bit(core),)])
            moves.append(pltpu.make_async_copy(got, out, local.at[index]))
            moves[-1].start()
        for at in range(steps):
            for copy in copies(at):
                copy.wait_send()
        for move in moves:
            move.wait()


def spread_back(normed, dkv, wk, wv, dx, dw_k, dw_v, k_rows, v_rows):
    store_tiles(dw_k, k_rows, transposed(dkv[:, :QUAD], normed[...]))
    store_tiles(dw_v, v_rows, transposed(dkv[:, QUAD:], normed[...]))
    weights = jnp.concatenate([wk[...], wv[...]], axis=1)

    size = dx.shape[0] // 4

    def chunk(index, carry):
        rows = pl.ds(pl.multiple_of(index * size, 16), size)
        dx[rows, :] += against(dkv[rows, :], weights)
        return carry

    lax.fori_loop(0, 4, chunk, 0)


def finish_pages(pages, dx, keep, send):
    gain_sum = jnp.zeros((1, D), F32)
    shift_sum = jnp.zeros((1, D), F32)
    count, size, _ = pages.shape
    half = count // 2
    for index in range(count):
        scaled, _ = standardize(pages[index].astype(F32))
        part = dx[index * size : (index + 1) * size, :]
        gain_sum += column_sum(part * scaled)
        shift_sum += column_sum(part)
        target = keep if index < half else send
        place = index % half
        target[place * size : (place + 1) * size, :] = part.astype(BF16)
    return gain_sum, shift_sum


END = 99


def moves_of(plan, jobs):
    done = [-1] * len(jobs)
    moves = {}
    for point in sorted(plan):
        moves[point] = []
        for index in plan[point]:
            moves[point].append((index, done[index]))
            done[index] += 1
    moves[END] = [
        (index, stage)
        for stage in range(-1, max(len(job.order) for job in jobs))
        for index, job in enumerate(jobs)
        if done[index] <= stage < len(job.order)
    ]
    return moves


def run_moves(moves, point, scatters, outs):
    for index, stage in moves.get(point, ()):
        scatter = scatters[index]
        if stage < 0:
            scatter.start()
        else:
            scatter.add(stage)
        if stage + 1 == scatter.stages and not scatter.job.ends:
            scatter.store(outs[index]).start()


def finish_moves(moves, scatters, outs):
    run_moves(moves, END, scatters, outs)
    for scatter, out in zip(scatters, outs):
        scatter.end(out)


def cross_back_kernel(wide, blk, jobs, plan, *refs):
    refs = iter(refs)
    (
        pages, gain, shift, closed, q_in, k_in, v_in, do_in, lse, delta, wk, wv,
        w_query, w_gate, w_self, hidden, self_out, grad_mixed, grad_logit, joined,
    ) = (next(refs) for _ in range(20))
    sources = [next(refs) for _ in jobs]
    (
        keep, send, dw_pairs, dw_query, dw_self, dw_gate, grad_hidden, self_do, self_delta, small,
        joined_out,
    ) = (next(refs) for _ in range(11))
    outs = [next(refs) for _ in jobs]
    normed, dkv, dx, dq, gates = (next(refs) for _ in range(5))
    step = pl.program_id(0)
    moves = moves_of(plan, jobs)
    places = Places(wide, blk)
    scatters = [Scatter(places, job, source, refs) for job, source in zip(jobs, sources)]
    home = Home(places, refs)

    def pump(point):
        run_moves(moves, point, scatters, outs)

    @pl.when(step == 0)
    def _():
        greet(places, bit_names(wide, blk), True)
        pump(0)
        for turn in range(DOCS):
            home.put(turn, joined[turn])
        normalize_pages(pages, gain[2:3, :], shift[2:3, :], normed)
        dx[...] = jnp.zeros_like(dx)

    def middle():
        for at in range(QUADS):
            pl.when(step == at)(functools.partial(pump, 2 * at + 1))

    cols = pl.ds(pl.multiple_of(step * QUAD, QUAD), QUAD)
    attend_backward(
        q_in, k_in, v_in, do_in, lse, delta, closed, dq.at[:, cols], dkv, middle
    )
    spread_back(
        normed, dkv, wk, wv, dx, dw_pairs, dw_pairs,
        cols, pl.ds(pl.multiple_of(D + step * QUAD, QUAD), QUAD),
    )
    for at in range(QUADS):
        pl.when(step == at)(functools.partial(pump, 2 * at + 2))

    @pl.when(step == QUADS - 1)
    def _():
        image_gain, image_shift = finish_pages(pages, dx, keep, send)
        scaled, inverse = standardize(hidden[...])
        cross = (scaled * gain[1:2, :] + shift[1:2, :]).astype(BF16)
        grad_query = dq[...]
        store_tiles(dw_query, slice(None), transposed(grad_query, cross))
        dw_gate[...] = transposed(grad_logit[...], cross.astype(F32), HIGHEST)[:16, :]
        gates[...] = jnp.zeros_like(gates)
        gates[0:H, :] = w_gate[...]
        upstream = against(grad_query, w_query[...]) + jnp.dot(
            grad_logit[...], gates[...].astype(F32), precision=HIGHEST
        )
        grad = grad_mixed[...] + norm_back(upstream, scaled, inverse, gain[1:2, :])
        grad_hidden[...] = grad
        branch = grad.astype(BF16)
        store_tiles(dw_self, slice(None), transposed(branch, self_out[...].astype(BF16)))
        grad_result = against(branch, w_self[...]).astype(BF16)
        self_do[...] = grad_result
        self_delta[...] = head_rows(head_sums(grad_result.astype(F32) * self_out[...]))
        small[...] = jnp.concatenate(
            [
                column_sum(upstream * scaled),
                column_sum(upstream),
                image_gain,
                image_shift,
                jnp.zeros((4, D), F32),
            ],
            axis=0,
        )
        home.end(joined_out)
        finish_moves(moves, scatters, outs)


def self_back_kernel(wide, blk, jobs, plan, *refs):
    refs = iter(refs)
    (
        pages, gain, shift, closed, q_in, k_in, v_in, do_in, lse, delta, wq, wk, wv,
        image_keep, image_send, image_own,
    ) = (next(refs) for _ in range(16))
    sources = [next(refs) for _ in jobs]
    keep, send, dw_project, small, image_out = (next(refs) for _ in range(5))
    outs = [next(refs) for _ in jobs]
    normed, dkv, dx, dq = (next(refs) for _ in range(4))
    step = pl.program_id(0)
    moves = moves_of(plan, jobs)
    places = Places(wide, blk)
    groups = group_bits(blk)
    scatters = [Scatter(places, job, source, refs) for job, source in zip(jobs, sources)]
    image = Rows(places, groups, image_keep, image_send, refs)

    def pump(point):
        if point == 1:
            image.add(0)
        if point == 4:
            for stage in range(1, len(groups)):
                image.add(stage)
            image.norm(image_own, gain[2:3, :], None)
        run_moves(moves, point, scatters, outs)

    @pl.when(step == 0)
    def _():
        greet(places, bit_names(wide, blk), True)
        image.start()
        pump(0)
        normalize_pages(pages, gain[0:1, :], shift[0:1, :], normed)
        dx[...] = jnp.zeros_like(dx)

    def middle():
        for at in range(QUADS):
            pl.when(step == at)(functools.partial(pump, 2 * at + 1))

    attend_backward(q_in, k_in, v_in, do_in, lse, delta, closed, dq, dkv, middle)
    spread_back(
        normed, dkv, wk, wv, dx, dw_project, dw_project,
        pl.ds(pl.multiple_of(D + step * QUAD, QUAD), QUAD),
        pl.ds(pl.multiple_of(2 * D + step * QUAD, QUAD), QUAD),
    )
    store_tiles(
        dw_project,
        pl.ds(pl.multiple_of(step * QUAD, QUAD), QUAD),
        transposed(dq[...], normed[0:ROWS, :]),
    )
    dx[0:ROWS, :] += against(dq[...], wq[...])
    for at in range(QUADS - 1):
        pl.when(step == at)(functools.partial(pump, 2 * at + 2))

    @pl.when(step == QUADS - 1)
    def _():
        gain_sum, shift_sum = finish_pages(pages, dx, keep, send)
        small[...] = jnp.concatenate([gain_sum, shift_sum, jnp.zeros((6, D), F32)], axis=0)
        finish_moves(moves, scatters, outs)
        image.end(image_out)


class Places:
    def __init__(self, wide, blk):
        self.wide = wide
        self.blk = blk
        self.part = blk // 4
        self.w = lax.axis_index("wide")
        self.b = lax.axis_index("blk")
        self.quarter = self.b // self.part
        self.turn = self.quarter % 2

    def bit(self, name):
        axis, bit = name
        return ((self.w if axis == "w" else self.b) // (1 << bit)) % 2

    def flip(self, name):
        axis, bit = name
        step = (1 << bit) * (1 - 2 * self.bit(name))
        return (self.w + step, self.b) if axis == "w" else (self.w, self.b + step)

    def swap(self, turn):
        core = self.w % 2
        turned = self.turn if turn == 0 else 1 - self.turn
        return (
            self.w - core + self.quarter // 2,
            (2 * core + turned) * self.part + self.b % self.part,
        )

    def swap_stays(self):
        return self.w % 2 == self.quarter // 2


def bit_names(wide, blk):
    return [("w", bit) for bit in range(wide.bit_length() - 1)] + [
        ("b", bit) for bit in range(blk.bit_length() - 1)
    ]


def group_bits(blk):
    return [("b", bit) for bit in range((blk // 4).bit_length() - 1)] + [("w", 0)]


def tile_bits(wide, blk):
    return (
        [("w", bit) for bit in range(wide.bit_length() - 2, 0, -1)]
        + [("b", bit) for bit in range(blk.bit_length() - 2, -1, -1)]
        + [("w", 0)]
    )


def remote(source, target, send, receive, device):
    return pltpu.make_async_remote_copy(
        src_ref=source,
        dst_ref=target,
        send_sem=send,
        recv_sem=receive,
        device_id=device,
        device_id_type=pl.DeviceIdType.MESH,
    )


def greet(places, names, swaps):
    barrier = pltpu.get_barrier_semaphore()
    for name in names:
        pl.semaphore_signal(
            barrier, inc=1, device_id=places.flip(name), device_id_type=pl.DeviceIdType.MESH
        )
    count = len(names)
    if swaps:
        pl.semaphore_signal(
            barrier, inc=1, device_id=places.swap(1), device_id_type=pl.DeviceIdType.MESH
        )

        @pl.when(jnp.logical_not(places.swap_stays()))
        def _():
            pl.semaphore_signal(
                barrier, inc=1, device_id=places.swap(0), device_id_type=pl.DeviceIdType.MESH
            )

        count = count + 2 - places.swap_stays().astype(jnp.int32)
    pl.semaphore_wait(barrier, count)


class Job(NamedTuple):
    left: tuple
    order: tuple
    start: int
    rows: int
    lanes: int
    ends: bool

    def after(self):
        return tuple(name for name in self.left if name not in self.order)

    def scratch(self):
        count = len(self.left)
        kinds = []
        if self.order:
            kinds.append(pltpu.VMEM((2,) * (count - 1) + (self.rows, self.lanes), BF16))
        for stage in range(len(self.order)):
            kinds.append(pltpu.VMEM((2,) * (count - 1 - stage) + (self.rows, self.lanes), BF16))
        if self.ends:
            kinds.append(pltpu.VMEM((2, self.rows, self.lanes // 2), BF16))
        waits = len(self.order) + int(self.ends)
        return kinds + [pltpu.SemaphoreType.DMA((waits,))] * 2 + [pltpu.SemaphoreType.DMA]

    def result(self):
        if self.ends:
            return shaped((2, self.rows, self.lanes // 2), BF16)
        return shaped((2,) * len(self.after()) + (self.rows, self.lanes), BF16)


def bits_of(index, count):
    return tuple((index // (1 << (count - 1 - place))) % 2 for place in range(count))


def add_blocks(target, source):
    lead = len(target.shape) - 2
    if lead == 0:
        target[...] = target[...] + source[...]
        return

    def block(index, carry):
        at = bits_of(index, lead)
        target[at] = target[at] + source[at]
        return carry

    lax.fori_loop(0, 1 << lead, block, 0)


class Scatter:
    def __init__(self, places, job, source, scratch):
        self.places = places
        self.job = job
        self.source = source
        self.own = next(scratch) if job.order else None
        self.got = [next(scratch) for _ in job.order] or [source]
        self.ends = next(scratch) if job.ends else None
        self.sends, self.receives, self.local = next(scratch), next(scratch), next(scratch)
        self.stages = len(job.order)
        self.axes = []
        left = list(job.left)
        for name in job.order:
            self.axes.append(left.index(name))
            left.remove(name)

    def cut(self, ref, stage, index):
        axis = self.axes[stage]
        at = (slice(None),) * axis + (index,)
        if ref.shape[-2] != self.job.rows:
            at += (slice(None),) * (len(ref.shape) - 3 - axis)
            at += (pl.ds(self.job.start, self.job.rows), slice(None))
        return ref.at[at]

    def copy(self, stage):
        if stage == self.stages:
            source, target, name = self.ends.at[0], self.ends.at[1], ("w", 0)
        else:
            name = self.job.order[stage]
            source = self.source if stage == 0 else self.got[stage - 1]
            source = self.cut(source, stage, 1 - self.places.bit(name))
            target = self.got[stage]
        return remote(
            source, target, self.sends.at[stage], self.receives.at[stage], self.places.flip(name)
        )

    def fetch(self):
        kept = self.cut(self.source, 0, self.places.bit(self.job.order[0]))
        return pltpu.make_async_copy(kept, self.own, self.local)

    def start(self):
        if self.stages == 0:
            self.halve()
        self.copy(0).start()
        if self.stages > 0:
            self.fetch().start()

    def halve(self):
        lanes = self.job.lanes // 2
        piece = self.got[-1][...]
        second = self.places.bit(("w", 0)) == 1
        self.ends[0] = jnp.where(second, piece[:, :lanes], piece[:, lanes:])

    def add(self, stage):
        self.copy(stage).wait_recv()
        if stage == 0:
            self.fetch().wait()
            source = self.own
        else:
            bit = self.places.bit(self.job.order[stage])
            source = self.cut(self.got[stage - 1], stage, bit)
        add_blocks(self.got[stage], source)
        if stage + 1 < self.stages:
            self.copy(stage + 1).start()
        elif self.job.ends:
            self.halve()
            self.copy(stage + 1).start()

    def store(self, out):
        return pltpu.make_async_copy(self.got[-1], out, self.local)

    def end(self, out):
        if self.job.ends:
            self.copy(self.stages).wait_recv()
            lanes = self.job.lanes // 2
            piece = self.got[-1][...]
            other = self.ends[1]
            second = self.places.bit(("w", 0)) == 1
            mine = jnp.where(second, piece[:, lanes:], piece[:, :lanes])
            out[0] = jnp.where(second, other, mine)
            out[1] = jnp.where(second, mine, other)
        else:
            self.store(out).wait()
        for stage in range(self.stages + int(self.job.ends)):
            self.copy(stage).wait_send()


class Home:
    def __init__(self, places, scratch):
        self.places = places
        self.home, self.landed, self.sends, self.receives = (next(scratch) for _ in range(4))

    @staticmethod
    def scratch():
        return [pltpu.VMEM((DOCS, PAGE, D), BF16)] * 2 + [pltpu.SemaphoreType.DMA((DOCS,))] * 2

    def copy(self, turn):
        return remote(
            self.home.at[turn], self.landed.at[self.places.turn], self.sends.at[turn],
            self.receives.at[turn], self.places.swap(turn),
        )

    def go(self, turn, begin):
        def carry():
            if begin:
                self.copy(turn).start()
            else:
                self.copy(turn).wait()

        if turn > 0:
            carry()
            return
        stays = self.places.swap_stays()
        pl.when(jnp.logical_not(stays))(carry)
        if begin:

            @pl.when(stays)
            def _():
                self.landed[self.places.turn] = self.home[turn]

    def put(self, turn, page):
        self.home[turn] = page
        self.go(turn, True)

    def end(self, out):
        for turn in range(DOCS):
            self.go(turn, False)
        out[...] = self.landed[...]


class Rows:
    def __init__(self, places, names, keep, send, scratch):
        self.places = places
        self.size = keep.shape[0] // (DOCS << (len(names) - 1))
        self.names = list(reversed(names))
        self.keep = keep
        self.send = send
        self.sums = next(scratch)
        self.got = [next(scratch) for _ in names]
        self.sends, self.receives = next(scratch), next(scratch)
        self.back = Home(places, scratch)

    @staticmethod
    def scratch(names, rows):
        kinds = [pltpu.VMEM((rows, D), BF16)]
        kinds += [pltpu.VMEM((rows >> stage, D), BF16) for stage in range(len(names))]
        return kinds + [pltpu.SemaphoreType.DMA((len(names),))] * 2 + Home.scratch()

    def copy(self, stage):
        source = self.send if stage == 0 else self.sums
        rows = self.got[stage].shape[0]
        if stage > 0:
            source = source.at[pl.ds(rows, rows)]
        return remote(
            source, self.got[stage], self.sends.at[stage], self.receives.at[stage],
            self.places.flip(self.names[stage]),
        )

    def start(self):
        self.copy(0).start()

    def add(self, stage):
        self.copy(stage).wait_recv()
        if stage > 0:
            self.copy(stage).wait_send()
        source = self.keep if stage == 0 else self.sums
        rows = self.got[stage].shape[0]

        def block(index, carry):
            at = pl.ds(pl.multiple_of(index * self.size, 16), self.size)
            self.sums[at, :] = source[at, :] + self.got[stage][at, :]
            return carry

        lax.fori_loop(0, rows // self.size, block, 0)
        if stage + 1 < len(self.names):
            self.copy(stage + 1).start()

    def norm(self, pages, gain, added):
        for turn in range(DOCS):
            rows = slice(turn * self.size, (turn + 1) * self.size)
            scaled, inverse = standardize(pages[turn].astype(F32))
            grad = norm_back(self.sums[rows, :].astype(F32), scaled, inverse, gain)
            if added is not None:
                grad = grad + added[rows, :]
            if self.size < PAGE:
                rest = jnp.zeros((PAGE - self.size, D), F32)
                grad = jnp.concatenate([grad, rest], axis=0)
            self.back.put(turn, grad.astype(BF16))

    def end(self, out):
        self.back.end(out)
        self.copy(0).wait_send()


class Total:
    def __init__(self, places, names, scratch):
        self.places = places
        self.names = names
        self.mine, self.got, self.sends, self.receives = (next(scratch) for _ in range(4))

    @staticmethod
    def scratch(names, rows):
        count = len(names)
        return [pltpu.VMEM((count, rows, D), F32)] * 2 + [pltpu.SemaphoreType.DMA((count,))] * 2

    def copy(self, stage):
        return remote(
            self.mine.at[stage], self.got.at[stage], self.sends.at[stage], self.receives.at[stage],
            self.places.flip(self.names[stage]),
        )

    def start(self, value):
        self.mine[0] = value
        self.copy(0).start()

    def add(self, stage, out):
        self.copy(stage).wait()
        value = self.mine[stage] + self.got[stage]
        if stage + 1 < len(self.names):
            self.mine[stage + 1] = value
            self.copy(stage + 1).start()
        else:
            out[...] = value


def tail_kernel(wide, blk, jobs, plan, *refs):
    refs = iter(refs)
    sources = [next(refs) for _ in jobs]
    keep, send, texts, grad_hidden, gain = (next(refs) for _ in range(5))
    small = [next(refs) for _ in range(4)]
    text_out, small_out = next(refs), next(refs)
    outs = [next(refs) for _ in jobs]
    moves = moves_of(plan, jobs)
    places = Places(wide, blk)
    names = bit_names(wide, blk)
    groups = group_bits(blk)
    scatters = [Scatter(places, job, source, refs) for job, source in zip(jobs, sources)]
    text = Rows(places, groups, keep, send, refs)
    total = Total(places, names, refs)

    greet(places, names, True)
    text.start()
    run_moves(moves, 0, scatters, outs)
    total.start(jnp.concatenate([part[...] for part in small], axis=0))
    for stage in range(len(groups) - 1):
        text.add(stage)
    run_moves(moves, 1, scatters, outs)
    total.add(0, small_out)
    run_moves(moves, 2, scatters, outs)
    text.add(len(groups) - 1)
    text.norm(texts, gain[0:1, :], grad_hidden)
    total.add(1, small_out)
    run_moves(moves, 3, scatters, outs)
    for stage in range(2, len(names)):
        total.add(stage, small_out)
        run_moves(moves, 2 + stage, scatters, outs)
    text.end(text_out)
    finish_moves(moves, scatters, outs)


def finish_kernel(layout, *refs):
    refs = iter(refs)
    pieces = [[next(refs) for _ in range(count)] for count in layout]
    streams = [next(refs) for _ in range(3)]
    sums = next(refs)
    for index, parts in enumerate(pieces):
        out = next(refs)
        halves = [part[half] for half in range(2) for part in parts]
        value = jnp.concatenate(halves, axis=0).astype(F32)
        out[...] = value if index + 1 == len(pieces) else jnp.transpose(value)
    for stream in streams:
        out = next(refs)
        out[...] = stream[...]
    gate, bias, last, gains, shifts = (next(refs) for _ in range(5))
    gate[...] = sums[0:H, :]
    for index in range(FF // D):
        bias[pl.ds(index * D, D)] = sums[24 + index, :]
    last[...] = sums[16, :]
    for out, at in ((gains, 0), (shifts, 1)):
        for index, row in enumerate((40 + at, 32 + at, 34 + at, 17 + at)):
            out[index : index + 1, :] = sums[row : row + 1, :]


def whole(shape):
    return pl.BlockSpec(shape, lambda step: (0,) * len(shape))


def columns(rows, offset=0):
    return pl.BlockSpec((rows, QUAD), lambda step: (0, offset + step))


def stat_rows():
    return pl.BlockSpec((8, ROWS), lambda step: (step, 0))


def shaped(shape, kind):
    return jax.ShapeDtypeStruct(shape, kind)


ANY = pl.BlockSpec(memory_space=pl.ANY)


def call(kernel, name, steps, ins, outs, scratch, flops, byte_count, collective=None):
    in_specs, operands = zip(*ins)
    out_specs, out_shapes = zip(*outs)
    return pl.pallas_call(
        kernel,
        grid=(steps,),
        in_specs=list(in_specs),
        out_specs=list(out_specs),
        out_shape=list(out_shapes),
        scratch_shapes=scratch,
        name=name,
        compiler_params=pltpu.CompilerParams(
            vmem_limit_bytes=VMEM_LIMIT,
            collective_id=collective,
            has_side_effects=collective is not None,
        ),
        cost_estimate=pl.CostEstimate(flops=flops, bytes_accessed=byte_count, transcendentals=0),
    )(*operands)


def own_pages(pages):
    return (whole((DOCS, *pages.shape[1:])), pages)


SMEM = pl.BlockSpec(memory_space=pltpu.SMEM)


def self_forward(texts, images, cots, mask, regions, doc_pages, gain, shift, project, wide, blk):
    groups = group_bits(blk)
    count = DOCS << len(groups)
    keys = count * PAGE
    return call(
        functools.partial(self_forward_kernel, wide, blk),
        "self_forward",
        QUADS,
        [
            (SMEM, regions),
            (SMEM, doc_pages),
            (whole(texts.shape), texts),
            (whole(images.shape), images),
            (whole(cots.shape), cots),
            (whole(mask.shape), mask),
            (whole(gain.shape), gain),
            (whole(shift.shape), shift),
            (columns(D), project),
            (columns(D, QUADS), project),
            (columns(D, 2 * QUADS), project),
        ],
        [
            (columns(ROWS), shaped((ROWS, D), F32)),
            (stat_rows(), shaped((8 * QUADS, ROWS), F32)),
            (columns(ROWS), shaped((ROWS, D), BF16)),
            (columns(keys), shaped((keys, D), BF16)),
            (columns(keys), shaped((keys, D), BF16)),
            (ANY, shaped((count, PAGE, D), BF16)),
            (ANY, shaped((count, IMAGE, D), BF16)),
            (ANY, shaped((DOCS, PAGE, D), BF16)),
            (whole((keys, PAIR)), shaped((keys, PAIR), BF16)),
            (whole((count * IMAGE, PAIR)), shaped((count * IMAGE, PAIR), BF16)),
        ],
        [
            pltpu.VMEM((keys, D), BF16),
            pltpu.VMEM((DOCS, PAGE + EXTRA, D), BF16),
            pltpu.VMEM((DOCS, IMAGE + EXTRA, D), BF16),
            pltpu.VMEM((count, PAGE + EXTRA, D), BF16),
            pltpu.VMEM((count, IMAGE + EXTRA, D), BF16),
            pltpu.VMEM((DOCS, PAGE, D), BF16),
        ]
        + Gather.waits(groups) * 2
        + Gather.waits([])
        + [pltpu.SemaphoreType.DMA((3,))],
        6 * 10**9,
        12 * 10**6,
        0,
    )


def cross_forward(texts, pages, self_out, w_self, w_gate, gain, shift, closed, w_query, w_pairs):
    keys = closed.shape[0]
    return call(
        cross_forward_kernel,
        "cross_forward",
        QUADS,
        [
            own_pages(texts),
            (whole(pages.shape), pages),
            (whole(self_out.shape), self_out),
            (whole(w_self.shape), w_self),
            (whole(w_gate.shape), w_gate),
            (whole(gain.shape), gain),
            (whole(shift.shape), shift),
            (whole(closed.shape), closed),
            (columns(D), w_query),
            (columns(D), w_pairs),
            (columns(D, QUADS), w_pairs),
        ],
        [
            (whole((ROWS, D)), shaped((ROWS, D), F32)),
            (whole((ROWS, PAIR)), shaped((ROWS, PAIR), F32)),
            (columns(ROWS), shaped((ROWS, D), F32)),
            (stat_rows(), shaped((8 * QUADS, ROWS), F32)),
            (columns(ROWS), shaped((ROWS, D), BF16)),
            (columns(keys), shaped((keys, D), BF16)),
            (columns(keys), shaped((keys, D), BF16)),
        ],
        [
            pltpu.VMEM((keys, D), BF16),
            pltpu.VMEM((ROWS, D), BF16),
            pltpu.VMEM((PAIR, D), BF16),
        ],
        7 * 10**9,
        14 * 10**6,
    )


def forward_back(
    hidden, raw, gate, cots, w_out, gain, shift, w_expand, b_expand, w_reduce, b_reduce, wide, blk
):
    steps = FF // D
    cuts = tile_cuts(wide)
    names = tile_bits(wide, blk)
    expand = (FF // (2 * blk), D // (wide // 2))
    reduce = (D // (2 * blk), FF // (wide // 2))
    full, part = (2,) * len(names), (2,) * (len(names) - 1)
    return call(
        functools.partial(forward_back_kernel, steps, wide, blk),
        "forward_back",
        steps,
        [
            (whole((ROWS, D)), hidden),
            (whole((ROWS, D)), raw),
            (whole((ROWS, PAIR)), gate),
            (whole((DOCS, PAGE, D)), cots),
            (whole((D, D)), w_out),
            (whole(gain.shape), gain),
            (whole(shift.shape), shift),
            (pl.BlockSpec((D, D), lambda step: (0, step)), w_expand),
            (pl.BlockSpec((1, D), lambda step: (0, step)), b_expand),
            (pl.BlockSpec((D, D), lambda step: (step, 0)), w_reduce),
            (whole((1, D)), b_reduce),
        ],
        [
            (whole((DOCS, PAGE, D)), shaped((DOCS, PAGE, D), BF16)),
            (ANY, shaped(part + expand, BF16)),
            (ANY, shaped(part + reduce, BF16)),
            (whole((cuts, D, D // cuts)), shaped((cuts, D, D // cuts), BF16)),
            (whole((ROWS, D)), shaped((ROWS, D), F32)),
            (whole((ROWS, D)), shaped((ROWS, D), BF16)),
            (whole((8 * QUADS, ROWS)), shaped((8 * QUADS, ROWS), F32)),
            (whole((ROWS, PAIR)), shaped((ROWS, PAIR), F32)),
            (whole((16, D)), shaped((16, D), F32)),
        ],
        [
            pltpu.VMEM((ROWS, D), BF16),
            pltpu.VMEM((ROWS, D), F32),
            pltpu.VMEM((ROWS, D), BF16),
            pltpu.VMEM((ROWS, D), BF16),
            pltpu.VMEM((ROWS, D), F32),
            pltpu.VMEM((ROWS, D), F32),
            pltpu.VMEM(full + expand, BF16),
            pltpu.VMEM(full + reduce, BF16),
            pltpu.VMEM(part + expand, BF16),
            pltpu.VMEM(part + reduce, BF16),
            pltpu.SemaphoreType.DMA((2, steps)),
            pltpu.SemaphoreType.DMA((2, steps)),
            pltpu.SemaphoreType.DMA((2,)),
        ],
        8 * 10**9,
        25 * 10**6,
        1,
    )


def back_scratch(keys, dq_columns):
    return [
        pltpu.VMEM((keys, D), BF16),
        pltpu.VMEM((keys, 2 * QUAD), BF16),
        pltpu.VMEM((keys, D), F32),
        pltpu.VMEM((ROWS, dq_columns), BF16),
    ]


def cross_back(
    pages, gain, shift, closed, q, k, v, grad_out, lse, delta, w_pairs,
    w_query, w_gate, w_self, hidden, self_out, grad_mixed, grad_logit, joined, jobs, sources,
    plan, wide, blk,
):
    keys = closed.shape[0]
    half = keys // 2
    cuts = tile_cuts(wide)
    return call(
        functools.partial(cross_back_kernel, wide, blk, jobs, plan),
        "cross_back",
        QUADS,
        [
            (whole(pages.shape), pages),
            (whole(gain.shape), gain),
            (whole(shift.shape), shift),
            (whole(closed.shape), closed),
            (columns(ROWS), q),
            (columns(keys), k),
            (columns(keys), v),
            (columns(ROWS), grad_out),
            (stat_rows(), lse),
            (stat_rows(), delta),
            (columns(D), w_pairs),
            (columns(D, QUADS), w_pairs),
            (whole((D, D)), w_query),
            (whole(w_gate.shape), w_gate),
            (whole((D, D)), w_self),
            (whole((ROWS, D)), hidden),
            (whole((ROWS, D)), self_out),
            (whole((ROWS, D)), grad_mixed),
            (whole((ROWS, PAIR)), grad_logit),
            (whole((DOCS, PAGE, D)), joined),
        ]
        + [(ANY, source) for source in sources],
        [
            (whole((half, D)), shaped((half, D), BF16)),
            (whole((half, D)), shaped((half, D), BF16)),
            (whole((cuts, 2 * D, D // cuts)), shaped((cuts, 2 * D, D // cuts), BF16)),
            (whole((cuts, D, D // cuts)), shaped((cuts, D, D // cuts), BF16)),
            (whole((cuts, D, D // cuts)), shaped((cuts, D, D // cuts), BF16)),
            (whole((16, D)), shaped((16, D), F32)),
            (whole((ROWS, D)), shaped((ROWS, D), F32)),
            (whole((ROWS, D)), shaped((ROWS, D), BF16)),
            (whole((8 * QUADS, ROWS)), shaped((8 * QUADS, ROWS), F32)),
            (whole((8, D)), shaped((8, D), F32)),
            (whole((DOCS, PAGE, D)), shaped((DOCS, PAGE, D), BF16)),
        ]
        + [(ANY, job.result()) for job in jobs],
        back_scratch(keys, D) + [pltpu.VMEM((PAIR, D), BF16)] + [kind for job in jobs for kind in job.scratch()] + Home.scratch(),
        12 * 10**9,
        20 * 10**6,
        2,
    )


def self_back(
    pages, gain, shift, closed, q, k, v, grad_out, lse, delta, project, image_sums, images,
    jobs, sources, plan, wide, blk,
):
    keys = closed.shape[0]
    half = keys // 2
    cuts = tile_cuts(wide)
    image_half = image_sums[0].shape[0]
    return call(
        functools.partial(self_back_kernel, wide, blk, jobs, plan),
        "self_back",
        QUADS,
        [
            (whole(pages.shape), pages),
            (whole(gain.shape), gain),
            (whole(shift.shape), shift),
            (whole(closed.shape), closed),
            (columns(ROWS), q),
            (columns(keys), k),
            (columns(keys), v),
            (columns(ROWS), grad_out),
            (stat_rows(), lse),
            (stat_rows(), delta),
            (columns(D), project),
            (columns(D, QUADS), project),
            (columns(D, 2 * QUADS), project),
        ]
        + [(whole((image_half, D)), part) for part in image_sums]
        + [own_pages(images)]
        + [(ANY, source) for source in sources],
        [
            (whole((half, D)), shaped((half, D), BF16)),
            (whole((half, D)), shaped((half, D), BF16)),
            (whole((cuts, 3 * D, D // cuts)), shaped((cuts, 3 * D, D // cuts), BF16)),
            (whole((8, D)), shaped((8, D), F32)),
            (whole((DOCS, PAGE, D)), shaped((DOCS, PAGE, D), BF16)),
        ]
        + [(ANY, job.result()) for job in jobs],
        back_scratch(keys, QUAD)
        + [kind for job in jobs for kind in job.scratch()]
        + Rows.scratch(group_bits(blk), image_half),
        11 * 10**9,
        17 * 10**6,
        3,
    )


def tail(wide, blk, jobs, plan, sources, sums, texts, grad_hidden, gain, small):
    names = bit_names(wide, blk)
    vmem = pl.BlockSpec(memory_space=pltpu.VMEM)
    rows = sum(part.shape[0] for part in small)
    operands = [*sources, *sums, texts, grad_hidden, gain, *small]
    own = len(jobs) + len(sums)
    in_specs = [ANY if job.order else vmem for job in jobs] + [vmem] * (len(operands) - len(jobs))
    in_specs[own] = own_pages(texts)[0]
    return pl.pallas_call(
        functools.partial(tail_kernel, wide, blk, jobs, plan),
        grid=(1,),
        in_specs=in_specs,
        out_specs=[vmem] * (2 + len(jobs)),
        out_shape=[
            shaped((DOCS, PAGE, D), BF16),
            shaped((rows, D), F32),
            *(job.result() for job in jobs),
        ],
        scratch_shapes=[kind for job in jobs for kind in job.scratch()]
        + Rows.scratch(group_bits(blk), sums[0].shape[0])
        + Total.scratch(names, rows),
        name="tail",
        compiler_params=pltpu.CompilerParams(
            vmem_limit_bytes=VMEM_LIMIT, collective_id=4, has_side_effects=True
        ),
        cost_estimate=pl.CostEstimate(flops=10**7, bytes_accessed=10**8, transcendentals=0),
    )(*operands)


def finish(pieces, streams, sums):
    vmem = pl.BlockSpec(memory_space=pltpu.VMEM)
    operands = [part for parts in pieces for part in parts] + [*streams, sums]
    results = []
    for index, parts in enumerate(pieces):
        shape = (parts[0].shape[2], sum(2 * part.shape[1] for part in parts))
        results.append(shaped(shape[::-1] if index + 1 == len(pieces) else shape, F32))
    results += [shaped(stream.shape, BF16) for stream in streams]
    results += [shaped((H, D), F32), shaped((FF,), F32), shaped((D,), F32)]
    results += [shaped((4, D), F32)] * 2
    return pl.pallas_call(
        functools.partial(finish_kernel, tuple(len(parts) for parts in pieces)),
        in_specs=[vmem] * len(operands),
        out_specs=[vmem] * len(results),
        out_shape=results,
        name="finish",
        compiler_params=pltpu.CompilerParams(vmem_limit_bytes=VMEM_LIMIT),
        cost_estimate=pl.CostEstimate(flops=10**6, bytes_accessed=5 * 10**6, transcendentals=0),
    )(*operands)


def tile_cuts(wide):
    cuts = wide // 2
    return cuts if (D // cuts) % PAIR == 0 else 1


def tiled(grad, wide, blk):
    cuts = wide // 2
    if grad.shape[0] != cuts:
        _, rows, lanes = grad.shape
        grad = jnp.transpose(grad.reshape(rows, cuts, lanes // cuts), (1, 0, 2))
    names = tile_bits(wide, blk)
    return grad.reshape((2,) * len(names) + (grad.shape[1] // (2 * blk), grad.shape[2]))


def body(
    text_blocks,
    image_blocks,
    cotangent,
    text_mask,
    page_regions,
    doc_pages,
    self_project,
    self_output,
    cross_query,
    cross_pairs,
    cross_output,
    gate_weight,
    expand_weight,
    expand_bias,
    reduce_weight,
    reduce_bias,
    norm_gain,
    norm_bias,
):
    wide = lax.axis_size("wide")
    blk = lax.axis_size("blk")
    names = tuple(tile_bits(wide, blk))
    core = ("w", 0)
    first = (("w", 1),)
    others = tuple(("w", bit) for bit in range(2, wide.bit_length() - 1))
    low = (("b", 0),)
    high = tuple(("b", bit) for bit in range(1, blk.bit_length() - 1))
    share = 2 * blk
    lanes = 2 * D // wide
    far = 2 * FF // wide
    gate_rows = jnp.transpose(gate_weight)

    (
        self_out, self_lse, self_q, self_k, self_v, text_pages, image_pages, cots, text_closed,
        image_closed,
    ) = self_forward(
        text_blocks, image_blocks, cotangent, text_mask, page_regions, doc_pages, norm_gain,
        norm_bias, self_project, wide, blk,
    )
    hidden, gate, raw, cross_lse, cross_q, cross_k, cross_v = cross_forward(
        text_pages, image_pages, self_out, self_output, gate_rows, norm_gain, norm_bias,
        image_closed, cross_query, cross_pairs,
    )
    (
        joined, expand_sum, reduce_sum, d_cross_output, grad_mixed, grad_raw, cross_delta,
        grad_logit, small_last,
    ) = forward_back(
        hidden, raw, gate, cots, cross_output, norm_gain, norm_bias, expand_weight,
        expand_bias.reshape(1, FF), reduce_weight, reduce_bias.reshape(1, D), wide, blk,
    )

    def jobs_of(rows, split, size, left, orders):
        if rows % 16 or not 0 < split < rows:
            return [Job(left, orders[-1], 0, rows, size, False)]
        return [
            Job(left, orders[0], 0, split, size, False),
            Job(left, orders[1], split, rows - split, size, False),
        ]

    expand_rows, reduce_rows = FF // share, D // share
    expand_jobs = jobs_of(
        expand_rows, expand_rows // 32 * 16, lanes, names[:-1], (first + high, first)
    )
    reduce_jobs = jobs_of(reduce_rows, 16, far, names[:-1], (low + high, low))
    jobs = tuple(expand_jobs + reduce_jobs)
    sources = [expand_sum] * len(expand_jobs) + [reduce_sum] * len(reduce_jobs)
    plan = {0: (0, 2), 1: (3,), 2: (2, 1), 4: (0, 2)} if len(jobs) == 4 else {0: range(len(jobs))}
    (
        image_keep, image_send, d_pairs, d_query, d_self_output, d_gate, grad_hidden, self_do,
        self_delta, small_cross, joined_home, *partial,
    ) = cross_back(
        image_pages, norm_gain, norm_bias, image_closed, cross_q, cross_k, cross_v, grad_raw,
        cross_lse, cross_delta, cross_pairs, cross_query, gate_rows, self_output, hidden, self_out,
        grad_mixed, grad_logit, joined, jobs, sources, plan, wide, blk,
    )

    def rest(job, order, ends):
        left = job.after()
        wanted = tuple(name for name in order if name in left)
        return Job(left, wanted, 0, job.rows, job.lanes, ends)

    count = len(jobs)
    jobs = tuple(
        [rest(job, high + low + first + others, False) for job in expand_jobs]
        + [rest(job, high + first + others + low, False) for job in reduce_jobs]
    )
    one = (0, D // share, lanes, False)
    cross_jobs = (
        Job(names, (core,) + low, 0, 2 * D // share, lanes, False),
        Job(names, (core,) + first, *one),
        Job(names, (core,) + first, *one),
        Job(names, (core,) + first, *one),
    )
    cross_grads = [
        tiled(grad, wide, blk) for grad in (d_pairs, d_query, d_cross_output, d_self_output)
    ]
    late = tuple(range(count, count + 4))
    plan = {0: late + tuple(range(count)), 2: late}
    if count == 4:
        plan = {
            0: late + (1, 0, 2), 1: (3,), 2: late + (1,), 3: (3, 0, 2), 4: (1,), 5: (3, 1),
        }
    text_keep, text_send, d_project, small_self, image_home, *partial = self_back(
        text_pages, norm_gain, norm_bias, text_closed, self_q, self_k, self_v, self_do,
        self_lse, self_delta, self_project, (image_keep, image_send), image_pages,
        jobs + cross_jobs, partial + cross_grads, plan, wide, blk,
    )

    project_rows = 3 * D // share
    project_jobs = [
        job._replace(ends=True)
        for job in jobs_of(
            project_rows,
            project_rows // 2 // 16 * 16 + 16,
            lanes,
            names,
            ((core,) + first + low + others + high, (core,) + low + first + others + high),
        )
    ]
    last_jobs = [rest(cross_jobs[0], first + high + others, True)] + [
        rest(job, high + low + others, True) for job in cross_jobs[1:]
    ]
    ended = [Job((), (), 0, job.rows, job.lanes, True) for job in jobs]
    most = len(project_jobs)
    both = tuple(range(most))
    crossed = tuple(range(most, most + 4))
    plan = {
        0: both + crossed + tuple(range(most + 4, most + 4 + count)),
        1: both,
        2: crossed,
        3: both + crossed,
        4: both + crossed,
        5: both,
        6: both,
    }
    text_home, sums, *pieces = tail(
        wide, blk, (*project_jobs, *last_jobs, *ended), plan,
        [tiled(d_project, wide, blk)] * most + partial[count:] + partial[:count],
        (text_keep, text_send), text_pages, grad_hidden, norm_gain,
        (d_gate, small_last, small_cross, small_self),
    )
    project_pieces = pieces[:most]
    cross_pieces = pieces[most : most + 4]
    expand_pieces = pieces[most + 4 : most + 4 + len(expand_jobs)]
    reduce_pieces = pieces[most + 4 + len(expand_jobs) :]
    (
        grad_cross_pairs, grad_cross_query, grad_cross_output, grad_self_output,
        grad_expand_weight, grad_self_project, grad_reduce_weight,
        joined_blocks, text_grad, image_grad,
        grad_gate_weight, grad_expand_bias, grad_reduce_bias, gains, shifts,
    ) = finish(
        [[piece] for piece in cross_pieces] + [expand_pieces, project_pieces, reduce_pieces],
        [joined_home, text_home, image_home], sums,
    )
    return (
        joined_blocks,
        text_grad,
        image_grad,
        grad_self_project,
        grad_self_output,
        grad_cross_query,
        grad_cross_pairs,
        grad_cross_output,
        grad_expand_weight,
        jnp.transpose(grad_reduce_weight),
        jnp.transpose(grad_gate_weight),
        grad_expand_bias,
        grad_reduce_bias,
        gains,
        shifts,
    )


def solution(mesh):
    rows = P("wide", "blk", None)
    return jax.shard_map(
        body,
        mesh=mesh,
        in_specs=(rows,) * 3 + (P("wide", "blk"),) * 2 + (P("wide"),) + (P(),) * 12,
        out_specs=(rows,) * 3 + (P("wide", "blk"),) * 7 + (P(),) * 5,
        check_vma=False,
    )
```

time: 310 us -> 232 us (0.75); the launches traced: 304 us -> 231 us
  starting transfers between devices: 33.9 us -> 0 us
  local copies, waits for them, and re-layouts: 19.2 us -> 2.56 us
  waiting for transfers between devices: 10.2 us -> 0 us
  other arithmetic: 8.04 us -> 0 us
    pallas_call x1 -> x2, Pallas kernels: 129 us -> 59.7 us  [the longest x1 56.4 us: tail(): pl.pallas_call(functools.partial(tail_kernel, wide, blk, jobs, plan), gri...]
    pallas_call x5, Pallas kernels: 102 us -> 168 us  [call(): pl.pallas_call(kernel, grid=(steps,), in_specs=list(in_specs), out_specs=...]
    ppermute x24 -> x0, starting transfers between devices: 33.9 us -> none  [exchange(): return lax.ppermute(value, AXES, pairs)]
    ppermute x24 -> x0, waiting for transfers between devices: 10.2 us -> none  [exchange(): return lax.ppermute(value, AXES, pairs)]
    convert_element_type x6 -> x0, local copies, waits for them, and re-layouts: 4.75 us -> none  [body(): jnp.transpose(piece.reshape(-1, piece.shape[-1])).astype(F32)]
    slice x6 -> x0, local copies, waits for them, and re-layouts: 3.88 us -> none  [the longest x1 1.58 us: body(): sums[at_self + 1]]
  transfers between devices with their start and end apart: 24 -> 0, of which waited for: 4 -> 0; matrix products, arithmetic and copies ran while one was open for 5% -> 0% of each run, Pallas kernels for 9% -> 0%
where the time goes in v3:
time: 232 us; the launch traced here: 231 us
  Pallas kernels  228 us (98%)
  local copies, waits for them, and re-layouts  2.56 us (1%)
    pallas_call x5, Pallas kernels, call(): pl.pallas_call(kernel, grid=(steps,), in_specs=list(in_specs), out_specs=...  168 us
    pallas_call x1, Pallas kernels, tail(): pl.pallas_call(functools.partial(tail_kernel, wide, blk, jobs, plan), gri...  56.4 us

profile of v3, /device:TPU:1, one launch (start us, length us, event | category | flops | bytes accessed | tf_op | source)
XLA Modules:
  0.0 231.5 jit_solution(2139209118193339212)
XLA Ops:
  0.6 1.3 copy.33.regions
  1.9 1.3 reshape.52.b_reduce
  3.2 41.2 %self_forward.1 = (f32[256,768]{1,0:T(8,128)}, f32[24,256]{1,0:T(8,128)}, bf16[256,768]{1,0:T(8,128)(2,1)}, bf16[1024,768]{1,0:T(8,128)(2,1)}, bf16[1024,768]{1,...) custom-call(s32[2,1]{1,0:T(2,128)} %copy.33.regions, ...), custom_call_target="tpu_custom_call" | custom-call | flops 6000000000 | bytes 12000000 | tf_op jit(solution)/shard_map/self_forward/pallas_call | solution.py:1145
  44.4 14.3 %cross_forward.1 = (f32[256,768]{1,0:T(8,128)}, f32[256,128]{1,0:T(8,128)}, f32[256,768]{1,0:T(8,128)}, f32[24,256]{1,0:T(8,128)}, bf16[256,768]{1,0:T(8,128)(2,...) custom-call(bf16[8,128,768]{2,1,0:T(8,128)(2,1)} %get-tuple-element.96.text.refs_0_.refs_12_, ...), custom_call_target="tpu_custom_call" | custom-call | flops 7000000000 | bytes 14000000 | tf_op jit(solution)/shard_map/cross_forward/pallas_call | solution.py:1145
  58.7 21.0 %forward_back.1 = (bf16[2,128,768]{2,1,0:T(8,128)(2,1)}, bf16[2,2,2,2,192,384]{5,4,3,2,1,0:T(8,128)(2,1)}, bf16[2,2,2,2,48,1536]{5,4,3,2,1,0:T(8,128)(2,1)}, bf1...) custom-call(f32[256,768]{1,0:T(8,128)} %get-tuple-element.107.hidden, ...), custom_call_target="tpu_custom_call" | custom-call | flops 8000000000 | bytes 25000000 | tf_op jit(solution)/shard_map/forward_back/pallas_call | solution.py:1145
  79.7 46.5 %cross_back.1 = (bf16[448,768]{1,0:T(8,128)(2,1)}, bf16[448,768]{1,0:T(8,128)(2,1)}, bf16[2,1536,384]{2,1,0:T(8,128)(2,1)}, bf16[2,768,384]{2,1,0:T(8,128)(2,1)}...) custom-call(bf16[8,112,768]{2,1,0:T(8,128)(2,1)} %get-tuple-element., ...), custom_call_target="tpu_custom_call" | custom-call | flops 12000000000 | bytes 20000000 | tf_op jit(solution)/shard_map/cross_back/pallas_call | solution.py:1145
  126.2 45.4 %self_back.1 = (bf16[512,768]{1,0:T(8,128)(2,1)}, bf16[512,768]{1,0:T(8,128)(2,1)}, bf16[2,2304,384]{2,1,0:T(8,128)(2,1)}, f32[8,768]{1,0:T(8,128)}, bf16[2,128,...) custom-call(bf16[8,128,768]{2,1,0:T(8,128)(2,1)} %get-tuple-element., ...), custom_call_target="tpu_custom_call" | custom-call | flops 11000000512 | bytes 17000000 | tf_op jit(solution)/shard_map/self_back/pallas_call | solution.py:1145
  171.6 56.4 %tail.1 = (bf16[2,128,768]{2,1,0:T(8,128)(2,1)}, f32[48,768]{1,0:T(8,128)}, bf16[2,80,192]{2,1,0:T(8,128)(2,1)}, bf16[2,64,192]{2,1,0:T(8,128)(2,1)}, bf16[2,96,...) custom-call(bf16[2,2,2,2,2,144,384]{6,5,4,3,2,1,0:T(8,128)(2,1)} %bi, ...), custom_call_target="tpu_custom_call" | custom-call | flops 10000000 | bytes 100000000 | tf_op jit(solution)/shard_map/tail/pallas_call | solution.py:1435
  228.0 3.3 %finish.1 = (f32[192,192]{1,0:T(8,128)}, f32[192,96]{1,0:T(8,128)}, f32[192,96]{1,0:T(8,128)}, f32[192,96]{1,0:T(8,128)}, f32[192,384]{1,0:T(8,128)}, /*index=5*...) custom-call(bf16[2,96,192]{2,1,0:T(8,128)(2,1)} %get-tuple-element.1, ...), custom_call_target="tpu_custom_call" | custom-call | flops 1000000 | bytes 5000000 | tf_op jit(solution)/shard_map/finish/pallas_call | solution.py:1466

commit v4 on v3

--- a/solution.py
+++ b/solution.py
@@ -20,12 +20,14 @@
 PAIR = 128
 IMAGE = 112
 EXTRA = 16
+SUMS = 24
+LONGEST = 1024
 EPSILON = 1e-05
 NEGATIVE = -1e30
 HIGHEST = lax.Precision.HIGHEST
 BF16 = jnp.bfloat16
 F32 = jnp.float32
-VMEM_LIMIT = 60 * 1024 * 1024
+VMEM_LIMIT = 62 * 1024 * 1024
 
 
 def product(left, right):
@@ -168,11 +170,19 @@
     return jnp.concatenate(parts, axis=1)
 
 
-def store_tiles(out_ref, rows, value):
-    cuts = out_ref.shape[0]
-    lanes = out_ref.shape[2]
-    for cut in range(cuts):
-        out_ref[cut, rows, :] = value[:, cut * lanes : (cut + 1) * lanes].astype(BF16)
+def put_rows(out, start, value):
+    rows, lanes = out.shape[-2:]
+    cuts = (value.shape[1] // lanes).bit_length() - 1
+    lead = len(out.shape) - 2
+    low = start
+    while low < start + value.shape[0]:
+        tile = low // rows
+        high = min(start + value.shape[0], (tile + 1) * rows)
+        for cut in range(1 << cuts):
+            piece = value[low - start : high - start, cut * lanes : (cut + 1) * lanes]
+            at = bits_of(cut, cuts) + bits_of(tile, lead - cuts)
+            out[at + (slice(low - tile * rows, high - tile * rows), slice(None))] = piece
+        low = high
 
 
 class Gather:
@@ -400,19 +410,24 @@
 def forward_back_kernel(
     steps, wide, blk,
     hidden, raw, gate, cots, w_out, gain, shift, w_expand, b_expand, w_reduce, b_reduce,
-    joined, expand_out, reduce_out, d_out, grad_mixed, grad_raw, delta, grad_logit, small,
+    joined, early_expand, late_expand, early_reduce, late_reduce, d_out, grad_mixed, grad_raw,
+    delta, grad_logit, small,
     gated, mixed, final, upstream, joined_sum, back_sum,
-    expand_all, reduce_all, expand_got, reduce_got, sends, receives, local,
+    expand_all, reduce_all, expand_got, reduce_got, expand_next, reduce_next,
+    sends, receives, next_sends, next_receives, local,
 ):
     step = pl.program_id(0)
     places = Places(wide, blk)
-    core = ("w", 0)
+    core, along, across = ("w", 0), ("w", 1), ("b", 0)
+    cuts = wide.bit_length() - 2
+    kinds = (
+        (expand_part, expand_all, expand_got, expand_next, along),
+        (reduce_part, reduce_all, reduce_got, reduce_next, across),
+    )
 
     def copies(at):
         found = []
-        for index, (part, grad, got) in enumerate(
-            ((expand_part, expand_all, expand_got), (reduce_part, reduce_all, reduce_got))
-        ):
+        for index, (part, grad, got, _, _) in enumerate(kinds):
             lead, tail = part(wide, blk, at)
             found.append(
                 remote(
@@ -425,9 +440,41 @@
             )
         return found
 
+    def add(at):
+        for (part, grad, got, _, _), copy in zip(kinds, copies(at)):
+            copy.wait_recv()
+            lead, tail = part(wide, blk, at)
+            add_blocks(got.at[lead + tail], grad.at[lead + (places.bit(core),) + tail])
+
+    def pieces(at):
+        (lead, tail), (far_lead, far_tail) = (
+            expand_part(wide, blk, at), reduce_part(wide, blk, at)
+        )
+        bit, far_bit = places.bit(along), places.bit(across)
+        head, rest = lead[: cuts - 1], lead[cuts:]
+        yield (
+            expand_got.at[head + (bit,) + rest + tail],
+            expand_got.at[head + (1 - bit,) + rest + tail],
+            expand_next.at[head + rest[1:] + tail],
+        )
+        yield (
+            reduce_got.at[far_lead[:-1] + (far_bit,) + far_tail],
+            reduce_got.at[far_lead[:-1] + (1 - far_bit,) + far_tail],
+            reduce_next.at[far_lead[1:-1] + far_tail],
+        )
+
+    def onward(at):
+        return [
+            remote(
+                send, land, next_sends.at[index, at], next_receives.at[index, at],
+                places.flip(kinds[index][4]),
+            )
+            for index, (_, send, land) in enumerate(pieces(at))
+        ]
+
     @pl.when(step == 0)
     def _():
-        greet(places, [core], False)
+        greet(places, [core, along, across], False)
         upstream[0:PAGE, :] = cots[0]
         upstream[PAGE:ROWS, :] = cots[1]
         small[...] = jnp.zeros_like(small)
@@ -449,12 +496,20 @@
     joined_sum[...] += product(active, w_reduce[...])
     grad_active = against(upstream[...], w_reduce[...]).astype(BF16)
     grad_inner = (grad_active.astype(F32) * slope).astype(BF16)
-    small[pl.ds(8 + step, 1), :] = column_sum(grad_inner.astype(F32))
+    small[pl.ds(4 + step, 1), :] = column_sum(grad_inner.astype(F32))
     back_sum[...] += against(grad_inner, w_expand[...])
     put_expand(expand_all, transposed(grad_inner, final[...]).astype(BF16), step, wide, blk)
     put_reduce(reduce_all, transposed(upstream[...], active).astype(BF16), step, wide, blk)
     for copy in copies(step):
         copy.start()
+    for at in range(steps - 1):
+
+        @pl.when(step == at + 1)
+        def _():
+            add(at)
+            if at < steps // 2:
+                for copy in onward(at):
+                    copy.start()
 
     @pl.when(step == steps - 1)
     def _():
@@ -467,7 +522,7 @@
         grad = cotangent + norm_back(back, scaled, inverse, gain[3:4, :])
         grad_mixed[...] = grad
         branch = grad.astype(BF16)
-        store_tiles(d_out, slice(None), transposed(branch, gated[...]))
+        put_rows(d_out, 0, transposed(branch, gated[...]).astype(BF16))
         grad_gated = against(branch, w_out[...]).astype(BF16).astype(F32)
         gates = gate[...]
         lanes = lane_index(ROWS)
@@ -481,17 +536,24 @@
         small[0:1, :] = column_sum(cotangent)
         small[1:2, :] = column_sum(back * scaled)
         small[2:3, :] = column_sum(back)
-        for at in range(steps):
-            for copy in copies(at):
-                copy.wait_recv()
-        moves = []
-        for index, (grad, got, out) in enumerate(
-            ((expand_all, expand_got, expand_out), (reduce_all, reduce_got, reduce_out))
-        ):
-            lead = len(got.shape) - 2
-            add_blocks(got, grad.at[(slice(None),) * lead + (places.bit(core),)])
-            moves.append(pltpu.make_async_copy(got, out, local.at[index]))
-            moves[-1].start()
+        add(steps - 1)
+        half = (slice(None),) * cuts
+        moves = [
+            pltpu.make_async_copy(expand_got.at[half + (1,)], late_expand, local.at[0]),
+            pltpu.make_async_copy(reduce_got.at[1], late_reduce, local.at[1]),
+        ]
+        for move in moves:
+            move.start()
+        for at in range(steps // 2):
+            for copy, (kept, _, land) in zip(onward(at), pieces(at)):
+                copy.wait()
+                add_blocks(land, kept)
+        moves += [
+            pltpu.make_async_copy(expand_next, early_expand, local.at[2]),
+            pltpu.make_async_copy(reduce_next, early_reduce, local.at[3]),
+        ]
+        for move in moves[2:]:
+            move.start()
         for at in range(steps):
             for copy in copies(at):
                 copy.wait_send()
@@ -499,9 +561,7 @@
             move.wait()
 
 
-def spread_back(normed, dkv, wk, wv, dx, dw_k, dw_v, k_rows, v_rows):
-    store_tiles(dw_k, k_rows, transposed(dkv[:, :QUAD], normed[...]))
-    store_tiles(dw_v, v_rows, transposed(dkv[:, QUAD:], normed[...]))
+def spread_back(dkv, wk, wv, dx):
     weights = jnp.concatenate([wk[...], wv[...]], axis=1)
 
     size = dx.shape[0] // 4
@@ -550,162 +610,208 @@
     return moves
 
 
-def run_moves(moves, point, scatters, outs):
+def run_moves(moves, point, scatters):
     for index, stage in moves.get(point, ()):
-        scatter = scatters[index]
         if stage < 0:
-            scatter.start()
+            scatters[index].start()
         else:
-            scatter.add(stage)
-        if stage + 1 == scatter.stages and not scatter.job.ends:
-            scatter.store(outs[index]).start()
-
-
-def finish_moves(moves, scatters, outs):
-    run_moves(moves, END, scatters, outs)
-    for scatter, out in zip(scatters, outs):
-        scatter.end(out)
-
-
-def cross_back_kernel(wide, blk, jobs, plan, *refs):
+            scatters[index].add(stage)
+
+
+def back_kernel(wide, blk, jobs, plan, *refs):
     refs = iter(refs)
     (
-        pages, gain, shift, closed, q_in, k_in, v_in, do_in, lse, delta, wk, wv,
-        w_query, w_gate, w_self, hidden, self_out, grad_mixed, grad_logit, joined,
-    ) = (next(refs) for _ in range(20))
-    sources = [next(refs) for _ in jobs]
-    (
-        keep, send, dw_pairs, dw_query, dw_self, dw_gate, grad_hidden, self_do, self_delta, small,
-        joined_out,
-    ) = (next(refs) for _ in range(11))
-    outs = [next(refs) for _ in jobs]
-    normed, dkv, dx, dq, gates = (next(refs) for _ in range(5))
+        images, image_own, texts, gain, shift, cross_closed, self_closed,
+        q_cross, k_cross, v_cross, do_cross, lse_cross, delta_cross, wk_cross, wv_cross,
+        q_self, k_self, v_self, lse_self, wq_self, wk_self, wv_self,
+        w_query, w_gate, w_self, hidden, self_out, grad_mixed, grad_logit, joined, last_small,
+    ) = (next(refs) for _ in range(31))
+    early_expand, late_expand, early_reduce, late_reduce, d_cross_output = (
+        next(refs) for _ in range(5)
+    )
+    joined_out, text_out, image_out, sums_out, last_out = (next(refs) for _ in range(5))
+    outs = [next(refs) if job.ends else None for job in jobs]
+    normed, dkv, dx, dq, gates, grad_hidden, self_do, self_delta = (next(refs) for _ in range(8))
+    pages, keep, send, row_sums, sums_in, local = (next(refs) for _ in range(6))
+    d_pairs, d_query, d_self_output, d_project, expand_both, reduce_both = (
+        next(refs) for _ in range(6)
+    )
+    sources = [
+        early_expand, late_expand, early_reduce, late_reduce, expand_both, reduce_both,
+        d_pairs, d_query, d_cross_output, d_self_output,
+    ] + [d_project] * (len(jobs) - 10)
+    lands = [expand_both.at[0], expand_both.at[1], reduce_both.at[0], reduce_both.at[1]]
+    lands += [None] * (len(jobs) - 4)
     step = pl.program_id(0)
+    places = Places(wide, blk)
+    names = bit_names(wide, blk)
+    groups = group_bits(blk)
+    scatters = [
+        Scatter(places, job, source, refs, last)
+        for job, source, last in zip(jobs, sources, lands)
+    ]
     moves = moves_of(plan, jobs)
-    places = Places(wide, blk)
-    scatters = [Scatter(places, job, source, refs) for job, source in zip(jobs, sources)]
     home = Home(places, refs)
+    image_rows = pl.ds(0, k_cross.shape[0] // 2)
+    image = Rows(
+        places, groups, keep.at[image_rows], send.at[image_rows], row_sums.at[image_rows], refs
+    )
+    text = Rows(places, groups, keep, send, row_sums, refs)
+    image_pages = pages.at[:, pl.ds(0, IMAGE)]
+    fetches = [
+        pltpu.make_async_copy(images, image_pages, local.at[0]),
+        pltpu.make_async_copy(texts, pages, local.at[1]),
+        pltpu.make_async_copy(grad_mixed, grad_hidden, local.at[2]),
+        pltpu.make_async_copy(w_self, normed.at[pl.ds(0, D)], local.at[3]),
+    ]
+    sums = Total(places, names, refs)
+    last_sums = Total(places, names, refs)
 
     def pump(point):
-        run_moves(moves, point, scatters, outs)
+        if 7 <= point <= 11:
+            sums.add(point - 7, sums_out)
+        if point == 7:
+            image.add(0)
+        if point == 10:
+            for stage in range(1, len(groups)):
+                image.add(stage)
+            image.norm(image_own, gain[2:3, :], None)
+        run_moves(moves, point, scatters)
+
+    def pumps(points):
+        for point in points:
+            pl.when(step == (point - 1) // 2)(functools.partial(pump, point))
 
     @pl.when(step == 0)
     def _():
-        greet(places, bit_names(wide, blk), True)
+        fetches[0].start()
+        fetches[2].start()
+        greet(places, names, True)
         pump(0)
         for turn in range(DOCS):
             home.put(turn, joined[turn])
-        normalize_pages(pages, gain[2:3, :], shift[2:3, :], normed)
-        dx[...] = jnp.zeros_like(dx)
-
-    def middle():
-        for at in range(QUADS):
-            pl.when(step == at)(functools.partial(pump, 2 * at + 1))
-
-    cols = pl.ds(pl.multiple_of(step * QUAD, QUAD), QUAD)
-    attend_backward(
-        q_in, k_in, v_in, do_in, lse, delta, closed, dq.at[:, cols], dkv, middle
-    )
-    spread_back(
-        normed, dkv, wk, wv, dx, dw_pairs, dw_pairs,
-        cols, pl.ds(pl.multiple_of(D + step * QUAD, QUAD), QUAD),
-    )
-    for at in range(QUADS):
-        pl.when(step == at)(functools.partial(pump, 2 * at + 2))
-
-    @pl.when(step == QUADS - 1)
+
+    @pl.when(step < QUADS)
     def _():
-        image_gain, image_shift = finish_pages(pages, dx, keep, send)
-        scaled, inverse = standardize(hidden[...])
-        cross = (scaled * gain[1:2, :] + shift[1:2, :]).astype(BF16)
-        grad_query = dq[...]
-        store_tiles(dw_query, slice(None), transposed(grad_query, cross))
-        dw_gate[...] = transposed(grad_logit[...], cross.astype(F32), HIGHEST)[:16, :]
-        gates[...] = jnp.zeros_like(gates)
-        gates[0:H, :] = w_gate[...]
-        upstream = against(grad_query, w_query[...]) + jnp.dot(
-            grad_logit[...], gates[...].astype(F32), precision=HIGHEST
-        )
-        grad = grad_mixed[...] + norm_back(upstream, scaled, inverse, gain[1:2, :])
-        grad_hidden[...] = grad
-        branch = grad.astype(BF16)
-        store_tiles(dw_self, slice(None), transposed(branch, self_out[...].astype(BF16)))
-        grad_result = against(branch, w_self[...]).astype(BF16)
-        self_do[...] = grad_result
-        self_delta[...] = head_rows(head_sums(grad_result.astype(F32) * self_out[...]))
-        small[...] = jnp.concatenate(
-            [
-                column_sum(upstream * scaled),
-                column_sum(upstream),
-                image_gain,
-                image_shift,
-                jnp.zeros((4, D), F32),
-            ],
-            axis=0,
-        )
-        home.end(joined_out)
-        finish_moves(moves, scatters, outs)
-
-
-def self_back_kernel(wide, blk, jobs, plan, *refs):
-    refs = iter(refs)
-    (
-        pages, gain, shift, closed, q_in, k_in, v_in, do_in, lse, delta, wq, wk, wv,
-        image_keep, image_send, image_own,
-    ) = (next(refs) for _ in range(16))
-    sources = [next(refs) for _ in jobs]
-    keep, send, dw_project, small, image_out = (next(refs) for _ in range(5))
-    outs = [next(refs) for _ in jobs]
-    normed, dkv, dx, dq = (next(refs) for _ in range(4))
-    step = pl.program_id(0)
-    moves = moves_of(plan, jobs)
-    places = Places(wide, blk)
-    groups = group_bits(blk)
-    scatters = [Scatter(places, job, source, refs) for job, source in zip(jobs, sources)]
-    image = Rows(places, groups, image_keep, image_send, refs)
-
-    def pump(point):
-        if point == 1:
-            image.add(0)
-        if point == 4:
-            for stage in range(1, len(groups)):
-                image.add(stage)
-            image.norm(image_own, gain[2:3, :], None)
-        run_moves(moves, point, scatters, outs)
-
-    @pl.when(step == 0)
+        keys = k_cross.shape[0]
+        rows = pl.ds(0, keys)
+        my_normed, my_dkv, my_dx = normed.at[rows], dkv.at[rows], dx.at[rows]
+
+        @pl.when(step == 0)
+        def _():
+            fetches[0].wait()
+            normalize_pages(image_pages, gain[2:3, :], shift[2:3, :], my_normed)
+            my_dx[...] = jnp.zeros(my_dx.shape, F32)
+
+        cols = pl.ds(pl.multiple_of(step * QUAD, QUAD), QUAD)
+        attend_backward(
+            q_cross, k_cross, v_cross, do_cross, lse_cross, delta_cross, cross_closed,
+            dq.at[:, cols], my_dkv, lambda: pumps((1, 3, 5)),
+        )
+        spread_back(my_dkv, wk_cross, wv_cross, my_dx)
+        for part in range(2):
+            value = transposed(my_dkv[:, part * QUAD : (part + 1) * QUAD], my_normed[...])
+            value = value.astype(BF16)
+            for at in range(QUADS):
+
+                @pl.when(step == at)
+                def _():
+                    put_rows(d_pairs, part * D + at * QUAD, value)
+
+        pumps((2, 4))
+
+        @pl.when(step == QUADS - 1)
+        def _():
+            image_gain, image_shift = finish_pages(
+                image_pages, my_dx, image.keep, image.send
+            )
+            fetches[1].start()
+            fetches[3].start()
+            image.start()
+            scaled, inverse = standardize(hidden[...])
+            cross = (scaled * gain[1:2, :] + shift[1:2, :]).astype(BF16)
+            grad_query = dq[...]
+            put_rows(d_query, 0, transposed(grad_query, cross).astype(BF16))
+            d_gate = transposed(grad_logit[...], cross.astype(F32), HIGHEST)[:H, :]
+            gates[...] = jnp.zeros_like(gates)
+            gates[0:H, :] = w_gate[...]
+            upstream = against(grad_query, w_query[...]) + jnp.dot(
+                grad_logit[...], gates[...].astype(F32), precision=HIGHEST
+            )
+            fetches[2].wait()
+            grad = grad_hidden[...] + norm_back(upstream, scaled, inverse, gain[1:2, :])
+            grad_hidden[...] = grad
+            branch = grad.astype(BF16)
+            put_rows(
+                d_self_output, 0, transposed(branch, self_out[...].astype(BF16)).astype(BF16)
+            )
+            fetches[3].wait()
+            grad_result = against(branch, normed[0:D, :]).astype(BF16)
+            self_do[...] = grad_result
+            self_delta[...] = head_rows(head_sums(grad_result.astype(F32) * self_out[...]))
+            sums_in[0:H, :] = d_gate
+            sums_in[H : H + 8, :] = last_small[...]
+            sums_in[H + 8 : SUMS, :] = jnp.concatenate(
+                [column_sum(upstream * scaled), column_sum(upstream), image_gain, image_shift],
+                axis=0,
+            )
+            sums.start(sums_in[...])
+            home.end(joined_out)
+            pump(6)
+            fetches[1].wait()
+            normalize_pages(pages, gain[0:1, :], shift[0:1, :], normed)
+            dx[...] = jnp.zeros(dx.shape, F32)
+
+    @pl.when(step >= QUADS)
     def _():
-        greet(places, bit_names(wide, blk), True)
-        image.start()
-        pump(0)
-        normalize_pages(pages, gain[0:1, :], shift[0:1, :], normed)
-        dx[...] = jnp.zeros_like(dx)
-
-    def middle():
-        for at in range(QUADS):
-            pl.when(step == at)(functools.partial(pump, 2 * at + 1))
-
-    attend_backward(q_in, k_in, v_in, do_in, lse, delta, closed, dq, dkv, middle)
-    spread_back(
-        normed, dkv, wk, wv, dx, dw_project, dw_project,
-        pl.ds(pl.multiple_of(D + step * QUAD, QUAD), QUAD),
-        pl.ds(pl.multiple_of(2 * D + step * QUAD, QUAD), QUAD),
-    )
-    store_tiles(
-        dw_project,
-        pl.ds(pl.multiple_of(step * QUAD, QUAD), QUAD),
-        transposed(dq[...], normed[0:ROWS, :]),
-    )
-    dx[0:ROWS, :] += against(dq[...], wq[...])
-    for at in range(QUADS - 1):
-        pl.when(step == at)(functools.partial(pump, 2 * at + 2))
-
-    @pl.when(step == QUADS - 1)
-    def _():
-        gain_sum, shift_sum = finish_pages(pages, dx, keep, send)
-        small[...] = jnp.concatenate([gain_sum, shift_sum, jnp.zeros((6, D), F32)], axis=0)
-        finish_moves(moves, scatters, outs)
-        image.end(image_out)
+        quad = step - QUADS
+        cols = pl.ds(pl.multiple_of(quad * QUAD, QUAD), QUAD)
+        my_dq = dq.at[:, cols]
+        attend_backward(
+            q_self, k_self, v_self, self_do.at[:, cols], lse_self,
+            self_delta.at[pl.ds(pl.multiple_of(quad * 8, 8), 8)], self_closed,
+            my_dq, dkv, lambda: pumps((7, 9, 11)),
+        )
+        spread_back(dkv, wk_self, wv_self, dx)
+        dx[0:ROWS, :] += against(my_dq[...], wq_self[...])
+        for part in range(3):
+            if part == 0:
+                value = transposed(my_dq[...], normed[0:ROWS, :])
+            else:
+                value = transposed(dkv[:, (part - 1) * QUAD : part * QUAD], normed[...])
+            value = value.astype(BF16)
+            for at in range(QUADS):
+
+                @pl.when(quad == at)
+                def _():
+                    put_rows(d_project, part * D + at * QUAD, value)
+
+        pumps((8, 10))
+
+        @pl.when(quad == QUADS - 1)
+        def _():
+            gain_sum, shift_sum = finish_pages(pages, dx, keep, send)
+            text.start()
+            run_moves(moves, 12, scatters)
+            last_sums.start(jnp.concatenate([gain_sum, shift_sum, jnp.zeros((6, D), F32)], axis=0))
+            for stage in range(5, len(names)):
+                sums.add(stage, sums_out)
+            run_moves(moves, 13, scatters)
+            for stage in range(len(groups) - 1):
+                text.add(stage)
+            run_moves(moves, 14, scatters)
+            last_sums.add(0, last_out)
+            run_moves(moves, 15, scatters)
+            text.add(len(groups) - 1)
+            text.norm(pages, gain[0:1, :], grad_hidden)
+            for stage in range(1, len(names)):
+                last_sums.add(stage, last_out)
+                run_moves(moves, 15 + stage, scatters)
+            image.end(image_out)
+            text.end(text_out)
+            run_moves(moves, END, scatters)
+            for scatter, out in zip(scatters, outs):
+                scatter.end(out)
 
 
 class Places:
@@ -797,6 +903,8 @@
     rows: int
     lanes: int
     ends: bool
+    near: bool = False
+    inner: bool = False
 
     def after(self):
         return tuple(name for name in self.left if name not in self.order)
@@ -804,9 +912,9 @@
     def scratch(self):
         count = len(self.left)
         kinds = []
-        if self.order:
+        if not self.near:
             kinds.append(pltpu.VMEM((2,) * (count - 1) + (self.rows, self.lanes), BF16))
-        for stage in range(len(self.order)):
+        for stage in range(len(self.order) - int(self.inner)):
             kinds.append(pltpu.VMEM((2,) * (count - 1 - stage) + (self.rows, self.lanes), BF16))
         if self.ends:
             kinds.append(pltpu.VMEM((2, self.rows, self.lanes // 2), BF16))
@@ -814,9 +922,7 @@
         return kinds + [pltpu.SemaphoreType.DMA((waits,))] * 2 + [pltpu.SemaphoreType.DMA]
 
     def result(self):
-        if self.ends:
-            return shaped((2, self.rows, self.lanes // 2), BF16)
-        return shaped((2,) * len(self.after()) + (self.rows, self.lanes), BF16)
+        return shaped((2, self.rows, self.lanes // 2), BF16)
 
 
 def bits_of(index, count):
@@ -838,12 +944,14 @@
 
 
 class Scatter:
-    def __init__(self, places, job, source, scratch):
+    def __init__(self, places, job, source, scratch, last=None):
         self.places = places
         self.job = job
         self.source = source
-        self.own = next(scratch) if job.order else None
-        self.got = [next(scratch) for _ in job.order] or [source]
+        self.own = None if job.near else next(scratch)
+        self.got = [next(scratch) for _ in range(len(job.order) - int(job.inner))]
+        if job.inner:
+            self.got.append(last)
         self.ends = next(scratch) if job.ends else None
         self.sends, self.receives, self.local = next(scratch), next(scratch), next(scratch)
         self.stages = len(job.order)
@@ -878,10 +986,8 @@
         return pltpu.make_async_copy(kept, self.own, self.local)
 
     def start(self):
-        if self.stages == 0:
-            self.halve()
         self.copy(0).start()
-        if self.stages > 0:
+        if not self.job.near:
             self.fetch().start()
 
     def halve(self):
@@ -892,12 +998,12 @@
 
     def add(self, stage):
         self.copy(stage).wait_recv()
-        if stage == 0:
+        if stage == 0 and not self.job.near:
             self.fetch().wait()
             source = self.own
         else:
             bit = self.places.bit(self.job.order[stage])
-            source = self.cut(self.got[stage - 1], stage, bit)
+            source = self.cut(self.source if stage == 0 else self.got[stage - 1], stage, bit)
         add_blocks(self.got[stage], source)
         if stage + 1 < self.stages:
             self.copy(stage + 1).start()
@@ -905,33 +1011,32 @@
             self.halve()
             self.copy(stage + 1).start()
 
-    def store(self, out):
-        return pltpu.make_async_copy(self.got[-1], out, self.local)
-
     def end(self, out):
-        if self.job.ends:
-            self.copy(self.stages).wait_recv()
-            lanes = self.job.lanes // 2
-            piece = self.got[-1][...]
-            other = self.ends[1]
-            second = self.places.bit(("w", 0)) == 1
-            mine = jnp.where(second, piece[:, lanes:], piece[:, :lanes])
-            out[0] = jnp.where(second, other, mine)
-            out[1] = jnp.where(second, mine, other)
-        else:
-            self.store(out).wait()
         for stage in range(self.stages + int(self.job.ends)):
             self.copy(stage).wait_send()
+        if not self.job.ends:
+            return
+        self.copy(self.stages).wait_recv()
+        lanes = self.job.lanes // 2
+        piece = self.got[-1][...]
+        other = self.ends[1]
+        second = self.places.bit(("w", 0)) == 1
+        mine = jnp.where(second, piece[:, lanes:], piece[:, :lanes])
+        out[0] = jnp.where(second, other, mine)
+        out[1] = jnp.where(second, mine, other)
 
 
 class Home:
     def __init__(self, places, scratch):
         self.places = places
-        self.home, self.landed, self.sends, self.receives = (next(scratch) for _ in range(4))
+        self.home, self.landed, self.sends, self.receives, self.local = (
+            next(scratch) for _ in range(5)
+        )
 
     @staticmethod
     def scratch():
-        return [pltpu.VMEM((DOCS, PAGE, D), BF16)] * 2 + [pltpu.SemaphoreType.DMA((DOCS,))] * 2
+        waits = [pltpu.SemaphoreType.DMA((DOCS,))] * 2 + [pltpu.SemaphoreType.DMA]
+        return [pltpu.VMEM((DOCS, PAGE, D), BF16)] * 2 + waits
 
     def copy(self, turn):
         return remote(
@@ -964,25 +1069,26 @@
     def end(self, out):
         for turn in range(DOCS):
             self.go(turn, False)
-        out[...] = self.landed[...]
+        copy = pltpu.make_async_copy(self.landed, out, self.local)
+        copy.start()
+        copy.wait()
 
 
 class Rows:
-    def __init__(self, places, names, keep, send, scratch):
+    def __init__(self, places, names, keep, send, sums, scratch):
         self.places = places
         self.size = keep.shape[0] // (DOCS << (len(names) - 1))
         self.names = list(reversed(names))
         self.keep = keep
         self.send = send
-        self.sums = next(scratch)
+        self.sums = sums
         self.got = [next(scratch) for _ in names]
         self.sends, self.receives = next(scratch), next(scratch)
         self.back = Home(places, scratch)
 
     @staticmethod
     def scratch(names, rows):
-        kinds = [pltpu.VMEM((rows, D), BF16)]
-        kinds += [pltpu.VMEM((rows >> stage, D), BF16) for stage in range(len(names))]
+        kinds = [pltpu.VMEM((rows >> stage, D), BF16) for stage in range(len(names))]
         return kinds + [pltpu.SemaphoreType.DMA((len(names),))] * 2 + Home.scratch()
 
     def copy(self, stage):
@@ -999,9 +1105,7 @@
         self.copy(0).start()
 
     def add(self, stage):
-        self.copy(stage).wait_recv()
-        if stage > 0:
-            self.copy(stage).wait_send()
+        self.copy(stage).wait()
         source = self.keep if stage == 0 else self.sums
         rows = self.got[stage].shape[0]
 
@@ -1028,7 +1132,6 @@
 
     def end(self, out):
         self.back.end(out)
-        self.copy(0).wait_send()
 
 
 class Total:
@@ -1062,46 +1165,11 @@
             out[...] = value
 
 
-def tail_kernel(wide, blk, jobs, plan, *refs):
-    refs = iter(refs)
-    sources = [next(refs) for _ in jobs]
-    keep, send, texts, grad_hidden, gain = (next(refs) for _ in range(5))
-    small = [next(refs) for _ in range(4)]
-    text_out, small_out = next(refs), next(refs)
-    outs = [next(refs) for _ in jobs]
-    moves = moves_of(plan, jobs)
-    places = Places(wide, blk)
-    names = bit_names(wide, blk)
-    groups = group_bits(blk)
-    scatters = [Scatter(places, job, source, refs) for job, source in zip(jobs, sources)]
-    text = Rows(places, groups, keep, send, refs)
-    total = Total(places, names, refs)
-
-    greet(places, names, True)
-    text.start()
-    run_moves(moves, 0, scatters, outs)
-    total.start(jnp.concatenate([part[...] for part in small], axis=0))
-    for stage in range(len(groups) - 1):
-        text.add(stage)
-    run_moves(moves, 1, scatters, outs)
-    total.add(0, small_out)
-    run_moves(moves, 2, scatters, outs)
-    text.add(len(groups) - 1)
-    text.norm(texts, gain[0:1, :], grad_hidden)
-    total.add(1, small_out)
-    run_moves(moves, 3, scatters, outs)
-    for stage in range(2, len(names)):
-        total.add(stage, small_out)
-        run_moves(moves, 2 + stage, scatters, outs)
-    text.end(text_out)
-    finish_moves(moves, scatters, outs)
-
-
 def finish_kernel(layout, *refs):
     refs = iter(refs)
     pieces = [[next(refs) for _ in range(count)] for count in layout]
     streams = [next(refs) for _ in range(3)]
-    sums = next(refs)
+    sums, last_sums = next(refs), next(refs)
     for index, parts in enumerate(pieces):
         out = next(refs)
         halves = [part[half] for half in range(2) for part in parts]
@@ -1113,11 +1181,12 @@
     gate, bias, last, gains, shifts = (next(refs) for _ in range(5))
     gate[...] = sums[0:H, :]
     for index in range(FF // D):
-        bias[pl.ds(index * D, D)] = sums[24 + index, :]
-    last[...] = sums[16, :]
+        bias[pl.ds(index * D, D)] = sums[H + 4 + index, :]
+    last[...] = sums[H, :]
     for out, at in ((gains, 0), (shifts, 1)):
-        for index, row in enumerate((40 + at, 32 + at, 34 + at, 17 + at)):
-            out[index : index + 1, :] = sums[row : row + 1, :]
+        out[0:1, :] = last_sums[at : at + 1, :]
+        for index, row in enumerate((H + 8 + at, H + 10 + at, H + 1 + at)):
+            out[index + 1 : index + 2, :] = sums[row : row + 1, :]
 
 
 def whole(shape):
@@ -1258,11 +1327,11 @@
     hidden, raw, gate, cots, w_out, gain, shift, w_expand, b_expand, w_reduce, b_reduce, wide, blk
 ):
     steps = FF // D
-    cuts = tile_cuts(wide)
     names = tile_bits(wide, blk)
+    small = (D // (2 * blk), D // (wide // 2))
     expand = (FF // (2 * blk), D // (wide // 2))
     reduce = (D // (2 * blk), FF // (wide // 2))
-    full, part = (2,) * len(names), (2,) * (len(names) - 1)
+    full, part, half, less = ((2,) * (len(names) - gone) for gone in range(4))
     return call(
         functools.partial(forward_back_kernel, steps, wide, blk),
         "forward_back",
@@ -1282,14 +1351,16 @@
         ],
         [
             (whole((DOCS, PAGE, D)), shaped((DOCS, PAGE, D), BF16)),
-            (ANY, shaped(part + expand, BF16)),
-            (ANY, shaped(part + reduce, BF16)),
-            (whole((cuts, D, D // cuts)), shaped((cuts, D, D // cuts), BF16)),
+            (ANY, shaped(less + expand, BF16)),
+            (ANY, shaped(half + expand, BF16)),
+            (ANY, shaped(less + reduce, BF16)),
+            (ANY, shaped(half + reduce, BF16)),
+            (whole(full + small), shaped(full + small, BF16)),
             (whole((ROWS, D)), shaped((ROWS, D), F32)),
             (whole((ROWS, D)), shaped((ROWS, D), BF16)),
             (whole((8 * QUADS, ROWS)), shaped((8 * QUADS, ROWS), F32)),
             (whole((ROWS, PAIR)), shaped((ROWS, PAIR), F32)),
-            (whole((16, D)), shaped((16, D), F32)),
+            (whole((8, D)), shaped((8, D), F32)),
         ],
         [
             pltpu.VMEM((ROWS, D), BF16),
@@ -1302,9 +1373,13 @@
             pltpu.VMEM(full + reduce, BF16),
             pltpu.VMEM(part + expand, BF16),
             pltpu.VMEM(part + reduce, BF16),
+            pltpu.VMEM(less + expand, BF16),
+            pltpu.VMEM(less + reduce, BF16),
             pltpu.SemaphoreType.DMA((2, steps)),
             pltpu.SemaphoreType.DMA((2, steps)),
-            pltpu.SemaphoreType.DMA((2,)),
+            pltpu.SemaphoreType.DMA((2, steps // 2)),
+            pltpu.SemaphoreType.DMA((2, steps // 2)),
+            pltpu.SemaphoreType.DMA((4,)),
         ],
         8 * 10**9,
         25 * 10**6,
@@ -1312,150 +1387,135 @@
     )
 
 
-def back_scratch(keys, dq_columns):
-    return [
-        pltpu.VMEM((keys, D), BF16),
-        pltpu.VMEM((keys, 2 * QUAD), BF16),
-        pltpu.VMEM((keys, D), F32),
-        pltpu.VMEM((ROWS, dq_columns), BF16),
-    ]
-
-
-def cross_back(
-    pages, gain, shift, closed, q, k, v, grad_out, lse, delta, w_pairs,
-    w_query, w_gate, w_self, hidden, self_out, grad_mixed, grad_logit, joined, jobs, sources,
-    plan, wide, blk,
+def back(
+    cross, own, images, texts, gain, shift, closed, w_pairs, project, w_query, w_gate, w_self,
+    hidden, self_out, grad_mixed, grad_logit, joined, last_small, far_sources, jobs, plan, wide, blk,
 ):
-    keys = closed.shape[0]
-    half = keys // 2
-    cuts = tile_cuts(wide)
+    q_cross, k_cross, v_cross, do_cross, lse_cross, delta_cross = cross
+    q_self, k_self, v_self, lse_self = own
+    cross_keys, self_keys = k_cross.shape[0], k_self.shape[0]
+    names = bit_names(wide, blk)
+    groups = group_bits(blk)
+    tile = (2,) * len(tile_bits(wide, blk))
+    lanes = 2 * D // wide
+    stream = shaped((DOCS, PAGE, D), BF16)
+
+    def fixed(array):
+        count = len(array.shape)
+        spec = pl.BlockSpec(
+            array.shape, lambda step: (0,) * count, pipeline_mode=pl.Buffered(buffer_count=1)
+        )
+        return (spec, array)
+
+    def early(array, rows, offset=0):
+        last = QUADS - 1
+        return (
+            pl.BlockSpec(
+                (rows, QUAD), lambda step: (0, offset + step - step // QUADS * (step - last))
+            ),
+            array,
+        )
+
+    def late(array, rows, offset=0):
+        return (
+            pl.BlockSpec((rows, QUAD), lambda step: (0, offset + step // QUADS * (step - QUADS))),
+            array,
+        )
+
+    def early_rows(array):
+        last = QUADS - 1
+        return (
+            pl.BlockSpec((8, ROWS), lambda step: (step - step // QUADS * (step - last), 0)), array
+        )
+
+    def late_rows(array):
+        return (pl.BlockSpec((8, ROWS), lambda step: (step // QUADS * (step - QUADS), 0)), array)
+
+    def tiles(columns_here):
+        return pltpu.VMEM(tile + (columns_here // (2 * blk), lanes), BF16)
+
+    def both(job):
+        return pltpu.VMEM((2,) * (1 + len(job.after())) + (job.rows, job.lanes), BF16)
+
+    image_rows, text_rows = cross_keys // 2, self_keys // 2
     return call(
-        functools.partial(cross_back_kernel, wide, blk, jobs, plan),
-        "cross_back",
-        QUADS,
+        functools.partial(back_kernel, wide, blk, jobs, plan),
+        "back",
+        2 * QUADS,
         [
-            (whole(pages.shape), pages),
-            (whole(gain.shape), gain),
-            (whole(shift.shape), shift),
-            (whole(closed.shape), closed),
-            (columns(ROWS), q),
-            (columns(keys), k),
-            (columns(keys), v),
-            (columns(ROWS), grad_out),
-            (stat_rows(), lse),
-            (stat_rows(), delta),
-            (columns(D), w_pairs),
-            (columns(D, QUADS), w_pairs),
-            (whole((D, D)), w_query),
-            (whole(w_gate.shape), w_gate),
-            (whole((D, D)), w_self),
-            (whole((ROWS, D)), hidden),
-            (whole((ROWS, D)), self_out),
-            (whole((ROWS, D)), grad_mixed),
-            (whole((ROWS, PAIR)), grad_logit),
-            (whole((DOCS, PAGE, D)), joined),
+            (ANY, images),
+            own_pages(images),
+            (ANY, texts),
+            fixed(gain),
+            fixed(shift),
+            fixed(closed[0]),
+            fixed(closed[1]),
+            early(q_cross, ROWS),
+            early(k_cross, cross_keys),
+            early(v_cross, cross_keys),
+            early(do_cross, ROWS),
+            early_rows(lse_cross),
+            early_rows(delta_cross),
+            early(w_pairs, D),
+            early(w_pairs, D, QUADS),
+            late(q_self, ROWS),
+            late(k_self, self_keys),
+            late(v_self, self_keys),
+            late_rows(lse_self),
+            late(project, D),
+            late(project, D, QUADS),
+            late(project, D, 2 * QUADS),
+            fixed(w_query),
+            fixed(w_gate),
+            (ANY, w_self),
+            fixed(hidden),
+            fixed(self_out),
+            (ANY, grad_mixed),
+            fixed(grad_logit),
+            fixed(joined),
+            fixed(last_small),
         ]
-        + [(ANY, source) for source in sources],
+        + [(ANY, source) for source in far_sources],
+        [(ANY, stream)] * 3
+        + [(whole((SUMS, D)), shaped((SUMS, D), F32)), (whole((8, D)), shaped((8, D), F32))]
+        + [(whole(job.result().shape), job.result()) for job in jobs if job.ends],
         [
-            (whole((half, D)), shaped((half, D), BF16)),
-            (whole((half, D)), shaped((half, D), BF16)),
-            (whole((cuts, 2 * D, D // cuts)), shaped((cuts, 2 * D, D // cuts), BF16)),
-            (whole((cuts, D, D // cuts)), shaped((cuts, D, D // cuts), BF16)),
-            (whole((cuts, D, D // cuts)), shaped((cuts, D, D // cuts), BF16)),
-            (whole((16, D)), shaped((16, D), F32)),
-            (whole((ROWS, D)), shaped((ROWS, D), F32)),
-            (whole((ROWS, D)), shaped((ROWS, D), BF16)),
-            (whole((8 * QUADS, ROWS)), shaped((8 * QUADS, ROWS), F32)),
-            (whole((8, D)), shaped((8, D), F32)),
-            (whole((DOCS, PAGE, D)), shaped((DOCS, PAGE, D), BF16)),
+            pltpu.VMEM((self_keys, D), BF16),
+            pltpu.VMEM((self_keys, 2 * QUAD), BF16),
+            pltpu.VMEM((self_keys, D), F32),
+            pltpu.VMEM((ROWS, D), BF16),
+            pltpu.VMEM((PAIR, D), BF16),
+            pltpu.VMEM((ROWS, D), F32),
+            pltpu.VMEM((ROWS, D), BF16),
+            pltpu.VMEM((8 * QUADS, ROWS), F32),
+            pltpu.VMEM(texts.shape, BF16),
+            pltpu.VMEM((text_rows, D), BF16),
+            pltpu.VMEM((text_rows, D), BF16),
+            pltpu.VMEM((text_rows, D), BF16),
+            pltpu.VMEM((SUMS, D), F32),
+            pltpu.SemaphoreType.DMA((4,)),
+            tiles(2 * D),
+            tiles(D),
+            tiles(D),
+            tiles(3 * D),
+            both(jobs[0]),
+            both(jobs[2]),
         ]
-        + [(ANY, job.result()) for job in jobs],
-        back_scratch(keys, D) + [pltpu.VMEM((PAIR, D), BF16)] + [kind for job in jobs for kind in job.scratch()] + Home.scratch(),
-        12 * 10**9,
-        20 * 10**6,
+        + [kind for job in jobs for kind in job.scratch()]
+        + Home.scratch()
+        + Rows.scratch(groups, image_rows)
+        + Rows.scratch(groups, text_rows)
+        + Total.scratch(names, SUMS)
+        + Total.scratch(names, 8),
+        23 * 10**9,
+        30 * 10**6,
         2,
     )
 
 
-def self_back(
-    pages, gain, shift, closed, q, k, v, grad_out, lse, delta, project, image_sums, images,
-    jobs, sources, plan, wide, blk,
-):
-    keys = closed.shape[0]
-    half = keys // 2
-    cuts = tile_cuts(wide)
-    image_half = image_sums[0].shape[0]
-    return call(
-        functools.partial(self_back_kernel, wide, blk, jobs, plan),
-        "self_back",
-        QUADS,
-        [
-            (whole(pages.shape), pages),
-            (whole(gain.shape), gain),
-            (whole(shift.shape), shift),
-            (whole(closed.shape), closed),
-            (columns(ROWS), q),
-            (columns(keys), k),
-            (columns(keys), v),
-            (columns(ROWS), grad_out),
-            (stat_rows(), lse),
-            (stat_rows(), delta),
-            (columns(D), project),
-            (columns(D, QUADS), project),
-            (columns(D, 2 * QUADS), project),
-        ]
-        + [(whole((image_half, D)), part) for part in image_sums]
-        + [own_pages(images)]
-        + [(ANY, source) for source in sources],
-        [
-            (whole((half, D)), shaped((half, D), BF16)),
-            (whole((half, D)), shaped((half, D), BF16)),
-            (whole((cuts, 3 * D, D // cuts)), shaped((cuts, 3 * D, D // cuts), BF16)),
-            (whole((8, D)), shaped((8, D), F32)),
-            (whole((DOCS, PAGE, D)), shaped((DOCS, PAGE, D), BF16)),
-        ]
-        + [(ANY, job.result()) for job in jobs],
-        back_scratch(keys, QUAD)
-        + [kind for job in jobs for kind in job.scratch()]
-        + Rows.scratch(group_bits(blk), image_half),
-        11 * 10**9,
-        17 * 10**6,
-        3,
-    )
-
-
-def tail(wide, blk, jobs, plan, sources, sums, texts, grad_hidden, gain, small):
-    names = bit_names(wide, blk)
+def finish(pieces, streams, sums, last_sums):
     vmem = pl.BlockSpec(memory_space=pltpu.VMEM)
-    rows = sum(part.shape[0] for part in small)
-    operands = [*sources, *sums, texts, grad_hidden, gain, *small]
-    own = len(jobs) + len(sums)
-    in_specs = [ANY if job.order else vmem for job in jobs] + [vmem] * (len(operands) - len(jobs))
-    in_specs[own] = own_pages(texts)[0]
-    return pl.pallas_call(
-        functools.partial(tail_kernel, wide, blk, jobs, plan),
-        grid=(1,),
-        in_specs=in_specs,
-        out_specs=[vmem] * (2 + len(jobs)),
-        out_shape=[
-            shaped((DOCS, PAGE, D), BF16),
-            shaped((rows, D), F32),
-            *(job.result() for job in jobs),
-        ],
-        scratch_shapes=[kind for job in jobs for kind in job.scratch()]
-        + Rows.scratch(group_bits(blk), sums[0].shape[0])
-        + Total.scratch(names, rows),
-        name="tail",
-        compiler_params=pltpu.CompilerParams(
-            vmem_limit_bytes=VMEM_LIMIT, collective_id=4, has_side_effects=True
-        ),
-        cost_estimate=pl.CostEstimate(flops=10**7, bytes_accessed=10**8, transcendentals=0),
-    )(*operands)
-
-
-def finish(pieces, streams, sums):
-    vmem = pl.BlockSpec(memory_space=pltpu.VMEM)
-    operands = [part for parts in pieces for part in parts] + [*streams, sums]
+    operands = [part for parts in pieces for part in parts] + [*streams, sums, last_sums]
     results = []
     for index, parts in enumerate(pieces):
         shape = (parts[0].shape[2], sum(2 * part.shape[1] for part in parts))
@@ -1472,20 +1532,6 @@
         compiler_params=pltpu.CompilerParams(vmem_limit_bytes=VMEM_LIMIT),
         cost_estimate=pl.CostEstimate(flops=10**6, bytes_accessed=5 * 10**6, transcendentals=0),
     )(*operands)
-
-
-def tile_cuts(wide):
-    cuts = wide // 2
-    return cuts if (D // cuts) % PAIR == 0 else 1
-
-
-def tiled(grad, wide, blk):
-    cuts = wide // 2
-    if grad.shape[0] != cuts:
-        _, rows, lanes = grad.shape
-        grad = jnp.transpose(grad.reshape(rows, cuts, lanes // cuts), (1, 0, 2))
-    names = tile_bits(wide, blk)
-    return grad.reshape((2,) * len(names) + (grad.shape[1] // (2 * blk), grad.shape[2]))
 
 
 def body(
@@ -1533,115 +1579,77 @@
         image_closed, cross_query, cross_pairs,
     )
     (
-        joined, expand_sum, reduce_sum, d_cross_output, grad_mixed, grad_raw, cross_delta,
+        joined, *partial, d_cross_output, grad_mixed, grad_raw, cross_delta,
         grad_logit, small_last,
     ) = forward_back(
         hidden, raw, gate, cots, cross_output, norm_gain, norm_bias, expand_weight,
         expand_bias.reshape(1, FF), reduce_weight, reduce_bias.reshape(1, D), wide, blk,
     )
 
-    def jobs_of(rows, split, size, left, orders):
-        if rows % 16 or not 0 < split < rows:
-            return [Job(left, orders[-1], 0, rows, size, False)]
-        return [
-            Job(left, orders[0], 0, split, size, False),
-            Job(left, orders[1], split, rows - split, size, False),
-        ]
-
-    expand_rows, reduce_rows = FF // share, D // share
-    expand_jobs = jobs_of(
-        expand_rows, expand_rows // 32 * 16, lanes, names[:-1], (first + high, first)
-    )
-    reduce_jobs = jobs_of(reduce_rows, 16, far, names[:-1], (low + high, low))
-    jobs = tuple(expand_jobs + reduce_jobs)
-    sources = [expand_sum] * len(expand_jobs) + [reduce_sum] * len(reduce_jobs)
-    plan = {0: (0, 2), 1: (3,), 2: (2, 1), 4: (0, 2)} if len(jobs) == 4 else {0: range(len(jobs))}
-    (
-        image_keep, image_send, d_pairs, d_query, d_self_output, d_gate, grad_hidden, self_do,
-        self_delta, small_cross, joined_home, *partial,
-    ) = cross_back(
-        image_pages, norm_gain, norm_bias, image_closed, cross_q, cross_k, cross_v, grad_raw,
-        cross_lse, cross_delta, cross_pairs, cross_query, gate_rows, self_output, hidden, self_out,
-        grad_mixed, grad_logit, joined, jobs, sources, plan, wide, blk,
-    )
-
-    def rest(job, order, ends):
-        left = job.after()
-        wanted = tuple(name for name in order if name in left)
-        return Job(left, wanted, 0, job.rows, job.lanes, ends)
-
-    count = len(jobs)
-    jobs = tuple(
-        [rest(job, high + low + first + others, False) for job in expand_jobs]
-        + [rest(job, high + first + others + low, False) for job in reduce_jobs]
-    )
-    one = (0, D // share, lanes, False)
-    cross_jobs = (
-        Job(names, (core,) + low, 0, 2 * D // share, lanes, False),
-        Job(names, (core,) + first, *one),
-        Job(names, (core,) + first, *one),
-        Job(names, (core,) + first, *one),
-    )
-    cross_grads = [
-        tiled(grad, wide, blk) for grad in (d_pairs, d_query, d_cross_output, d_self_output)
-    ]
-    late = tuple(range(count, count + 4))
-    plan = {0: late + tuple(range(count)), 2: late}
-    if count == 4:
-        plan = {
-            0: late + (1, 0, 2), 1: (3,), 2: late + (1,), 3: (3, 0, 2), 4: (1,), 5: (3, 1),
-        }
-    text_keep, text_send, d_project, small_self, image_home, *partial = self_back(
-        text_pages, norm_gain, norm_bias, text_closed, self_q, self_k, self_v, self_do,
-        self_lse, self_delta, self_project, (image_keep, image_send), image_pages,
-        jobs + cross_jobs, partial + cross_grads, plan, wide, blk,
-    )
-
-    project_rows = 3 * D // share
-    project_jobs = [
-        job._replace(ends=True)
-        for job in jobs_of(
-            project_rows,
-            project_rows // 2 // 16 * 16 + 16,
-            lanes,
-            names,
-            ((core,) + first + low + others + high, (core,) + low + first + others + high),
-        )
-    ]
-    last_jobs = [rest(cross_jobs[0], first + high + others, True)] + [
-        rest(job, high + low + others, True) for job in cross_jobs[1:]
-    ]
-    ended = [Job((), (), 0, job.rows, job.lanes, True) for job in jobs]
-    most = len(project_jobs)
-    both = tuple(range(most))
-    crossed = tuple(range(most, most + 4))
+    blk_names = names[wide.bit_length() - 2 : -1]
+    top, top_wide = blk_names[:1], names[:1]
+    below = tuple(name for name in high if name not in top)
+    expand_shape = (0, FF // share, lanes, False)
+    reduce_shape = (0, D // share, far, False)
+    jobs = (
+        Job(others[::-1] + blk_names[1:], below, *expand_shape),
+        Job(others[::-1] + first + blk_names[1:], first + below, *expand_shape),
+        Job(names[1 : wide.bit_length() - 2] + blk_names[:-1], below, *reduce_shape),
+        Job(names[1 : wide.bit_length() - 2] + blk_names, low + below, *reduce_shape),
+    )
+    ends = {"ends": True, "near": True}
+    parts = tuple(job._replace(inner=True) for job in jobs)
+    middle_names = names[1 : wide.bit_length() - 2]
+    one = (0, D // share, lanes, True)
+    rows = 3 * D // share
+    split = rows // 2 // 16 * 16 + 16 if rows % 16 == 0 else 0
+    ahead = (core,) + first + low + others + high
+    behind = (core,) + low + first + others + high
+    cross_order = (core,) + first + high + low + others
+    jobs = parts + (
+        Job(top + jobs[0].after(), low + top + others, *expand_shape)._replace(**ends),
+        Job(top_wide + jobs[2].after(), top_wide + top + middle_names, *reduce_shape)._replace(**ends),
+        Job(names, (core,) + low + first + high + others, 0, 2 * D // share, lanes, True, True),
+        Job(names, cross_order, *one, True),
+        Job(names, cross_order, *one, False),
+        Job(names, cross_order, *one, True),
+    )
+    if split:
+        jobs += (Job(names, ahead, 0, split, lanes, True, True),)
+    jobs += (Job(names, behind, split, rows - split, lanes, True, True),)
+    project = tuple(range(10, len(jobs)))
     plan = {
-        0: both + crossed + tuple(range(most + 4, most + 4 + count)),
-        1: both,
-        2: crossed,
-        3: both + crossed,
-        4: both + crossed,
-        5: both,
-        6: both,
+        0: (1, 3, 0, 2),
+        4: (1, 3, 0, 2),
+        6: (6, 7, 8, 9),
+        7: (7, 8, 9),
+        8: (1, 3),
+        9: (4, 6, 5),
+        12: project,
+        13: (7, 8, 9),
+        14: project,
+        15: (4, 5, 6),
+        16: (7, 8, 9) + project,
+        17: (4, 5, 6) + project,
+        18: (7, 8, 9, 6) + project,
     }
-    text_home, sums, *pieces = tail(
-        wide, blk, (*project_jobs, *last_jobs, *ended), plan,
-        [tiled(d_project, wide, blk)] * most + partial[count:] + partial[:count],
-        (text_keep, text_send), text_pages, grad_hidden, norm_gain,
-        (d_gate, small_last, small_cross, small_self),
-    )
-    project_pieces = pieces[:most]
-    cross_pieces = pieces[most : most + 4]
-    expand_pieces = pieces[most + 4 : most + 4 + len(expand_jobs)]
-    reduce_pieces = pieces[most + 4 + len(expand_jobs) :]
+    joined_home, text_home, image_home, sums, last_sums, *pieces = back(
+        (cross_q, cross_k, cross_v, grad_raw, cross_lse, cross_delta),
+        (self_q, self_k, self_v, self_lse),
+        image_pages, text_pages, norm_gain, norm_bias, (image_closed, text_closed), cross_pairs,
+        self_project, cross_query, gate_rows, self_output, hidden, self_out, grad_mixed,
+        grad_logit, joined, small_last, (*partial, d_cross_output), jobs, plan, wide, blk,
+    )
+    expand_piece, reduce_piece, *cross_pieces = pieces[:6]
+    project_pieces = pieces[6:]
     (
         grad_cross_pairs, grad_cross_query, grad_cross_output, grad_self_output,
         grad_expand_weight, grad_self_project, grad_reduce_weight,
         joined_blocks, text_grad, image_grad,
         grad_gate_weight, grad_expand_bias, grad_reduce_bias, gains, shifts,
     ) = finish(
-        [[piece] for piece in cross_pieces] + [expand_pieces, project_pieces, reduce_pieces],
-        [joined_home, text_home, image_home], sums,
+        [[piece] for piece in cross_pieces] + [[expand_piece], project_pieces, [reduce_piece]],
+        [joined_home, text_home, image_home], sums, last_sums,
     )
     return (
         joined_blocks,
@@ -1662,10 +1670,338 @@
     )
 
 
+def normalize(values, gains, biases):
+    scaled, inverse = standardize(values)
+    return (scaled * gains + biases, scaled, inverse)
+
+
+def normalize_back(upstream, scaled, inverse, gains):
+    result = norm_back(upstream, scaled, inverse, gains)
+    return (result, jnp.sum(upstream * scaled, axis=0), jnp.sum(upstream, axis=0))
+
+
+def gelu_tanh(values):
+    return jax.nn.gelu(values, approximate=True)
+
+
+def forward_doc(queries, carried, key_pairs, allowed, scaling):
+    running_max, summed, accumulated = carried
+    key_count = key_pairs.shape[0]
+    keys_part = key_pairs[:, :D].reshape(key_count, H, HD)
+    values_part = key_pairs[:, D:].reshape(key_count, H, HD)
+    open_keys = (allowed > 0)[None, None, :]
+    scores = (
+        jnp.einsum("qhd,khd->hqk", queries, keys_part, preferred_element_type=F32) * scaling
+    )
+    scores = jnp.where(open_keys, scores, NEGATIVE)
+    new_max = jnp.maximum(running_max, jnp.max(scores, axis=-1))
+    fading = jnp.exp(running_max - new_max)
+    weights = jnp.where(open_keys, jnp.exp(scores - new_max[..., None]), 0.0)
+    summed = summed * fading + jnp.sum(weights, axis=-1)
+    accumulated = accumulated * fading[..., None] + jnp.einsum(
+        "hqk,khd->hqd",
+        weights.astype(BF16),
+        values_part,
+        preferred_element_type=F32,
+    )
+    return (new_max, summed, accumulated)
+
+
+def forward_fold(queries, scaling, carried, pieces):
+    key_pairs, allowed = pieces
+
+    def forward_per_doc(doc_items):
+        doc_queries, doc_max, doc_sum, doc_acc, doc_pairs, doc_allowed = doc_items
+        doc_carry = (doc_max, doc_sum, doc_acc)
+        result = forward_doc(doc_queries, doc_carry, doc_pairs, doc_allowed, scaling)
+        return result
+
+    return lax.map(
+        forward_per_doc, (queries, carried[0], carried[1], carried[2], key_pairs, allowed)
+    )
+
+
+def backward_doc(queries, grad_out, log_sum, row_delta, key_pairs, allowed, scaling):
+    key_count = key_pairs.shape[0]
+    keys_part = key_pairs[:, :D].reshape(key_count, H, HD)
+    values_part = key_pairs[:, D:].reshape(key_count, H, HD)
+    open_keys = (allowed > 0)[None, None, :]
+    scores = (
+        jnp.einsum("qhd,khd->hqk", queries, keys_part, preferred_element_type=F32) * scaling
+    )
+    probabilities = jnp.where(open_keys, jnp.exp(scores - log_sum[..., None]), 0.0)
+    grad_probs = jnp.einsum(
+        "qhd,khd->hqk", grad_out, values_part, preferred_element_type=F32
+    )
+    grad_scores = (probabilities * (grad_probs - row_delta[..., None])).astype(BF16)
+    query_grad = (
+        jnp.einsum("hqk,khd->qhd", grad_scores, keys_part, preferred_element_type=F32)
+        * scaling
+    )
+    key_grad = (
+        jnp.einsum("hqk,qhd->khd", grad_scores, queries, preferred_element_type=F32)
+        * scaling
+    )
+    value_grad = jnp.einsum(
+        "hqk,qhd->khd",
+        probabilities.astype(BF16),
+        grad_out,
+        preferred_element_type=F32,
+    )
+    return (
+        query_grad,
+        jnp.concatenate(
+            [key_grad.reshape(key_count, D), value_grad.reshape(key_count, D)], axis=-1
+        ),
+    )
+
+
+def backward_fold(queries, grad_out, log_sum, row_delta, scaling, pieces):
+    key_pairs, allowed = pieces
+
+    def backward_per_doc(doc_items):
+        doc_queries, doc_grad, doc_log, doc_delta, doc_pairs, doc_allowed = doc_items
+        result = backward_doc(
+            doc_queries, doc_grad, doc_log, doc_delta, doc_pairs, doc_allowed, scaling
+        )
+        return result
+
+    query_parts, pair_parts = lax.map(
+        backward_per_doc, (queries, grad_out, log_sum, row_delta, key_pairs, allowed)
+    )
+    return (query_parts, pair_parts)
+
+
+def start_state():
+    return (
+        jnp.full((DOCS, H, PAGE), NEGATIVE, F32),
+        jnp.zeros((DOCS, H, PAGE), F32),
+        jnp.zeros((DOCS, H, PAGE, HD), F32),
+    )
+
+
+def finish_state(state):
+    running_max, summed, accumulated = state
+    result = jnp.transpose(accumulated / summed[..., None], (0, 2, 1, 3))
+    return (result, running_max + jnp.log(summed))
+
+
+def tile_order(grad, wide_count, blk_count):
+    rows, cols = grad.shape
+    tiled = grad.reshape(wide_count, rows // wide_count, blk_count, cols // blk_count)
+    return jnp.transpose(tiled, (0, 2, 1, 3)).reshape(
+        wide_count * blk_count * (rows // wide_count), cols // blk_count
+    )
+
+
+def plain_body(
+    text_blocks,
+    image_blocks,
+    cotangent,
+    text_mask,
+    page_regions,
+    doc_pages,
+    self_project,
+    self_output,
+    cross_query,
+    cross_pairs,
+    cross_output,
+    gate_weight,
+    expand_weight,
+    expand_bias,
+    reduce_weight,
+    reduce_bias,
+    norm_gain,
+    norm_bias,
+):
+    scaling = HD ** (-0.5)
+    block_shape = text_blocks.shape
+    offsets = jnp.arange(PAGE, dtype=jnp.int32)
+    living = (lax.axis_index("blk") < doc_pages)[:, None]
+    text_open = (living & ((text_mask > 0) | (offsets[None, :] == 0))).astype(BF16)
+    image_open = (living & (offsets[None, :] < page_regions)).astype(BF16)
+    text_rows = text_blocks.reshape(-1, D).astype(F32)
+    image_rows = image_blocks.reshape(-1, D).astype(F32)
+    normed_text, scaled_first, inverse_first = normalize(text_rows, norm_gain[0], norm_bias[0])
+    normed_low = normed_text.astype(BF16)
+    triples = product(normed_low, self_project).astype(BF16)
+    self_queries = triples[:, :D].reshape(DOCS, PAGE, H, HD)
+    self_pairs = triples[:, D:].reshape(DOCS, PAGE, 2 * D)
+    self_state = forward_fold(
+        self_queries,
+        scaling,
+        start_state(),
+        (
+            lax.all_gather(self_pairs, "blk", axis=1, tiled=True),
+            lax.all_gather(text_open, "blk", axis=1, tiled=True),
+        ),
+    )
+    self_result, self_logsum = finish_state(self_state)
+    self_low = self_result.reshape(-1, D).astype(BF16)
+    hidden = text_rows + product(self_low, self_output)
+    cross_normed, scaled_cross, inverse_cross = normalize(hidden, norm_gain[1], norm_bias[1])
+    cross_low = cross_normed.astype(BF16)
+    gate_values = jax.nn.sigmoid(product(cross_low, gate_weight))
+    image_normed, scaled_image, inverse_image = normalize(image_rows, norm_gain[2], norm_bias[2])
+    image_low = image_normed.astype(BF16)
+    image_pairs = product(image_low, cross_pairs).astype(BF16).reshape(DOCS, PAGE, 2 * D)
+    cross_queries = product(cross_low, cross_query).astype(BF16).reshape(DOCS, PAGE, H, HD)
+    cross_state = forward_fold(
+        cross_queries,
+        scaling,
+        start_state(),
+        (
+            lax.all_gather(image_pairs, "blk", axis=1, tiled=True),
+            lax.all_gather(image_open, "blk", axis=1, tiled=True),
+        ),
+    )
+    cross_result, cross_logsum = finish_state(cross_state)
+    gate_heads = gate_values.reshape(DOCS, PAGE, H, 1)
+    gated_low = (cross_result * gate_heads).reshape(-1, D).astype(BF16)
+    mixed_rows = hidden + product(gated_low, cross_output)
+    final_normed, scaled_final, inverse_final = normalize(mixed_rows, norm_gain[3], norm_bias[3])
+    final_low = final_normed.astype(BF16)
+    inner_rows = product(final_low, expand_weight) + expand_bias
+    active_low = gelu_tanh(inner_rows).astype(BF16)
+    joined_blocks = (
+        (mixed_rows + product(active_low, reduce_weight) + reduce_bias)
+        .reshape(block_shape)
+        .astype(BF16)
+    )
+    upstream = cotangent.reshape(-1, D)
+    upstream_float = upstream.astype(F32)
+    grad_reduce_bias = jnp.sum(upstream_float, axis=0)
+    grad_reduce_weight = transposed(active_low, upstream)
+    grad_active = against(upstream, reduce_weight).astype(BF16)
+    gelu_value, gelu_pull = jax.vjp(gelu_tanh, inner_rows)
+    grad_inner = gelu_pull(grad_active.astype(F32))[0].astype(BF16)
+    grad_expand_bias = jnp.sum(grad_inner.astype(F32), axis=0)
+    grad_expand_weight = transposed(final_low, grad_inner)
+    back_final, gain_final, shift_final = normalize_back(
+        against(grad_inner, expand_weight), scaled_final, inverse_final, norm_gain[3]
+    )
+    grad_mixed = upstream_float + back_final
+    grad_branch = grad_mixed.astype(BF16)
+    grad_cross_output = transposed(gated_low, grad_branch)
+    grad_gated = against(grad_branch, cross_output).astype(BF16)
+    grad_gated_heads = grad_gated.astype(F32).reshape(DOCS, PAGE, H, HD)
+    grad_gate = jnp.sum(grad_gated_heads * cross_result, axis=-1).reshape(-1, H)
+    grad_logit = grad_gate * gate_values * (1.0 - gate_values)
+    grad_gate_weight = lax.dot_general(
+        cross_low.astype(F32), grad_logit, (((0,), (0,)), ((), ())), precision=HIGHEST
+    )
+    grad_raw = (grad_gated_heads * gate_heads).astype(BF16)
+    cross_delta = jnp.transpose(
+        jnp.sum(grad_raw.astype(F32) * cross_result, axis=-1), (0, 2, 1)
+    )
+    cross_carry = backward_fold(
+        cross_queries,
+        grad_raw,
+        cross_logsum,
+        cross_delta,
+        scaling,
+        (
+            lax.all_gather(image_pairs, "blk", axis=1, tiled=True),
+            lax.all_gather(image_open, "blk", axis=1, tiled=True),
+        ),
+    )
+    cross_home = lax.psum_scatter(
+        cross_carry[1].astype(BF16), "blk", scatter_dimension=1, tiled=True
+    ).astype(F32)
+    cross_query_sum = cross_carry[0]
+    cross_query_low = cross_query_sum.reshape(-1, D).astype(BF16)
+    cross_pair_low = cross_home.reshape(-1, 2 * D).astype(BF16)
+    grad_cross_query = transposed(cross_low, cross_query_low)
+    grad_cross_pairs = transposed(image_low, cross_pair_low)
+    back_image, gain_image, shift_image = normalize_back(
+        against(cross_pair_low, cross_pairs), scaled_image, inverse_image, norm_gain[2]
+    )
+    image_grad = back_image.reshape(block_shape).astype(BF16)
+    grad_cross_in = against(cross_query_low, cross_query) + lax.dot_general(
+        grad_logit, gate_weight.astype(F32), (((1,), (1,)), ((), ())), precision=HIGHEST
+    )
+    back_cross, gain_cross, shift_cross = normalize_back(
+        grad_cross_in, scaled_cross, inverse_cross, norm_gain[1]
+    )
+    grad_hidden = grad_mixed + back_cross
+    grad_self_branch = grad_hidden.astype(BF16)
+    grad_self_output = transposed(self_low, grad_self_branch)
+    grad_self_result = (
+        against(grad_self_branch, self_output).astype(BF16).reshape(DOCS, PAGE, H, HD)
+    )
+    self_delta = jnp.transpose(
+        jnp.sum(grad_self_result.astype(F32) * self_result, axis=-1), (0, 2, 1)
+    )
+    self_carry = backward_fold(
+        self_queries,
+        grad_self_result,
+        self_logsum,
+        self_delta,
+        scaling,
+        (
+            lax.all_gather(self_pairs, "blk", axis=1, tiled=True),
+            lax.all_gather(text_open, "blk", axis=1, tiled=True),
+        ),
+    )
+    self_home = lax.psum_scatter(
+        self_carry[1].astype(BF16), "blk", scatter_dimension=1, tiled=True
+    ).astype(F32)
+    self_query_sum = self_carry[0]
+    grad_triples = jnp.concatenate(
+        [self_query_sum.reshape(-1, D), self_home.reshape(-1, 2 * D)], axis=-1
+    ).astype(BF16)
+    grad_self_project = transposed(normed_low, grad_triples)
+    back_first, gain_first, shift_first = normalize_back(
+        against(grad_triples, self_project), scaled_first, inverse_first, norm_gain[0]
+    )
+    text_grad = (grad_hidden + back_first).reshape(block_shape).astype(BF16)
+    wide_count = lax.axis_size("wide")
+    blk_count = lax.axis_size("blk")
+    large_grads = (
+        grad_self_project,
+        grad_self_output,
+        grad_cross_query,
+        grad_cross_pairs,
+        grad_cross_output,
+        grad_expand_weight,
+        grad_reduce_weight,
+    )
+    ordered = tuple((tile_order(grad, wide_count, blk_count) for grad in large_grads))
+    summed_grads = lax.psum_scatter(ordered, ("wide", "blk"), scatter_dimension=0, tiled=True)
+    small_sums = lax.psum(
+        (
+            grad_gate_weight,
+            grad_expand_bias,
+            grad_reduce_bias,
+            jnp.stack([gain_first, gain_cross, gain_image, gain_final]),
+            jnp.stack([shift_first, shift_cross, shift_image, shift_final]),
+        ),
+        ("wide", "blk"),
+    )
+    return (
+        joined_blocks,
+        text_grad,
+        image_grad,
+        summed_grads[0],
+        summed_grads[1],
+        summed_grads[2],
+        summed_grads[3],
+        summed_grads[4],
+        summed_grads[5],
+        summed_grads[6],
+        small_sums[0],
+        small_sums[1],
+        small_sums[2],
+        small_sums[3],
+        small_sums[4],
+    )
+
+
 def solution(mesh):
     rows = P("wide", "blk", None)
+    longest = mesh.shape["blk"] * PAGE
     return jax.shard_map(
-        body,
+        body if longest <= LONGEST else plain_body,
         mesh=mesh,
         in_specs=(rows,) * 3 + (P("wide", "blk"),) * 2 + (P("wide"),) + (P(),) * 12,
         out_specs=(rows,) * 3 + (P("wide", "blk"),) * 7 + (P(),) * 5,

time: 232 us -> 223 us (0.961)
  Pallas kernels: 228 us -> 219 us
    pallas_call x1 -> x0, Pallas kernels: 56.4 us -> none  [tail(): pl.pallas_call(functools.partial(tail_kernel, wide, blk, jobs, plan), gri...]
    pallas_call x5 -> x4, Pallas kernels: 168 us -> 216 us  [call(): pl.pallas_call(kernel, grid=(steps,), in_specs=list(in_specs), out_specs=...]
where the time goes in v4:
time: 223 us; the launch traced here: 222 us
  Pallas kernels  219 us (98%)
  local copies, waits for them, and re-layouts  2.56 us (1%)
    pallas_call x4, Pallas kernels, call(): pl.pallas_call(kernel, grid=(steps,), in_specs=list(in_specs), out_specs=...  216 us

profile of v4, /device:TPU:1, one launch (start us, length us, event | category | flops | bytes accessed | tf_op | source)
XLA Modules:
  0.0 222.3 jit_solution(1989311289592525820)
XLA Ops:
  0.6 1.3 copy.33.regions
  1.9 1.3 reshape.37.b_reduce
  3.2 41.1 %self_forward.1 = (f32[256,768]{1,0:T(8,128)}, f32[24,256]{1,0:T(8,128)}, bf16[256,768]{1,0:T(8,128)(2,1)}, bf16[1024,768]{1,0:T(8,128)(2,1)}, bf16[1024,768]{1,...) custom-call(s32[2,1]{1,0:T(2,128)} %copy.33.regions, ...), custom_call_target="tpu_custom_call" | custom-call | flops 6000000000 | bytes 12000000 | tf_op jit(solution)/shard_map/self_forward/pallas_call | solution.py:1214
  44.4 14.3 %cross_forward.1 = (f32[256,768]{1,0:T(8,128)}, f32[256,128]{1,0:T(8,128)}, f32[256,768]{1,0:T(8,128)}, f32[24,256]{1,0:T(8,128)}, bf16[256,768]{1,0:T(8,128)(2,...) custom-call(bf16[8,128,768]{2,1,0:T(8,128)(2,1)} %get-tuple-element.72.text.refs_2_, ...), custom_call_target="tpu_custom_call" | custom-call | flops 7000000000 | bytes 14000000 | tf_op jit(solution)/shard_map/cross_forward/pallas_call | solution.py:1214
  58.6 27.2 %forward_back.1 = (bf16[2,128,768]{2,1,0:T(8,128)(2,1)}, bf16[2,2,192,384]{3,2,1,0:T(8,128)(2,1)}, bf16[2,2,2,192,384]{4,3,2,1,0:T(8,128)(2,1)}, bf16[2,2,48,153...) custom-call(f32[256,768]{1,0:T(8,128)} %get-tuple-element.79.hidden., ...), custom_call_target="tpu_custom_call" | custom-call | flops 8000000000 | bytes 25000000 | tf_op jit(solution)/shard_map/forward_back/pallas_call | solution.py:1214
  85.9 132.9 %back.1 = (bf16[2,128,768]{2,1,0:T(8,128)(2,1)}, bf16[2,128,768]{2,1,0:T(8,128)(2,1)}, bf16[2,128,768]{2,1,0:T(8,128)(2,1)}, f32[24,768]{1,0:T(8,128)}, f32[8,76...) custom-call(bf16[8,112,768]{2,1,0:T(8,128)(2,1)} %get-tuple-element., ...), custom_call_target="tpu_custom_call" | custom-call | flops 23000000512 | bytes 30000000 | tf_op jit(solution)/shard_map/back/pallas_call | solution.py:1214
  218.8 3.3 %finish.1 = (f32[192,192]{1,0:T(8,128)}, f32[192,96]{1,0:T(8,128)}, f32[192,96]{1,0:T(8,128)}, f32[192,96]{1,0:T(8,128)}, f32[192,384]{1,0:T(8,128)}, /*index=5*...) custom-call(bf16[2,96,192]{2,1,0:T(8,128)(2,1)} %get-tuple-element.9, ...), custom_call_target="tpu_custom_call" | custom-call | flops 1000000 | bytes 5000000 | tf_op jit(solution)/shard_map/finish/pallas_call | solution.py:1526
